TPU v7x, 256 devices: a whole 4x4x8 slice. The times are simulated.
256 devices in a mesh: sample: 2 (over z_hi), space: 8 (over y, core), filt: 16 (over z_lo, x).
Axes of the slice: x: 4, y: 4, z: 8 (z_hi: 2, z_lo: 4; z = z_hi * 4 + z_lo), core: 2. Of those that a mesh axis runs over, the one named last changes fastest.
Arguments:
- act_in: bfloat16 [2, 64, 16, 16, 128], P('sample', None, 'space'), may hold values from -6 to 6
- w_first: bfloat16 [27, 64, 128], P(None, None, 'filt'), may hold values from -0.15625 to 0.15625
- w_second: bfloat16 [27, 128, 128], P(None, None, 'filt'), may hold values from -0.109375 to 0.109375
- grad_out: bfloat16 [2, 128, 16, 16, 128], P('sample', 'filt', 'space'), may hold values from -6 to 6
Outputs:
- y_out: bfloat16 [2, 128, 16, 16, 128], P('sample', 'filt', 'space')
- grad_w_first: float32 [27, 64, 128], P(None, None, 'filt')
- grad_w_second: float32 [27, 128, 128], P(None, None, 'filt')
All inputs are finite; a program needn't handle non-finite values.
Results may differ from a plain program's by a relative error of at most 0.0054.
Values may be sent and summed in bfloat16 or wider, within the bound.
No kernel may reach another device: no remote copies, remote signals or barrier semaphores. Data moves between devices by JAX's collectives and lax.ppermute only.
A program may use at most 64 MiB of HBM per device.

v0:
```python
import math

import jax
import jax.numpy as jnp
from jax import lax
from jax.sharding import PartitionSpec as P


def padded(cells, sides, width):
    for axis, dim in sides:
        count = lax.axis_size(axis)
        ends = count - 1
        head = lax.slice_in_dim(cells, 0, width, axis=dim)
        tail = lax.slice_in_dim(cells, cells.shape[dim] - width, cells.shape[dim], axis=dim)
        cells = jnp.concatenate(
            [
                lax.ppermute(tail, axis, [(i, (i + 1) % count) for i in range(ends)]),
                cells,
                lax.ppermute(head, axis, [((i + 1) % count, i) for i in range(ends)]),
            ],
            axis=dim,
        )
    return cells


def correlate(source, kernel, rim_pad):
    taps = kernel.reshape(3, 3, 3, kernel.shape[1], kernel.shape[2])
    return lax.conv_general_dilated(
        source[None],
        taps,
        (1, 1, 1),
        ((0, 0), (rim_pad, rim_pad), (1, 1)),
        dimension_numbers=("NCDHW", "DHWIO", "NCDHW"),
        preferred_element_type=jnp.float32,
    )[0]


def transpose_correlate(gradient, kernel, rim_pad):
    taps = kernel.reshape(3, 3, 3, kernel.shape[1], kernel.shape[2])[::-1, ::-1, ::-1]
    return lax.conv_general_dilated(
        gradient[None],
        taps,
        (1, 1, 1),
        ((0, 0), (rim_pad, rim_pad), (1, 1)),
        dimension_numbers=("NCDHW", "DHWOI", "NCDHW"),
        preferred_element_type=jnp.float32,
    )[0]


def kernel_gradient(source, gradient, rim_pad):
    result = lax.conv_general_dilated(
        source[None],
        gradient[None],
        (1, 1, 1),
        ((0, 0), (rim_pad, rim_pad), (1, 1)),
        dimension_numbers=("CNDHW", "IODHW", "NCDHW"),
        preferred_element_type=jnp.float32,
    )
    return jnp.transpose(result, (2, 3, 4, 0, 1)).reshape(27, source.shape[0], gradient.shape[0])


def silu_slope(value):
    logistic = jax.nn.sigmoid(value)
    return logistic * (1.0 + value * (1.0 - logistic))


def local(act_in, w_first, w_second, grad_out):
    depth_rows = act_in.shape[2]
    height = act_in.shape[3]
    width = act_in.shape[4]
    n_space = lax.axis_size("space")
    n_sample = lax.axis_size("sample")
    slab = act_in[0]
    padded_in = padded(slab, (("space", 1),), 2)
    row_ids = lax.axis_index("space") * depth_rows - 1 + jnp.arange(depth_rows + 2, dtype=jnp.int32)
    inside = (row_ids >= 0) & (row_ids < depth_rows * n_space)
    z_first = correlate(padded_in, w_first, 1)
    act_ext = jnp.where(inside[None, :, None, None], jax.nn.silu(z_first), 0.0).astype(jnp.bfloat16)
    gathered = lax.all_gather(act_ext, "filt", axis=0, tiled=True)
    z_second = correlate(gathered, w_second, 1)
    y_local = jax.nn.silu(z_second).astype(jnp.bfloat16)
    grad_second = (grad_out[0].astype(jnp.float32) * silu_slope(z_second)).astype(jnp.bfloat16)
    grad_rim = padded(grad_second, (("space", 1),), 1)
    back_own = lax.psum_scatter(
        transpose_correlate(grad_rim, w_second, 1), "filt", scatter_dimension=0, tiled=True
    )
    dw_second = kernel_gradient(gathered, grad_second, 1)
    grad_first = (back_own * silu_slope(z_first[:, 1:-1])).astype(jnp.bfloat16)
    dw_first = kernel_gradient(padded_in[:, 1:-1], grad_first, 1)
    sum_first, sum_second = lax.psum((dw_first, dw_second), ("sample", "space"))
    factor = 1.0 / math.sqrt(n_sample * depth_rows * n_space * height * width)
    return (y_local[None], sum_first * factor, sum_second * factor)


def solution(mesh):
    placed = (
        P("sample", None, "space", None, None),
        P(None, None, "filt"),
        P(None, None, "filt"),
        P("sample", "filt", "space", None, None),
    )
    return jax.shard_map(
        local,
        mesh=mesh,
        in_specs=placed,
        out_specs=(
            P("sample", "filt", "space", None, None),
            P(None, None, "filt"),
            P(None, None, "filt"),
        ),
        check_vma=False,
    )
```

profile of v0, /device:TPU:1, one launch (start us, length us, event | category | flops | bytes accessed | tf_op | source)
XLA Modules:
  0.0 603.4 jit_solution(2420930683141478989)
XLA Ops:
  7.2 4.6 collective-permute-start
  13.8 3.3 copy.90
  24.7 2.4 pad_maximum_fusion
  28.7 18.2 %broadcast_select_fusion = f32[4,16,8,17,8]{4,2,3,1,0:T(8,128)} fusion(pred[8,17]{0,1:T(8,128)(4,1)S(1)} %copy-done.5, bf16[3,3,3,64,8]{3,4,2,1,0:T(8,128)(2,1)S(1)} %bitcast.98, bf16[64,6,16,1,7,2]{0,4,5,2,1,3:T(8,128)(2,1)S(1)} %slice.24, bf16[64,6,16,1,8,17]{0,4,5,2,1,3:T(8,128)(2,1)S(1)} %copy.96), kind=kOutput, calls=%fused_computation.27 | convolution fusion | flops 236294144 | bytes 2149512 | tf_op jit(solution)/shard_map/conv_general_dilated | solution.py:28
  46.9 6.1 %copy.97 = f32[4,16,8,17,8]{3,2,4,1,0:T(8,128)} copy(f32[4,16,8,17,8]{4,2,3,1,0:T(8,128)} %broadcast_select_fusion) | data formatting | bytes 557056 | tf_op jit(solution)/shard_map/conv_general_dilated | solution.py:28
  53.0 2.8 reshape.38
  57.5 67.3 %all-gather.2.cloned.1.call-done = bf16[128,4,16,128]{3,0,2,1:T(8,128)(2,1)} async-done(((bf16[8,4,16,128]{3,0,2,1:T(8,128)(2,1)}), bf16[128,4,16,128]{3,0,2,1:T(8,128)(2,1)}) %all-gather.2.cloned.1.call-update) | async-done | bytes 2097168 | tf_op jit(solution)/shard_map/all_gather | solution.py:79
  124.9 4.9 copy.127
  132.4 9.6 %fusion.18 = f32[2,16,8,17,8]{4,2,3,1,0:T(8,128)} fusion(bf16[3,3,3,128,8]{3,4,2,1,0:T(8,128)(2,1)S(1)} %bitcast.85, bf16[128,4,16,1,7,2]{0,4,5,2,1,3:T(8,128)(2,1)S(1)} %slice.26, bf16[128,4,16,1,8,17]{0,4,5,2,1,3:T(8,128)(2,1)S(1)} %copy.100), kind=kOutput, calls=%fused_computation.20 | convolution fusion | flops 238092288 | bytes 2652160 | tf_op jit(solution)/shard_map/conv_general_dilated | solution.py:28
  142.0 3.7 copy.101
  145.7 2.9 add_multiply_fusion
  151.3 2.4 copy.106
  157.7 12.5 %collective-permute-start.2 = (bf16[8,1,16,128]{3,0,2,1:T(8,128)(2,1)S(1)}, bf16[8,1,16,128]{3,0,2,1:T(8,128)(2,1)S(1)}, u32[]{:S(2)}, u32[]{:S(2)}) collective-permute-start(bf16[8,1,16,128]{3,0,2,1:T(8,128)(2,1)S(1)} %get-tuple-element.20), channel_id=1, source_target_pairs={{0,16},{16,32},{32,48},{48,64},{64,80},{80,96},{96,112},{1,17},{17... | collective-permute-start | bytes 98312 | tf_op jit(solution)/shard_map/ppermute | solution.py:17
  172.1 3.7 copy.117
  175.8 10.7 %copy.116 = bf16[1,128,4,16,128]{1,0,4,3,2:T(2,128)(2,1)} copy(bf16[1,128,4,16,128]{4,1,3,2,0:T(8,128)(2,1)} %bitcast.91) | data formatting | bytes 4194304 | tf_op jit(solution)/shard_map/broadcast_in_dim | solution.py:29
  186.6 31.9 %fusion.49 = f32[3,3,3,128,8]{3,4,2,1,0:T(8,128)} fusion(bf16[1,128,4,16,128]{1,0,4,3,2:T(2,128)(2,1)} %copy.116, bf16[1,8,2,16,128]{1,0,4,3,2:T(2,128)(2,1)} %copy.117), kind=kOutput, calls=%fused_computation.64 | convolution fusion | flops 215924736 | bytes 2273280 | tf_op jit(solution)/shard_map/transpose | solution.py:59
  220.5 5.6 copy.109
  227.1 5.2 fusion.29
  234.2 3.0 copy.126
  241.0 149.1 %all-reduce.2.cloned.1.call-done = f32[27,128,8]{1,2,0:T(8,128)} async-done(((f32[27,128,8]{1,2,0:T(8,128)}), f32[27,128,8]{1,2,0:T(8,128)}) %all-reduce.2.cloned.1.call-update) | async-done | bytes 110608 | tf_op jit(solution)/shard_map/psum | solution.py:90
  391.7 78.4 %reduce-scatter.2.cloned.1.call-done = f32[8,2,16,128]{3,0,2,1:T(8,128)} async-done(((f32[128,2,16,128]{3,0,2,1:T(8,128)}), f32[8,2,16,128]{3,0,2,1:T(8,128)}) %reduce-scatter.2.cloned.1.call-update) | async-done | bytes 131088 | tf_op jit(solution)/shard_map/reduce_scatter | solution.py:84
  471.1 3.7 copy.113
  474.8 33.6 %fusion.3 = f32[3,3,3,64,8]{3,4,2,1,0:T(8,128)S(1)} fusion(bf16[1,8,2,16,128]{1,0,4,3,2:T(2,128)(2,1)} %copy.113, bf16[1,64,4,16,128]{1,3,4,2,0:T(8,128)(2,1)S(1)} %copy-done.1), kind=kOutput, calls=%fused_computation.6 | convolution fusion | flops 107962368 | bytes 1169408 | tf_op jit(solution)/shard_map/transpose | solution.py:59
  508.4 87.6 %psum.14 = f32[27,64,8]{1,2,0:T(8,128)S(1)} all-reduce(f32[27,64,8]{1,2,0:T(8,128)S(1)} %bitcast.97), channel_id=1, replica_groups=mesh['sample'=2,'space'=8,'filt'=16] {'sample','space'}, use_global_device_ids=true, to_apply=%region_1.2 | all-reduce | flops 13824 | bytes 110592 | tf_op jit(solution)/shard_map/psum | solution.py:90
  (55 shorter events, 36.1 us)
Async XLA Ops:
  7.2 125.2 %copy-start = (bf16[27,128,8]{1,2,0:T(8,128)(2,1)S(1)}, bf16[27,128,8]{1,2,0:T(8,128)(2,1)}, u32[]{:S(2)}) copy-start(bf16[27,128,8]{1,2,0:T(8,128)(2,1)} %param.6) | copy-start | bytes 165892
  7.2 117.7 %all-gather.2.cloned.1.call-start = ((), (), s32[]{:S(2)}) async-start(), calls=%async_computation.1 | async-start | bytes 2228224 | tf_op jit(solution)/shard_map/all_gather | solution.py:79
  7.2 11.0 %collective-permute-start = (bf16[64,2,16,128]{3,2,1,0:T(8,128)(2,1)}, bf16[64,2,16,128]{3,2,1,0:T(8,128)(2,1)S(1)}, u32[]{:S(2)}, u32[]{:S(2)}) collective-permute-start(bf16[64,2,16,128]{3,2,1,0:T(8,128)(2,1)} %bitcast.94), channel_id=1, source_target_pairs={{0,16},{16,32},{32,48},{48,64},{64,80},{80,96},{96,112},{1,17},{17... | collective-permute-start | bytes 1572872 | tf_op jit(solution)/shard_map/ppermute | solution.py:17
  11.8 10.7 %collective-permute-start.1 = (bf16[64,2,16,128]{3,2,1,0:T(8,128)(2,1)}, bf16[64,2,16,128]{3,2,1,0:T(8,128)(2,1)S(1)}, u32[]{:S(2)}, u32[]{:S(2)}) collective-permute-start(bf16[64,2,16,128]{3,2,1,0:T(8,128)(2,1)} %bitcast.95), channel_id=1, source_target_pairs={{16,0},{32,16},{48,32},{64,48},{80,64},{96,80},{112,96},{17,1},{33... | collective-permute-start | bytes 1572872 | tf_op jit(solution)/shard_map/ppermute | solution.py:19
  27.7 1.0 copy-start.4
  27.7 1.0 copy-start.5
  57.5 332.6 %all-reduce.2.cloned.1.call-start = ((), (), s32[]{:S(2)}) async-start(), calls=%async_computation.3 | async-start | bytes 221184 | tf_op jit(solution)/shard_map/psum | solution.py:90
  142.0 3.7 copy-start.3
  157.7 60.8 %collective-permute-start.2 = (bf16[8,1,16,128]{3,0,2,1:T(8,128)(2,1)S(1)}, bf16[8,1,16,128]{3,0,2,1:T(8,128)(2,1)S(1)}, u32[]{:S(2)}, u32[]{:S(2)}) collective-permute-start(bf16[8,1,16,128]{3,0,2,1:T(8,128)(2,1)S(1)} %get-tuple-element.20), channel_id=1, source_target_pairs={{0,16},{16,32},{32,48},{48,64},{64,80},{80,96},{96,112},{1,17},{17... | collective-permute-start | bytes 98312 | tf_op jit(solution)/shard_map/ppermute | solution.py:17
  170.2 48.4 %collective-permute-start.3 = (bf16[8,1,16,128]{3,0,2,1:T(8,128)(2,1)S(1)}, bf16[8,1,16,128]{3,0,2,1:T(8,128)(2,1)S(1)}, u32[]{:S(2)}, u32[]{:S(2)}) collective-permute-start(bf16[8,1,16,128]{3,0,2,1:T(8,128)(2,1)S(1)} %get-tuple-element.21), channel_id=1, source_target_pairs={{16,0},{32,16},{48,32},{64,48},{80,64},{96,80},{112,96},{17,1},{33... | collective-permute-start | bytes 98312 | tf_op jit(solution)/shard_map/ppermute | solution.py:19
  218.5 251.6 %reduce-scatter.2.cloned.1.call-start = ((), (), s32[]{:S(2)}) async-start(), calls=%async_computation.2 | async-start | bytes 2228224 | tf_op jit(solution)/shard_map/reduce_scatter | solution.py:84
  237.2 2.7 copy-start.2
  239.9 234.9 %copy-start.1 = (bf16[1,64,4,16,128]{1,3,4,2,0:T(8,128)(2,1)S(1)}, bf16[1,64,4,16,128]{1,3,4,2,0:T(8,128)(2,1)}, u32[]{:S(2)}) copy-start(bf16[1,64,4,16,128]{1,3,4,2,0:T(8,128)(2,1)} %slice_bitcast_fusion) | copy-start | bytes 3145732
Sparse Core Ops, SparseCore 0:
  57.6 67.2 all-gather.1
  218.6 171.4 all-reduce.1
  392.8 77.2 reduce-scatter.1
where the time goes:
time: 613 us; the launch traced here: 603 us
  waiting for transfers between devices  298 us (49%)
  matrix products  98.5 us (16%)
  blocking collectives  87.6 us (14%)
  local copies, waits for them, and re-layouts  71.8 us (12%)
  starting transfers between devices  21 us (3%)
  between operations  14.2 us (2%)
  other arithmetic  11.9 us (2%)
    psum x1, waiting for transfers between devices, local(): sum_first, sum_second = lax.psum((dw_first, dw_second), ('sample', 'space'))  149 us
    psum x1, blocking collectives, local(): sum_first, sum_second = lax.psum((dw_first, dw_second), ('sample', 'space'))  87.6 us
    reduce_scatter x1, waiting for transfers between devices, local(): lax.psum_scatter(transpose_correlate(grad_rim, w_second, 1), 'filt', scat...  78.4 us
    all_gather x1, waiting for transfers between devices, local(): gathered = lax.all_gather(act_ext, 'filt', axis=0, tiled=True)  67.3 us
    transpose x2, matrix products, kernel_gradient(): jnp.transpose(result, (2, 3, 4, 0, 1))  65.5 us
    conv_general_dilated x2, matrix products, correlate(): lax.conv_general_dilated(source[None], taps, (1, 1, 1), ((0, 0), (rim_pad...  27.8 us
    conv_general_dilated x9, local copies, waits for them, and re-layouts, correlate(): lax.conv_general_dilated(source[None], taps, (1, 1, 1), ((0, 0), (rim_pad...  18.8 us
    ppermute x2, starting transfers between devices, padded(): lax.ppermute(tail, axis, [(i, (i + 1) % count) for i in range(ends)])  17.1 us
  transfers between devices with their start and end apart: 7, of which 5 were waited for; matrix products, arithmetic and copies ran while one was open for 13% of the time, Pallas kernels for 0%

commit v1 on v0

v1 whole, which is shorter than its diff:
```python
import jax
import jax.numpy as jnp
from jax import lax
from jax.experimental import pallas as pl
from jax.experimental.pallas import tpu as pltpu
from jax.sharding import PartitionSpec as P

F32 = jnp.float32
BF16 = jnp.bfloat16
W = 128
K1, K2 = 27 * 64, 27 * 128
K1P = 1792
KB = 896
VMEM = pl.BlockSpec(memory_space=pltpu.VMEM)
NT = (((1,), (1,)), ((), ()))


def run(kernel, outs, args, scratch=()):
    return pl.pallas_call(
        kernel,
        out_shape=outs,
        in_specs=[VMEM] * len(args),
        out_specs=[VMEM] * len(outs),
        scratch_shapes=list(scratch),
        compiler_params=pltpu.CompilerParams(vmem_limit_bytes=48 * 1024 * 1024),
    )(*args)


def sds(shape, dtype):
    return jax.ShapeDtypeStruct(shape, dtype)


def split():
    f = lax.axis_index("filt")
    return lax.rem(f, 4), lax.div(f, 4)


def xor(a, k):
    return lax.bitwise_xor(a, jnp.int32(k))


def rows8(i):
    return pl.ds(pl.multiple_of(i * 8, 8), 8)


def rows32(i):
    return pl.ds(pl.multiple_of(i * 32, 32), 32)


def shifted(x):
    lane = lax.broadcasted_iota(jnp.int32, x.shape, 1)
    left = jnp.where(lane == 0, 0.0, pltpu.roll(x, 1, 1))
    right = jnp.where(lane == W - 1, 0.0, pltpu.roll(x, W - 1, 1))
    return left, x, right


def logistic(v):
    return 1.0 / (1.0 + jnp.exp(-v))


def pack_kernel(w1_ref, w2_ref, g_ref, b0, b1, b2, b3, rows_ref):
    x, _ = split()
    w1 = w1_ref[...].astype(F32).T
    w2 = w2_ref[...].astype(F32).T
    for d in range(2):
        t = jnp.swapaxes(g_ref[:, d].astype(F32), 0, 1)
        rows_ref[d, 0] = jnp.zeros((8, W), F32)
        rows_ref[d, 17] = jnp.zeros((8, W), F32)
        rows_ref[d, 1:17] = t
    w1p = jnp.concatenate([w1, jnp.zeros((8, K1P - K1), F32)], axis=1)
    for k, out in enumerate((b0, b1, b2, b3)):
        h0 = xor(x, k) * 4
        parts = [rows_ref[d, h0 + h] for d in range(2) for h in range(6)]
        low = jnp.concatenate([w1p] + parts + [jnp.zeros((8, W), F32)], axis=1)
        out[...] = jnp.concatenate([w2, low], axis=0).astype(BF16)


def group_kernel(b0, b1, b2, b3, w1_ref, w2_ref, go_ref, w2b_ref, top, bot):
    x, _ = split()
    for k, b in enumerate((b0, b1, b2, b3)):
        v = b[...].astype(F32)
        at = rows8(xor(x, k))
        top[at, :] = v[:8]
        bot[at, :] = v[8:]
    w1_ref[...] = bot[:, :K1P].astype(BF16)
    go_ref[...] = bot[:, K1P : K1P + 12 * W].astype(BF16)
    w2_ref[...] = top[...].astype(BF16)
    for j in range(7):
        taps = [top[:, t * W : (t + 1) * W] if t < 27 else jnp.zeros((32, W), F32) for t in range(4 * j, 4 * j + 4)]
        w2b_ref[:, j * W : (j + 1) * W] = jnp.concatenate(taps, axis=0).T.astype(BF16)


def forward_kernel(
    c0, c1, c2, c3, w2_ref, go_ref, xo_ref, xp_ref, xn_ref,
    y_ref, gs0_ref, gs1_ref, slope_ref, xa_ref, xi_ref,
    w1s, zs,
):
    x, zl = split()
    p = lax.axis_index("space")
    for k, c in enumerate((c0, c1, c2, c3)):
        w1s[rows32(xor(zl, k)), :] = c[...]

    def widen(ref, base):
        @pl.loop(0, 20)
        def _(r):
            a, b, c = shifted(ref[r].astype(F32))
            xi_ref[base + r, 0:64] = a.astype(BF16)
            xi_ref[base + r, 64:128] = b.astype(BF16)
            xi_ref[base + r, 128:192] = c.astype(BF16)

    widen(xp_ref, 0)
    widen(xo_ref, 20)
    widen(xn_ref, 40)

    w1 = w1s[:, :K1]

    @pl.loop(0, 16)
    def _(i):
        dd = lax.div(i, 4)
        hh = lax.rem(i, 4) * 2
        cols = []
        for j in range(2):
            cols.append(
                jnp.concatenate(
                    [xi_ref[(dd + a) * 10 + hh + j + b] for a in range(3) for b in range(3)], axis=0
                )
            )
        z = jnp.dot(w1, jnp.concatenate(cols, axis=1), preferred_element_type=F32)
        depth = p * 2 - 1 + dd
        for j in range(2):
            height = x * 4 - 2 + hh + j
            inside = (depth >= 0) & (depth < 16) & (height >= 0) & (height < 16)
            zr = z[:, j * W : (j + 1) * W]
            r = dd * 8 + hh + j
            zs[r] = zr
            act = jnp.where(inside, zr * logistic(zr), 0.0).astype(BF16).astype(F32)
            left, mid, right = shifted(act)
            xa_ref[r, 0:128] = left.astype(BF16)
            xa_ref[r, 128:256] = mid.astype(BF16)
            xa_ref[r, 256:384] = right.astype(BF16)

    for d in range(2):
        for h in range(4):
            v = zs[(d + 1) * 8 + h + 2, rows32(zl), :]
            q = logistic(v)
            slope_ref[:, (d * 4 + h) * W : (d * 4 + h + 1) * W] = q * (1.0 + v * (1.0 - q))

    w2 = w2_ref[...]
    for d in range(2):
        for hp in range(3):
            cols = []
            for j in range(2):
                hh = hp * 2 + j
                cols.append(
                    jnp.concatenate(
                        [xa_ref[(d + a) * 8 + hh + b] for a in range(3) for b in range(3)], axis=0
                    )
                )
            z = jnp.dot(w2, jnp.concatenate(cols, axis=1), preferred_element_type=F32)
            for j in range(2):
                hh = hp * 2 + j
                v = z[:, j * W : (j + 1) * W]
                q = logistic(v)
                if 1 <= hh <= 4:
                    at = (d * 4 + hh - 1) * W
                    y_ref[:, at : at + W] = (v * q).astype(BF16)
                g = go_ref[:, (d * 6 + hh) * W : (d * 6 + hh + 1) * W].astype(F32)
                gs = (g * (q * (1.0 + v * (1.0 - q)))).astype(BF16)
                (gs0_ref if d == 0 else gs1_ref)[hh] = gs


def second_kernel(xa_ref, gs0_ref, gs1_ref, dw_ref):
    gs = jnp.concatenate([(gs0_ref, gs1_ref)[d][h + 1] for d in range(2) for h in range(4)], axis=1)
    for a in range(3):
        for b in range(3):
            col = jnp.concatenate(
                [xa_ref[(d + a) * 8 + h + 1 + b] for d in range(2) for h in range(4)], axis=1
            )
            at = (a * 3 + b) * 384
            dw_ref[:, at : at + 384] = lax.dot_general(gs, col, NT, preferred_element_type=F32)


def back_kernel(gs0_ref, gs1_ref, gp_ref, gn_ref, w2b_ref, own_ref, s1, s2, s3, g3, acc):
    _, zl = split()
    for d, ref in enumerate((gp_ref, gs0_ref, gs1_ref, gn_ref)):
        for h in range(6):
            before, mid, after = shifted(ref[h].astype(F32))
            g3[d * 6 + h, 0:32] = after.astype(BF16)
            g3[d * 6 + h, 32:64] = mid.astype(BF16)
            g3[d * 6 + h, 64:96] = before.astype(BF16)
    w = w2b_ref[...]
    for d in range(2):
        for hp in range(2):
            cols = []
            for j in range(2):
                h = hp * 2 + j
                cols.append(
                    jnp.concatenate(
                        [g3[(d + 2 - a) * 6 + h + 2 - b] for a in range(3) for b in range(3)]
                        + [jnp.zeros((32, W), BF16)],
                        axis=0,
                    )
                )
            at = (d * 4 + hp * 2) * W
            acc[:, at : at + 2 * W] = jnp.dot(w, jnp.concatenate(cols, axis=1), preferred_element_type=F32)
    own_ref[...] = acc[rows32(zl), :]
    for k, out in enumerate((s1, s2, s3)):
        out[...] = acc[rows32(xor(zl, k + 1)), :].astype(BF16)


def first_kernel(own_ref, r1, r2, r3, slope_ref, xi_ref, dw2_ref, y_ref, o0, s1, s2, s3, low):
    x, _ = split()
    back = (own_ref[...] + r1[...].astype(F32)) + (r2[...].astype(F32) + r3[...].astype(F32))
    gf = (back * slope_ref[...]).astype(BF16)
    parts = []
    for a in range(3):
        col = jnp.concatenate(
            [
                jnp.concatenate(
                    [xi_ref[(d + 1 + a) * 10 + h + 2 + b] for d in range(2) for h in range(4)], axis=1
                )
                for b in range(3)
            ],
            axis=0,
        )
        parts.append(lax.dot_general(gf, col, NT, preferred_element_type=F32))
    low[:, :K1P] = jnp.concatenate(parts + [jnp.zeros((32, K1P - K1), F32)], axis=1)
    low[:, K1P : K1P + 1024] = y_ref[...].astype(F32)
    low[:, K1P + 1024 :] = jnp.zeros((32, K2 - K1P - 1024), F32)
    for k, out in enumerate((o0, s1, s2, s3)):
        at = rows8(xor(x, k))
        both = jnp.concatenate([dw2_ref[at, :], low[at, :]], axis=0)
        out[...] = both.astype(out.dtype)


def sum_kernel(o0, r1, r2, r3, dw_ref, y_ref):
    x, _ = split()
    parts = [o0[...], r1[...].astype(F32), r2[...].astype(F32), r3[...].astype(F32)]
    total = (parts[0] + parts[1]) + (parts[2] + parts[3])
    flat = jnp.concatenate([total[:8], total[8:, :K1P], jnp.zeros((8, W), F32)], axis=1)
    dw_ref[...] = jnp.concatenate([flat[:, :2688], flat[:, 2688:]], axis=0).astype(BF16)
    for k, v in enumerate(parts):
        h0 = xor(x, k) * 4
        for d in range(2):
            for h in range(4):
                at = K1P + (d * 4 + h) * W
                y_ref[d, h0 + h] = v[8:, at : at + W]


def last_kernel(a0, a1, a2, a3, dw1_ref, dw2_ref):
    v = [a[...].astype(F32) for a in (a0, a1, a2, a3)]
    total = ((v[0] + v[1]) + (v[2] + v[3])) * (1.0 / 256.0)
    top = total[:8].T
    bot = total[8:].T
    dw2_ref[:2688] = top
    dw2_ref[2688:] = bot[: K2 - 2688]
    dw1_ref[...] = bot[K2 - 2688 : K2 - 2688 + K1]


def local(act_in, w_first, w_second, grad_out):
    X = [[(z * 4 + x, z * 4 + (x ^ k)) for z in range(4) for x in range(4)] for k in range(4)]
    Z = [[(z * 4 + x, (z ^ k) * 4 + x) for z in range(4) for x in range(4)] for k in range(4)]
    up = [(i, i + 1) for i in range(7)]
    down = [(i + 1, i) for i in range(7)]
    x = lax.rem(lax.axis_index("filt"), 4)

    b = run(
        pack_kernel,
        [sds((16, K2), BF16)] * 4,
        [w_first.reshape(K1, 8), w_second.reshape(K2, 8), grad_out[0]],
        [pltpu.VMEM((2, 18, 8, W), F32)],
    )
    b = [b[0]] + [lax.ppermute(b[k], "filt", X[k]) for k in (1, 2, 3)]

    rows = jnp.pad(jnp.transpose(act_in[0], (1, 2, 0, 3)), ((0, 0), (3, 3), (0, 0), (0, 0)))
    xo = lax.dynamic_slice_in_dim(rows, x * 4, 10, axis=1).reshape(20, 64, W)
    xp = lax.ppermute(xo, "space", up)
    xn = lax.ppermute(xo, "space", down)

    w1, w2, go, w2b = run(
        group_kernel,
        [sds((32, K1P), BF16), sds((32, K2), BF16), sds((32, 12 * W), BF16), sds((128, KB), BF16)],
        b,
        [pltpu.VMEM((32, K2), F32), pltpu.VMEM((32, K2), F32)],
    )
    c = [w1] + [lax.ppermute(w1, "filt", Z[k]) for k in (1, 2, 3)]

    y, gs0, gs1, slope, xa, xi = run(
        forward_kernel,
        [
            sds((32, 1024), BF16),
            sds((6, 32, W), BF16),
            sds((6, 32, W), BF16),
            sds((32, 1024), F32),
            sds((32, 384, W), BF16),
            sds((60, 192, W), BF16),
        ],
        c + [w2, go, xo, xp, xn],
        [pltpu.VMEM((128, K1P), BF16), pltpu.VMEM((32, 128, W), F32)],
    )
    gp = lax.ppermute(gs1, "space", up)
    gn = lax.ppermute(gs0, "space", down)
    (dw2,) = run(second_kernel, [sds((32, K2), F32)], [xa, gs0, gs1])

    own, *s = run(
        back_kernel,
        [sds((32, 1024), F32)] + [sds((32, 1024), BF16)] * 3,
        [gs0, gs1, gp, gn, w2b],
        [pltpu.VMEM((24, 96, W), BF16), pltpu.VMEM((128, 1024), F32)],
    )
    s = [lax.ppermute(s[k - 1], "filt", Z[k]) for k in (1, 2, 3)]

    o, *s = run(
        first_kernel,
        [sds((16, K2), F32)] + [sds((16, K2), BF16)] * 3,
        [own] + s + [slope, xi, dw2, y],
        [pltpu.VMEM((32, K2), F32)],
    )
    s = [lax.ppermute(s[k - 1], "filt", X[k]) for k in (1, 2, 3)]
    part, yt = run(sum_kernel, [sds((16, 2688), BF16), sds((2, 16, 8, W), F32)], [o] + s)
    y_out = jnp.transpose(yt, (2, 0, 1, 3)).astype(BF16)[None]

    def pair(ds, dc):
        return [(s * 8 + i, (s ^ ds) * 8 + (i ^ dc)) for s in range(2) for i in range(8)]

    both = ("sample", "space")
    q = [part] + [lax.ppermute(part, both, pair(ds, dc)) for ds, dc in ((0, 1), (1, 0), (1, 1))]
    q = [v.astype(F32) for v in q]
    part = ((q[0] + q[1]) + (q[2] + q[3])).astype(BF16)
    q = [part] + [lax.ppermute(part, "space", [(i, i ^ (2 * k)) for i in range(8)]) for k in (1, 2, 3)]
    dw1, dw2 = run(last_kernel, [sds((K1, 8), F32), sds((K2, 8), F32)], q)
    return y_out, dw1.reshape(27, 64, 8), dw2.reshape(27, 128, 8)


def solution(mesh):
    placed = (
        P("sample", None, "space", None, None),
        P(None, None, "filt"),
        P(None, None, "filt"),
        P("sample", "filt", "space", None, None),
    )
    return jax.shard_map(
        local,
        mesh=mesh,
        in_specs=placed,
        out_specs=(
            P("sample", "filt", "space", None, None),
            P(None, None, "filt"),
            P(None, None, "filt"),
        ),
        check_vma=False,
    )
```

time: 613 us -> 104 us (0.17); the launches traced: 603 us -> 102 us
  waiting for transfers between devices: 298 us -> 34 us
  matrix products: 98.5 us -> 0 us
  blocking collectives: 87.6 us -> 0 us
  local copies, waits for them, and re-layouts: 71.8 us -> 8.3 us
  Pallas kernels: 0 us -> 19.9 us
  starting transfers between devices: 21 us -> 39.4 us
  between operations: 14.2 us -> 0.81 us
  other arithmetic: 11.9 us -> 0.06 us
    psum x1 -> x0, waiting for transfers between devices: 149 us -> none  [local(): sum_first, sum_second = lax.psum((dw_first, dw_second), ('sample', 'space'))]
    psum x1 -> x0, blocking collectives: 87.6 us -> none  [local(): sum_first, sum_second = lax.psum((dw_first, dw_second), ('sample', 'space'))]
    reduce_scatter x1 -> x0, waiting for transfers between devices: 78.4 us -> none  [local(): lax.psum_scatter(transpose_correlate(grad_rim, w_second, 1), 'filt', scat...]
    all_gather x1 -> x0, waiting for transfers between devices: 67.3 us -> none  [local(): gathered = lax.all_gather(act_ext, 'filt', axis=0, tiled=True)]
    transpose x2 -> x0, matrix products: 65.5 us -> none  [kernel_gradient(): jnp.transpose(result, (2, 3, 4, 0, 1))]
    conv_general_dilated x3 -> x0, matrix products: 33 us -> none  [the longest x2 27.8 us: correlate(): lax.conv_general_dilated(source[None], taps, (1, 1, 1), ((0, 0), (rim_pad...]
    ppermute x4 -> x22, waiting for transfers between devices: 3.34 us -> 34 us  [the longest x3 8.68 us: local(): c = [w1] + [lax.ppermute(w1, 'filt', Z[k]) for k in (1, 2, 3)]]
    conv_general_dilated x14 -> x0, local copies, waits for them, and re-layouts: 29 us -> none  [the longest x9 18.8 us: correlate(): lax.conv_general_dilated(source[None], taps, (1, 1, 1), ((0, 0), (rim_pad...]
  transfers between devices with their start and end apart: 7 -> 22, of which waited for: 5 -> 14; matrix products, arithmetic and copies ran while one was open for 13% -> 3% of each run, Pallas kernels for 0% -> 3%
where the time goes in v1:
time: 104 us; the launch traced here: 102 us
  starting transfers between devices  39.4 us (38%)
  waiting for transfers between devices  34 us (33%)
  Pallas kernels  19.9 us (19%)
  local copies, waits for them, and re-layouts  8.3 us (8%)
    pallas_call x8, Pallas kernels, run(): pl.pallas_call(kernel, out_shape=outs, in_specs=[VMEM] * len(args), out_s...  19.9 us
    ppermute x3, waiting for transfers between devices, local(): c = [w1] + [lax.ppermute(w1, 'filt', Z[k]) for k in (1, 2, 3)]  8.68 us
    ppermute x3, waiting for transfers between devices, local(): lax.ppermute(part, both, pair(ds, dc))  7.8 us
    ppermute x3, waiting for transfers between devices, local(): b = [b[0]] + [lax.ppermute(b[k], 'filt', X[k]) for k in (1, 2, 3)]  7.27 us
    unnamed x9, local copies, waits for them, and re-layouts  6.91 us
    ppermute x3, starting transfers between devices, local(): lax.ppermute(part, both, pair(ds, dc))  6.61 us
    ppermute x3, waiting for transfers between devices, local(): s = [lax.ppermute(s[k - 1], 'filt', X[k]) for k in (1, 2, 3)]  5.28 us
    ppermute x1, starting transfers between devices, local(): xn = lax.ppermute(xo, 'space', down)  5.15 us
  transfers between devices with their start and end apart: 22, of which 14 were waited for; matrix products, arithmetic and copies ran while one was open for 3% of the time, Pallas kernels for 3%

profile of v1, /device:TPU:1, one launch (start us, length us, event | category | flops | bytes accessed | tf_op | source)
XLA Modules:
  0.0 102.4 jit_solution(13526353252186539213)
XLA Ops:
  0.6 1.3 %pad_dynamic-slice_fusion = bf16[2,10,64,128]{3,1,0,2:T(8,128)(2,1)S(1)} fusion(s32[]{:T(128)S(6)} %select_n.3, bf16[2,16,64,128]{3,1,0,2:T(8,128)(2,1)} %bitcast.21), kind=kLoop, calls=%fused_computation | loop fusion | bytes 851972 | tf_op jit(solution)/shard_map/dynamic_slice | solution.py:276
  2.0 5.1 %collective-permute-start.7 = (bf16[20,64,128]{2,1,0:T(8,128)(2,1)S(1)}, bf16[20,64,128]{2,1,0:T(8,128)(2,1)S(1)}, u32[]{:S(2)}, u32[]{:S(2)}) collective-permute-start(bf16[20,64,128]{2,1,0:T(8,128)(2,1)S(1)} %bitcast.16), channel_id=1, source_target_pairs={{16,0},{32,16},{48,32},{64,48},{80,64},{96,80},{112,96},{17,1},{33... | collective-permute-start | bytes 983048 | tf_op jit(solution)/shard_map/ppermute | solution.py:278
  7.2 1.9 %collective-permute-start.6 = (bf16[20,64,128]{2,1,0:T(8,128)(2,1)S(1)}, bf16[20,64,128]{2,1,0:T(8,128)(2,1)S(1)}, u32[]{:S(2)}, u32[]{:S(2)}) collective-permute-start(bf16[20,64,128]{2,1,0:T(8,128)(2,1)S(1)} %bitcast.17), channel_id=1, source_target_pairs={{0,16},{16,32},{32,48},{48,64},{64,80},{80,96},{96,112},{1,17},{17... | collective-permute-start | bytes 983048 | tf_op jit(solution)/shard_map/ppermute | solution.py:277
  12.6 2.4 %collective-permute-start.1 = (bf16[16,3456]{1,0:T(8,128)(2,1)S(1)}, bf16[16,3456]{1,0:T(8,128)(2,1)S(1)}, u32[]{:S(2)}, u32[]{:S(2)}) collective-permute-start(bf16[16,3456]{1,0:T(8,128)(2,1)S(1)} %get-tuple-element.31), channel_id=1, source_target_pairs={{0,2},{1,3},{2,0},{3,1},{4,6},{5,7},{6,4},{7,5},{8,10},{9,11},{10,... | collective-permute-start | bytes 331784 | tf_op jit(solution)/shard_map/ppermute | solution.py:273
  16.0 4.5 %collective-permute-done.1.b2 = bf16[16,3456]{1,0:T(8,128)(2,1)S(1)} collective-permute-done((bf16[16,3456]{1,0:T(8,128)(2,1)S(1)}, bf16[16,3456]{1,0:T(8,128)(2,1)S(1)}, u32[]{:S(2)}, u32[]{:S(2)}) %collective-permute-start.1) | collective-permute-done | bytes 110624 | tf_op jit(solution)/shard_map/ppermute | solution.py:273
  20.5 2.5 %collective-permute-done.2.b3 = bf16[16,3456]{1,0:T(8,128)(2,1)S(1)} collective-permute-done((bf16[16,3456]{1,0:T(8,128)(2,1)S(1)}, bf16[16,3456]{1,0:T(8,128)(2,1)S(1)}, u32[]{:S(2)}, u32[]{:S(2)}) %collective-permute-start.2) | collective-permute-done | bytes 110624 | tf_op jit(solution)/shard_map/ppermute | solution.py:273
  23.3 4.4 %collective-permute-start.5 = (bf16[32,1792]{1,0:T(8,128)(2,1)S(1)}, bf16[32,1792]{1,0:T(8,128)(2,1)S(1)}, u32[]{:S(2)}, u32[]{:S(2)}) collective-permute-start(bf16[32,1792]{1,0:T(8,128)(2,1)S(1)} %get-tuple-element.33.c0), channel_id=1, source_target_pairs={{0,12},{1,13},{2,14},{3,15},{4,8},{5,9},{6,10},{7,11},{8,4},{9,5},... | collective-permute-start | bytes 344072 | tf_op jit(solution)/shard_map/ppermute | solution.py:286
  28.1 2.8 %collective-permute-done.5.c3 = bf16[32,1792]{1,0:T(8,128)(2,1)S(1)} collective-permute-done((bf16[32,1792]{1,0:T(8,128)(2,1)S(1)}, bf16[32,1792]{1,0:T(8,128)(2,1)S(1)}, u32[]{:S(2)}, u32[]{:S(2)}) %collective-permute-start.5) | collective-permute-done | bytes 114720 | tf_op jit(solution)/shard_map/ppermute | solution.py:286
  30.9 5.9 %collective-permute-done.4.c2 = bf16[32,1792]{1,0:T(8,128)(2,1)S(1)} collective-permute-done((bf16[32,1792]{1,0:T(8,128)(2,1)S(1)}, bf16[32,1792]{1,0:T(8,128)(2,1)S(1)}, u32[]{:S(2)}, u32[]{:S(2)}) %collective-permute-start.4) | collective-permute-done | bytes 114720 | tf_op jit(solution)/shard_map/ppermute | solution.py:286
  36.8 14.6 %shard_map.69 = (bf16[32,1024]{1,0:T(8,128)(2,1)S(1)}, bf16[6,32,128]{2,1,0:T(8,128)(2,1)S(1)}, bf16[6,32,128]{2,1,0:T(8,128)(2,1)S(1)}, f32[32,1024]{1,0:T(8,12...) custom-call(bf16[32,1792]{1,0:T(8,128)(2,1)S(1)} %get-tuple-element.33.c0, ...), custom_call_target="tpu_custom_call" | custom-call | tf_op jit(solution)/shard_map/pallas_call | solution.py:19
  51.4 3.0 %collective-permute-start.9 = (bf16[6,32,128]{2,1,0:T(8,128)(2,1)S(1)}, bf16[6,32,128]{2,1,0:T(8,128)(2,1)S(1)}, u32[]{:S(2)}, u32[]{:S(2)}) collective-permute-start(bf16[6,32,128]{2,1,0:T(8,128)(2,1)S(1)} %get-tuple-element.36.gs0_ref), channel_id=1, source_target_pairs={{16,0},{32,16},{48,32},{64,48},{80,64},{96,80},{112,96},{17,1},{33... | collective-permute-start | bytes 147464 | tf_op jit(solution)/shard_map/ppermute | solution.py:302
  54.4 3.1 %collective-permute-start.8 = (bf16[6,32,128]{2,1,0:T(8,128)(2,1)S(1)}, bf16[6,32,128]{2,1,0:T(8,128)(2,1)S(1)}, u32[]{:S(2)}, u32[]{:S(2)}) collective-permute-start(bf16[6,32,128]{2,1,0:T(8,128)(2,1)S(1)} %get-tuple-element.37.gs1_ref), channel_id=1, source_target_pairs={{0,16},{16,32},{32,48},{48,64},{64,80},{80,96},{96,112},{1,17},{17... | collective-permute-start | bytes 147464 | tf_op jit(solution)/shard_map/ppermute | solution.py:301
  59.7 2.3 %collective-permute-start.11 = (bf16[32,1024]{1,0:T(8,128)(2,1)S(1)}, bf16[32,1024]{1,0:T(8,128)(2,1)S(1)}, u32[]{:S(2)}, u32[]{:S(2)}) collective-permute-start(bf16[32,1024]{1,0:T(8,128)(2,1)S(1)} %get-tuple-element.41), channel_id=1, source_target_pairs={{0,8},{1,9},{2,10},{3,11},{4,12},{5,13},{6,14},{7,15},{8,0},{9,1},... | collective-permute-start | bytes 196616 | tf_op jit(solution)/shard_map/ppermute | solution.py:311
  62.8 1.9 %copy-done = bf16[32,384,128]{2,1,0:T(8,128)(2,1)S(1)} copy-done((bf16[32,384,128]{2,1,0:T(8,128)(2,1)S(1)}, bf16[32,384,128]{2,1,0:T(8,128)(2,1)}, u32[]{:S(2)}) %copy-start) | copy-done | bytes 3145752
  64.7 2.1 %shard_map.71.dw2_ref = f32[32,3456]{1,0:T(8,128)S(1)} custom-call(bf16[32,384,128]{2,1,0:T(8,128)(2,1)S(1)} %copy-done, bf16[6,32,128]{2,1,0:T(8,128)(2,1)S(1)} %get-tuple-element.36.gs0_ref, bf16[6,32,128]{2,1,0:T(8,128)(2,1)S(1)} %get-tuple-element.37.gs1_ref), custom_call_target="tpu_custom_call" | custom-call | tf_op jit(solution)/shard_map/pallas_call | solution.py:19
  69.1 1.5 %collective-permute-start.14 = (bf16[16,3456]{1,0:T(8,128)(2,1)S(1)}, bf16[16,3456]{1,0:T(8,128)(2,1)S(1)}, u32[]{:S(2)}, u32[]{:S(2)}) collective-permute-start(bf16[16,3456]{1,0:T(8,128)(2,1)S(1)} %get-tuple-element.49), channel_id=1, source_target_pairs={{0,2},{1,3},{2,0},{3,1},{4,6},{5,7},{6,4},{7,5},{8,10},{9,11},{10,... | collective-permute-start | bytes 331784 | tf_op jit(solution)/shard_map/ppermute | solution.py:319
  70.5 2.4 %collective-permute-start.15 = (bf16[16,3456]{1,0:T(8,128)(2,1)S(1)}, bf16[16,3456]{1,0:T(8,128)(2,1)S(1)}, u32[]{:S(2)}, u32[]{:S(2)}) collective-permute-start(bf16[16,3456]{1,0:T(8,128)(2,1)S(1)} %get-tuple-element.50), channel_id=1, source_target_pairs={{0,3},{1,2},{2,1},{3,0},{4,7},{5,6},{6,5},{7,4},{8,11},{9,10},{10,... | collective-permute-start | bytes 331784 | tf_op jit(solution)/shard_map/ppermute | solution.py:319
  73.2 2.5 %collective-permute-done.14.r2 = bf16[16,3456]{1,0:T(8,128)(2,1)S(1)} collective-permute-done((bf16[16,3456]{1,0:T(8,128)(2,1)S(1)}, bf16[16,3456]{1,0:T(8,128)(2,1)S(1)}, u32[]{:S(2)}, u32[]{:S(2)}) %collective-permute-start.14) | collective-permute-done | bytes 110624 | tf_op jit(solution)/shard_map/ppermute | solution.py:319
  75.7 2.5 %collective-permute-done.15.r3 = bf16[16,3456]{1,0:T(8,128)(2,1)S(1)} collective-permute-done((bf16[16,3456]{1,0:T(8,128)(2,1)S(1)}, bf16[16,3456]{1,0:T(8,128)(2,1)S(1)}, u32[]{:S(2)}, u32[]{:S(2)}) %collective-permute-start.15) | collective-permute-done | bytes 110624 | tf_op jit(solution)/shard_map/ppermute | solution.py:319
  78.3 6.1 %collective-permute-start.18 = (bf16[16,2688]{1,0:T(8,128)(2,1)S(1)}, bf16[16,2688]{1,0:T(8,128)(2,1)S(1)}, u32[]{:S(2)}, u32[]{:S(2)}) collective-permute-start(bf16[16,2688]{1,0:T(8,128)(2,1)S(1)} %get-tuple-element.52), channel_id=1, source_target_pairs={{0,144},{16,128},{32,176},{48,160},{64,208},{80,192},{96,240},{112... | collective-permute-start | bytes 258056 | tf_op jit(solution)/shard_map/ppermute | solution.py:327
  84.9 2.8 %collective-permute-done.18 = bf16[16,2688]{1,0:T(8,128)(2,1)S(1)} collective-permute-done((bf16[16,2688]{1,0:T(8,128)(2,1)S(1)}, bf16[16,2688]{1,0:T(8,128)(2,1)S(1)}, u32[]{:S(2)}, u32[]{:S(2)}) %collective-permute-start.18) | collective-permute-done | bytes 86048 | tf_op jit(solution)/shard_map/ppermute | solution.py:327
  87.6 5.0 %collective-permute-done.17 = bf16[16,2688]{1,0:T(8,128)(2,1)S(1)} collective-permute-done((bf16[16,2688]{1,0:T(8,128)(2,1)S(1)}, bf16[16,2688]{1,0:T(8,128)(2,1)S(1)}, u32[]{:S(2)}, u32[]{:S(2)}) %collective-permute-start.17) | collective-permute-done | bytes 86048 | tf_op jit(solution)/shard_map/ppermute | solution.py:327
  92.7 1.6 %collective-permute-start.21 = (bf16[16,2688]{1,0:T(8,128)(2,1)S(1)}, bf16[16,2688]{1,0:T(8,128)(2,1)S(1)}, u32[]{:S(2)}, u32[]{:S(2)}) collective-permute-start(bf16[16,2688]{1,0:T(8,128)(2,1)S(1)} %add_convert_fusion.a0), channel_id=1, source_target_pairs={{0,96},{16,112},{32,64},{48,80},{64,32},{80,48},{96,0},{112,16},{1... | collective-permute-start | bytes 258056 | tf_op jit(solution)/shard_map/ppermute | solution.py:330
  97.3 2.2 %collective-permute-done.20.a2 = bf16[16,2688]{1,0:T(8,128)(2,1)S(1)} collective-permute-done((bf16[16,2688]{1,0:T(8,128)(2,1)S(1)}, bf16[16,2688]{1,0:T(8,128)(2,1)S(1)}, u32[]{:S(2)}, u32[]{:S(2)}) %collective-permute-start.20) | collective-permute-done | bytes 86048 | tf_op jit(solution)/shard_map/ppermute | solution.py:330
  (41 shorter events, 17.2 us)
Async XLA Ops:
  0.6 10.8 %copy-start.1 = (bf16[1,8,2,16,128]{4,3,2,1,0:T(8,128)(2,1)S(1)}, bf16[1,8,2,16,128]{4,3,2,1,0:T(8,128)(2,1)}, u32[]{:S(2)}) copy-start(bf16[1,8,2,16,128]{4,3,2,1,0:T(8,128)(2,1)} %param.7) | copy-start | bytes 196612
  2.0 34.7 %collective-permute-start.7 = (bf16[20,64,128]{2,1,0:T(8,128)(2,1)S(1)}, bf16[20,64,128]{2,1,0:T(8,128)(2,1)S(1)}, u32[]{:S(2)}, u32[]{:S(2)}) collective-permute-start(bf16[20,64,128]{2,1,0:T(8,128)(2,1)S(1)} %bitcast.16), channel_id=1, source_target_pairs={{16,0},{32,16},{48,32},{64,48},{80,64},{96,80},{112,96},{17,1},{33... | collective-permute-start | bytes 983048 | tf_op jit(solution)/shard_map/ppermute | solution.py:278
  7.2 29.5 %collective-permute-start.6 = (bf16[20,64,128]{2,1,0:T(8,128)(2,1)S(1)}, bf16[20,64,128]{2,1,0:T(8,128)(2,1)S(1)}, u32[]{:S(2)}, u32[]{:S(2)}) collective-permute-start(bf16[20,64,128]{2,1,0:T(8,128)(2,1)S(1)} %bitcast.17), channel_id=1, source_target_pairs={{0,16},{16,32},{32,48},{48,64},{64,80},{80,96},{96,112},{1,17},{17... | collective-permute-start | bytes 983048 | tf_op jit(solution)/shard_map/ppermute | solution.py:277
  11.8 4.2 %collective-permute-start = (bf16[16,3456]{1,0:T(8,128)(2,1)S(1)}, bf16[16,3456]{1,0:T(8,128)(2,1)S(1)}, u32[]{:S(2)}, u32[]{:S(2)}) collective-permute-start(bf16[16,3456]{1,0:T(8,128)(2,1)S(1)} %get-tuple-element.30), channel_id=1, source_target_pairs={{0,1},{1,0},{2,3},{3,2},{4,5},{5,4},{6,7},{7,6},{8,9},{9,8},{10,11... | collective-permute-start | bytes 331784 | tf_op jit(solution)/shard_map/ppermute | solution.py:273
  12.6 7.9 %collective-permute-start.1 = (bf16[16,3456]{1,0:T(8,128)(2,1)S(1)}, bf16[16,3456]{1,0:T(8,128)(2,1)S(1)}, u32[]{:S(2)}, u32[]{:S(2)}) collective-permute-start(bf16[16,3456]{1,0:T(8,128)(2,1)S(1)} %get-tuple-element.31), channel_id=1, source_target_pairs={{0,2},{1,3},{2,0},{3,1},{4,6},{5,7},{6,4},{7,5},{8,10},{9,11},{10,... | collective-permute-start | bytes 331784 | tf_op jit(solution)/shard_map/ppermute | solution.py:273
  14.9 8.1 %collective-permute-start.2 = (bf16[16,3456]{1,0:T(8,128)(2,1)S(1)}, bf16[16,3456]{1,0:T(8,128)(2,1)S(1)}, u32[]{:S(2)}, u32[]{:S(2)}) collective-permute-start(bf16[16,3456]{1,0:T(8,128)(2,1)S(1)} %get-tuple-element.32), channel_id=1, source_target_pairs={{0,3},{1,2},{2,1},{3,0},{4,7},{5,6},{6,5},{7,4},{8,11},{9,10},{10,... | collective-permute-start | bytes 331784 | tf_op jit(solution)/shard_map/ppermute | solution.py:273
  23.3 7.6 %collective-permute-start.5 = (bf16[32,1792]{1,0:T(8,128)(2,1)S(1)}, bf16[32,1792]{1,0:T(8,128)(2,1)S(1)}, u32[]{:S(2)}, u32[]{:S(2)}) collective-permute-start(bf16[32,1792]{1,0:T(8,128)(2,1)S(1)} %get-tuple-element.33.c0), channel_id=1, source_target_pairs={{0,12},{1,13},{2,14},{3,15},{4,8},{5,9},{6,10},{7,11},{8,4},{9,5},... | collective-permute-start | bytes 344072 | tf_op jit(solution)/shard_map/ppermute | solution.py:286
  27.7 9.1 %collective-permute-start.4 = (bf16[32,1792]{1,0:T(8,128)(2,1)S(1)}, bf16[32,1792]{1,0:T(8,128)(2,1)S(1)}, u32[]{:S(2)}, u32[]{:S(2)}) collective-permute-start(bf16[32,1792]{1,0:T(8,128)(2,1)S(1)} %get-tuple-element.33.c0), channel_id=1, source_target_pairs={{0,8},{1,9},{2,10},{3,11},{4,12},{5,13},{6,14},{7,15},{8,0},{9,1},... | collective-permute-start | bytes 344072 | tf_op jit(solution)/shard_map/ppermute | solution.py:286
  27.7 9.1 %collective-permute-start.3 = (bf16[32,1792]{1,0:T(8,128)(2,1)S(1)}, bf16[32,1792]{1,0:T(8,128)(2,1)S(1)}, u32[]{:S(2)}, u32[]{:S(2)}) collective-permute-start(bf16[32,1792]{1,0:T(8,128)(2,1)S(1)} %get-tuple-element.33.c0), channel_id=1, source_target_pairs={{0,4},{1,5},{2,6},{3,7},{4,0},{5,1},{6,2},{7,3},{8,12},{9,13},{10,... | collective-permute-start | bytes 344072 | tf_op jit(solution)/shard_map/ppermute | solution.py:286
  51.4 6.1 %collective-permute-start.9 = (bf16[6,32,128]{2,1,0:T(8,128)(2,1)S(1)}, bf16[6,32,128]{2,1,0:T(8,128)(2,1)S(1)}, u32[]{:S(2)}, u32[]{:S(2)}) collective-permute-start(bf16[6,32,128]{2,1,0:T(8,128)(2,1)S(1)} %get-tuple-element.36.gs0_ref), channel_id=1, source_target_pairs={{16,0},{32,16},{48,32},{64,48},{80,64},{96,80},{112,96},{17,1},{33... | collective-permute-start | bytes 147464 | tf_op jit(solution)/shard_map/ppermute | solution.py:302
  54.4 4.2 %collective-permute-start.8 = (bf16[6,32,128]{2,1,0:T(8,128)(2,1)S(1)}, bf16[6,32,128]{2,1,0:T(8,128)(2,1)S(1)}, u32[]{:S(2)}, u32[]{:S(2)}) collective-permute-start(bf16[6,32,128]{2,1,0:T(8,128)(2,1)S(1)} %get-tuple-element.37.gs1_ref), channel_id=1, source_target_pairs={{0,16},{16,32},{32,48},{48,64},{64,80},{80,96},{96,112},{1,17},{17... | collective-permute-start | bytes 147464 | tf_op jit(solution)/shard_map/ppermute | solution.py:301
  59.2 7.7 %collective-permute-start.10 = (bf16[32,1024]{1,0:T(8,128)(2,1)S(1)}, bf16[32,1024]{1,0:T(8,128)(2,1)S(1)}, u32[]{:S(2)}, u32[]{:S(2)}) collective-permute-start(bf16[32,1024]{1,0:T(8,128)(2,1)S(1)} %get-tuple-element.40), channel_id=1, source_target_pairs={{0,4},{1,5},{2,6},{3,7},{4,0},{5,1},{6,2},{7,3},{8,12},{9,13},{10,... | collective-permute-start | bytes 196616 | tf_op jit(solution)/shard_map/ppermute | solution.py:311
  59.7 7.2 %collective-permute-start.11 = (bf16[32,1024]{1,0:T(8,128)(2,1)S(1)}, bf16[32,1024]{1,0:T(8,128)(2,1)S(1)}, u32[]{:S(2)}, u32[]{:S(2)}) collective-permute-start(bf16[32,1024]{1,0:T(8,128)(2,1)S(1)} %get-tuple-element.41), channel_id=1, source_target_pairs={{0,8},{1,9},{2,10},{3,11},{4,12},{5,13},{6,14},{7,15},{8,0},{9,1},... | collective-permute-start | bytes 196616 | tf_op jit(solution)/shard_map/ppermute | solution.py:311
  61.9 5.9 %collective-permute-start.12 = (bf16[32,1024]{1,0:T(8,128)(2,1)S(1)}, bf16[32,1024]{1,0:T(8,128)(2,1)S(1)}, u32[]{:S(2)}, u32[]{:S(2)}) collective-permute-start(bf16[32,1024]{1,0:T(8,128)(2,1)S(1)} %get-tuple-element.42), channel_id=1, source_target_pairs={{0,12},{1,13},{2,14},{3,15},{4,8},{5,9},{6,10},{7,11},{8,4},{9,5},... | collective-permute-start | bytes 196616 | tf_op jit(solution)/shard_map/ppermute | solution.py:311
  62.8 1.9 %copy-start = (bf16[32,384,128]{2,1,0:T(8,128)(2,1)S(1)}, bf16[32,384,128]{2,1,0:T(8,128)(2,1)}, u32[]{:S(2)}) copy-start(bf16[32,384,128]{2,1,0:T(8,128)(2,1)} %get-tuple-element.45.xa_ref) | copy-start | bytes 9437188
  69.0 4.2 %collective-permute-start.13 = (bf16[16,3456]{1,0:T(8,128)(2,1)S(1)}, bf16[16,3456]{1,0:T(8,128)(2,1)S(1)}, u32[]{:S(2)}, u32[]{:S(2)}) collective-permute-start(bf16[16,3456]{1,0:T(8,128)(2,1)S(1)} %get-tuple-element.48), channel_id=1, source_target_pairs={{0,1},{1,0},{2,3},{3,2},{4,5},{5,4},{6,7},{7,6},{8,9},{9,8},{10,11... | collective-permute-start | bytes 331784 | tf_op jit(solution)/shard_map/ppermute | solution.py:319
  69.1 6.6 %collective-permute-start.14 = (bf16[16,3456]{1,0:T(8,128)(2,1)S(1)}, bf16[16,3456]{1,0:T(8,128)(2,1)S(1)}, u32[]{:S(2)}, u32[]{:S(2)}) collective-permute-start(bf16[16,3456]{1,0:T(8,128)(2,1)S(1)} %get-tuple-element.49), channel_id=1, source_target_pairs={{0,2},{1,3},{2,0},{3,1},{4,6},{5,7},{6,4},{7,5},{8,10},{9,11},{10,... | collective-permute-start | bytes 331784 | tf_op jit(solution)/shard_map/ppermute | solution.py:319
  70.5 7.7 %collective-permute-start.15 = (bf16[16,3456]{1,0:T(8,128)(2,1)S(1)}, bf16[16,3456]{1,0:T(8,128)(2,1)S(1)}, u32[]{:S(2)}, u32[]{:S(2)}) collective-permute-start(bf16[16,3456]{1,0:T(8,128)(2,1)S(1)} %get-tuple-element.50), channel_id=1, source_target_pairs={{0,3},{1,2},{2,1},{3,0},{4,7},{5,6},{6,5},{7,4},{8,11},{9,10},{10,... | collective-permute-start | bytes 331784 | tf_op jit(solution)/shard_map/ppermute | solution.py:319
  78.3 9.4 %collective-permute-start.18 = (bf16[16,2688]{1,0:T(8,128)(2,1)S(1)}, bf16[16,2688]{1,0:T(8,128)(2,1)S(1)}, u32[]{:S(2)}, u32[]{:S(2)}) collective-permute-start(bf16[16,2688]{1,0:T(8,128)(2,1)S(1)} %get-tuple-element.52), channel_id=1, source_target_pairs={{0,144},{16,128},{32,176},{48,160},{64,208},{80,192},{96,240},{112... | collective-permute-start | bytes 258056 | tf_op jit(solution)/shard_map/ppermute | solution.py:327
  84.4 8.3 %collective-permute-start.17 = (bf16[16,2688]{1,0:T(8,128)(2,1)S(1)}, bf16[16,2688]{1,0:T(8,128)(2,1)S(1)}, u32[]{:S(2)}, u32[]{:S(2)}) collective-permute-start(bf16[16,2688]{1,0:T(8,128)(2,1)S(1)} %get-tuple-element.52), channel_id=1, source_target_pairs={{0,128},{16,144},{32,160},{48,176},{64,192},{80,208},{96,224},{112... | collective-permute-start | bytes 258056 | tf_op jit(solution)/shard_map/ppermute | solution.py:327
  84.6 8.1 %collective-permute-start.16 = (bf16[16,2688]{1,0:T(8,128)(2,1)S(1)}, bf16[16,2688]{1,0:T(8,128)(2,1)S(1)}, u32[]{:S(2)}, u32[]{:S(2)}) collective-permute-start(bf16[16,2688]{1,0:T(8,128)(2,1)S(1)} %get-tuple-element.52), channel_id=1, source_target_pairs={{0,16},{16,0},{32,48},{48,32},{64,80},{80,64},{96,112},{112,96},{1... | collective-permute-start | bytes 258056 | tf_op jit(solution)/shard_map/ppermute | solution.py:327
  92.7 4.6 %collective-permute-start.21 = (bf16[16,2688]{1,0:T(8,128)(2,1)S(1)}, bf16[16,2688]{1,0:T(8,128)(2,1)S(1)}, u32[]{:S(2)}, u32[]{:S(2)}) collective-permute-start(bf16[16,2688]{1,0:T(8,128)(2,1)S(1)} %add_convert_fusion.a0), channel_id=1, source_target_pairs={{0,96},{16,112},{32,64},{48,80},{64,32},{80,48},{96,0},{112,16},{1... | collective-permute-start | bytes 258056 | tf_op jit(solution)/shard_map/ppermute | solution.py:330
  94.4 5.2 %collective-permute-start.20 = (bf16[16,2688]{1,0:T(8,128)(2,1)S(1)}, bf16[16,2688]{1,0:T(8,128)(2,1)S(1)}, u32[]{:S(2)}, u32[]{:S(2)}) collective-permute-start(bf16[16,2688]{1,0:T(8,128)(2,1)S(1)} %add_convert_fusion.a0), channel_id=1, source_target_pairs={{0,64},{16,80},{32,96},{48,112},{64,0},{80,16},{96,32},{112,48},{1... | collective-permute-start | bytes 258056 | tf_op jit(solution)/shard_map/ppermute | solution.py:330
  95.4 4.2 %collective-permute-start.19 = (bf16[16,2688]{1,0:T(8,128)(2,1)S(1)}, bf16[16,2688]{1,0:T(8,128)(2,1)S(1)}, u32[]{:S(2)}, u32[]{:S(2)}) collective-permute-start(bf16[16,2688]{1,0:T(8,128)(2,1)S(1)} %add_convert_fusion.a0), channel_id=1, source_target_pairs={{0,32},{16,48},{32,0},{48,16},{64,96},{80,112},{96,64},{112,80},{1... | collective-permute-start | bytes 258056 | tf_op jit(solution)/shard_map/ppermute | solution.py:330

commit v2 on v1

v2 whole, which is shorter than its diff:
```python
import jax
import jax.numpy as jnp
from jax import lax
from jax.experimental import pallas as pl
from jax.experimental.pallas import tpu as pltpu
from jax.sharding import PartitionSpec as P

F32 = jnp.float32
BF16 = jnp.bfloat16
W = 128
K1, K2 = 27 * 64, 27 * 128
K1P = 1792
K1H = 896
HALF = 2688
KB = 896
VMEM = pl.BlockSpec(memory_space=pltpu.VMEM)
NT = (((1,), (1,)), ((), ()))


def run(kernel, outs, args, scratch=(), flops=10**8):
    return pl.pallas_call(
        kernel,
        out_shape=outs,
        in_specs=[VMEM] * len(args),
        out_specs=[VMEM] * len(outs),
        scratch_shapes=list(scratch),
        cost_estimate=pl.CostEstimate(flops=flops, bytes_accessed=10**5, transcendentals=0),
        compiler_params=pltpu.CompilerParams(vmem_limit_bytes=20 * 1024 * 1024),
    )(*args)


def sds(shape, dtype):
    return jax.ShapeDtypeStruct(shape, dtype)


def split():
    f = lax.axis_index("filt")
    return lax.rem(f, 4), lax.div(f, 4)


def xor(a, k):
    return lax.bitwise_xor(a, jnp.int32(k))


def rows8(i):
    return pl.ds(pl.multiple_of(i * 8, 8), 8)


def rows32(i):
    return pl.ds(pl.multiple_of(i * 32, 32), 32)


def lanes(core):
    return pl.ds(pl.multiple_of(core * HALF, W), HALF)


def shifted(x):
    lane = lax.broadcasted_iota(jnp.int32, x.shape, 1)
    left = jnp.where(lane == 0, 0.0, pltpu.roll(x, 1, 1))
    right = jnp.where(lane == W - 1, 0.0, pltpu.roll(x, W - 1, 1))
    return left, x, right


def logistic(v):
    return 0.5 * jnp.tanh(0.5 * v) + 0.5


def pack_first_kernel(w1_ref, out, acc):
    core = lax.rem(lax.axis_index("space"), 2)
    w1 = [w1_ref[t].astype(F32) for t in range(27)]
    acc[...] = jnp.concatenate(w1 + [jnp.zeros((8, K1P - K1), F32)], axis=1)
    out[...] = acc[:, pl.ds(pl.multiple_of(core * K1H, W), K1H)].astype(BF16)


def pack_second_kernel(w2_ref, g_ref, b0, b1, b2, b3, rows_ref):
    x, _ = split()
    w2 = [w2_ref[t].astype(F32) for t in range(27)]
    for d in range(2):
        t = jnp.swapaxes(g_ref[:, d].astype(F32), 0, 1)
        rows_ref[d, 0] = jnp.zeros((8, W), F32)
        rows_ref[d, 17] = jnp.zeros((8, W), F32)
        rows_ref[d, 1:17] = t
    for k, out in enumerate((b0, b1, b2, b3)):
        h0 = xor(x, k) * 4
        parts = [rows_ref[d, h0 + h] for d in range(2) for h in range(6)]
        out[...] = jnp.concatenate(w2 + parts, axis=1).astype(BF16)


def stack_kernel(b0, b1, b2, b3, w1_ref, acc):
    _, zl = split()
    for k, b in enumerate((b0, b1, b2, b3)):
        acc[rows8(xor(zl, k)), :] = b[...].astype(F32)
    w1_ref[...] = acc[...].astype(BF16)


def order_kernel(c0, c1, c2, c3, w1_ref, acc):
    x, _ = split()
    for k, c in enumerate((c0, c1, c2, c3)):
        v = c[...].astype(F32)
        for z in range(4):
            acc[rows8(z * 4 + xor(x, k)), :] = v[z * 8 : z * 8 + 8]
    w1_ref[...] = acc[...].astype(BF16)


def widen_kernel(xo_ref, xp_ref, xn_ref, xi_ref):
    p = lax.axis_index("space")
    for base, ref, inside in ((0, xp_ref, p > 0), (20, xo_ref, None), (40, xn_ref, p < 7)):
        for r in range(20):
            v = ref[r].astype(F32)
            a, b, c = shifted(v if inside is None else jnp.where(inside, v, 0.0))
            xi_ref[base + r, 0:64] = a.astype(BF16)
            xi_ref[base + r, 64:128] = b.astype(BF16)
            xi_ref[base + r, 128:192] = c.astype(BF16)


def conv_first_kernel(own_ref, got_ref, xi_ref, slope_ref, xa_ref, zs):
    x, zl = split()
    p = lax.axis_index("space")
    own, got = own_ref[...], got_ref[...]
    first = lax.rem(p, 2) == 0
    w1 = jnp.concatenate([jnp.where(first, own, got), jnp.where(first, got, own)], axis=1)[:, :K1]

    for i in range(16):
        dd, hh = i // 4, i % 4 * 2
        cols = []
        for j in range(2):
            cols.append(
                jnp.concatenate(
                    [xi_ref[(dd + a) * 10 + hh + j + b] for a in range(3) for b in range(3)], axis=0
                )
            )
        z = jnp.dot(w1, jnp.concatenate(cols, axis=1), preferred_element_type=F32)
        depth = p * 2 - 1 + dd
        for j in range(2):
            height = x * 4 - 2 + hh + j
            inside = (depth >= 0) & (depth < 16) & (height >= 0) & (height < 16)
            zr = z[:, j * W : (j + 1) * W]
            r = dd * 8 + hh + j
            zs[r] = zr
            act = jnp.where(inside, zr * logistic(zr), 0.0).astype(BF16).astype(F32)
            left, mid, right = shifted(act)
            xa_ref[r, 0:128] = left.astype(BF16)
            xa_ref[r, 128:256] = mid.astype(BF16)
            xa_ref[r, 256:384] = right.astype(BF16)

    for d in range(2):
        for h in range(4):
            v = zs[(d + 1) * 8 + h + 2, rows32(zl), :]
            q = logistic(v)
            slope_ref[:, (d * 4 + h) * W : (d * 4 + h + 1) * W] = q * (1.0 + v * (1.0 - q))


def conv_second_kernel(b0, b1, b2, b3, xa_ref, y_ref, gs0_ref, gs1_ref, w2b_ref, acc, w2_ref):
    x, _ = split()
    for k, b in enumerate((b0, b1, b2, b3)):
        acc[rows8(xor(x, k)), :] = b[...].astype(F32)
    w2_ref[...] = acc[:, :K2].astype(BF16)
    for j in range(7):
        taps = [acc[:, t * W : (t + 1) * W] if t < 27 else jnp.zeros((32, W), F32) for t in range(4 * j, 4 * j + 4)]
        w2b_ref[:, j * W : (j + 1) * W] = jnp.concatenate(taps, axis=0).T.astype(BF16)
    planes = [[], []]
    for dd in range(4):
        taps = [a for a in range(3) if 0 <= dd - a <= 1]
        w = jnp.concatenate(
            [w2_ref[:, t * 384 : (t + 1) * 384] for a in taps for t in range(3 * a, 3 * a + 3)], axis=0
        )
        col = jnp.concatenate([xa_ref[dd * 8 + h] for h in range(8)], axis=1)
        part = jnp.dot(w, col, preferred_element_type=F32)
        for k, a in enumerate(taps):
            for b in range(3):
                at = (k * 3 + b) * 32
                planes[dd - a].append(part[at : at + 32, b * W : (b + 6) * W])
    for d in range(2):
        t = planes[d]
        z = ((t[0] + t[1]) + (t[2] + t[3])) + ((t[4] + t[5]) + (t[6] + t[7])) + t[8]
        for hh in range(6):
            v = z[:, hh * W : (hh + 1) * W]
            q = logistic(v)
            if 1 <= hh <= 4:
                at = (d * 4 + hh - 1) * W
                y_ref[:, at : at + W] = (v * q).astype(BF16)
            g = acc[:, K2 + (d * 6 + hh) * W : K2 + (d * 6 + hh + 1) * W]
            gs = (g * (q * (1.0 + v * (1.0 - q)))).astype(BF16)
            (gs0_ref if d == 0 else gs1_ref)[hh] = gs


def second_kernel(xa_ref, gs0_ref, gs1_ref, dw_ref):
    gs = jnp.concatenate([(gs0_ref, gs1_ref)[d][h + 1] for d in range(2) for h in range(4)], axis=1)
    for a in range(3):
        for b in range(3):
            col = jnp.concatenate(
                [xa_ref[(d + a) * 8 + h + 1 + b] for d in range(2) for h in range(4)], axis=1
            )
            at = (a * 3 + b) * 384
            dw_ref[:, at : at + 384] = lax.dot_general(gs, col, NT, preferred_element_type=F32)


def back_kernel(gs0_ref, gs1_ref, gp_ref, gn_ref, w2b_ref, own_ref, s1, s2, s3, g3, acc):
    _, zl = split()
    p = lax.axis_index("space")
    sides = ((gp_ref, p > 0), (gs0_ref, None), (gs1_ref, None), (gn_ref, p < 7))
    for d, (ref, inside) in enumerate(sides):
        for h in range(6):
            v = ref[h].astype(F32)
            before, mid, after = shifted(v if inside is None else jnp.where(inside, v, 0.0))
            g3[d * 6 + h, 0:32] = after.astype(BF16)
            g3[d * 6 + h, 32:64] = mid.astype(BF16)
            g3[d * 6 + h, 64:96] = before.astype(BF16)
    w = w2b_ref[...]
    for d in range(2):
        for hp in range(2):
            cols = []
            for j in range(2):
                h = hp * 2 + j
                cols.append(
                    jnp.concatenate(
                        [g3[(d + 2 - a) * 6 + h + 2 - b] for a in range(3) for b in range(3)]
                        + [jnp.zeros((32, W), BF16)],
                        axis=0,
                    )
                )
            at = (d * 4 + hp * 2) * W
            acc[:, at : at + 2 * W] = jnp.dot(w, jnp.concatenate(cols, axis=1), preferred_element_type=F32)
    own_ref[...] = acc[rows32(zl), :]
    for k, out in enumerate((s1, s2, s3)):
        out[...] = acc[rows32(xor(zl, k + 1)), :].astype(BF16)


def first_kernel(own_ref, r1, r2, r3, slope_ref, xi_ref, dw2_ref, keep_ref, give_ref, acc):
    core = lax.rem(lax.axis_index("space"), 2)
    back = (own_ref[...] + r1[...].astype(F32)) + (r2[...].astype(F32) + r3[...].astype(F32))
    gf = (back * slope_ref[...]).astype(BF16)
    parts = []
    for a in range(3):
        col = jnp.concatenate(
            [
                jnp.concatenate(
                    [xi_ref[(d + 1 + a) * 10 + h + 2 + b] for d in range(2) for h in range(4)], axis=1
                )
                for b in range(3)
            ],
            axis=0,
        )
        parts.append(lax.dot_general(gf, col, NT, preferred_element_type=F32))
    acc[:, :K2] = dw2_ref[...]
    acc[:, K2:] = jnp.concatenate(parts + [jnp.zeros((32, 2 * HALF - K2 - K1), F32)], axis=1)
    keep_ref[...] = acc[:, lanes(core)]
    give_ref[...] = acc[:, lanes(1 - core)]


def chip_kernel(keep_ref, got_ref, y_ref, o0, y0, s1, s2, s3, acc, yacc):
    x, _ = split()
    acc[...] = keep_ref[...] + got_ref[...]
    yacc[...] = y_ref[...].astype(F32)
    o0[...] = acc[rows8(x), :]
    y0[...] = yacc[rows8(x), :]
    for k, out in enumerate((s1, s2, s3)):
        at = rows8(xor(x, k + 1))
        out[...] = jnp.concatenate([acc[at, :], yacc[at, :]], axis=1).astype(BF16)


def sum_kernel(o0, y0, r1, r2, r3, dw_ref, y_ref):
    x, _ = split()
    parts = [r[...].astype(F32) for r in (r1, r2, r3)]
    dw_ref[...] = ((o0[...] + parts[0][:, :HALF]) + (parts[1][:, :HALF] + parts[2][:, :HALF])).astype(BF16)
    for k, v in enumerate([y0[...]] + [r[:, HALF:] for r in parts]):
        h0 = xor(x, k) * 4
        for d in range(2):
            for h in range(4):
                at = (d * 4 + h) * W
                y_ref[d, h0 + h] = v[:, at : at + W]


def last_kernel(own_ref, got_ref, dw1_ref, dw2_ref):
    core = lax.rem(lax.axis_index("space"), 2)
    own, got = own_ref[...], got_ref[...]
    both = [jnp.where(core == 0, own, got), jnp.where(core == 0, got, own)]
    both = jnp.concatenate(both, axis=1) * (1.0 / 256.0)
    for t in range(27):
        dw2_ref[t] = both[:, t * W : (t + 1) * W]
        dw1_ref[t] = both[:, K2 + t * 64 : K2 + (t + 1) * 64]


def local(act_in, w_first, w_second, grad_out):
    X = [[(z * 4 + x, z * 4 + (x ^ k)) for z in range(4) for x in range(4)] for k in range(4)]
    Z = [[(z * 4 + x, (z ^ k) * 4 + x) for z in range(4) for x in range(4)] for k in range(4)]
    up = [(i, (i + 1) % 8) for i in range(8)]
    down = [((i + 1) % 8, i) for i in range(8)]
    other = [(i, i ^ 1) for i in range(8)]
    x = lax.rem(lax.axis_index("filt"), 4)

    (w0,) = run(
        pack_first_kernel,
        [sds((8, K1H), BF16)],
        [jnp.transpose(w_first, (0, 2, 1))],
        [pltpu.VMEM((8, K1P), F32)],
    )
    c = [w0] + [lax.ppermute(w0, "filt", Z[k]) for k in (1, 2, 3)]
    act_in, w0 = lax.optimization_barrier((act_in, w0))
    w_second, grad_out, w0 = lax.optimization_barrier((w_second, grad_out, w0))
    rows = jnp.pad(jnp.transpose(act_in[0], (1, 2, 0, 3)), ((0, 0), (3, 3), (0, 0), (0, 0)))
    xo = lax.dynamic_slice_in_dim(rows, x * 4, 10, axis=1).reshape(20, 64, W)
    xp = lax.ppermute(xo, "space", up)
    xn = lax.ppermute(xo, "space", down)

    (w1,) = run(stack_kernel, [sds((32, K1H), BF16)], c, [pltpu.VMEM((32, K1H), F32)])
    c = [w1] + [lax.ppermute(w1, "filt", X[k]) for k in (1, 2, 3)]
    b = run(
        pack_second_kernel,
        [sds((8, K2 + 12 * W), BF16)] * 4,
        [jnp.transpose(w_second, (0, 2, 1)), grad_out[0]],
        [pltpu.VMEM((2, 18, 8, W), F32)],
    )
    b, c = lax.optimization_barrier((b, c))
    (w1,) = run(order_kernel, [sds((128, K1H), BF16)], c, [pltpu.VMEM((128, K1H), F32)])
    w1got = lax.ppermute(w1, "space", other)

    b, w1 = lax.optimization_barrier((b, w1))
    b = [b[0]] + [lax.ppermute(b[k], "filt", X[k]) for k in (1, 2, 3)]
    (xi,) = run(widen_kernel, [sds((60, 192, W), BF16)], [xo, xp, xn], flops=8 * 10**8)
    slope, xa = run(
        conv_first_kernel,
        [sds((32, 1024), F32), sds((32, 384, W), BF16)],
        [w1, w1got, xi],
        [pltpu.VMEM((32, 128, W), F32)],
        4 * 10**9,
    )
    y, gs0, gs1, w2b = run(
        conv_second_kernel,
        [sds((32, 1024), BF16), sds((6, 32, W), BF16), sds((6, 32, W), BF16), sds((128, KB), BF16)],
        b + [xa],
        [pltpu.VMEM((32, K2 + 12 * W), F32), pltpu.VMEM((32, K2), BF16)],
    )
    gp = lax.ppermute(gs1, "space", up)
    gn = lax.ppermute(gs0, "space", down)
    (dw2,) = run(second_kernel, [sds((32, K2), F32)], [xa, gs0, gs1], flops=25 * 10**8)

    own, *s = run(
        back_kernel,
        [sds((32, 1024), F32)] + [sds((32, 1024), BF16)] * 3,
        [gs0, gs1, gp, gn, w2b],
        [pltpu.VMEM((24, 96, W), BF16), pltpu.VMEM((128, 1024), F32)],
    )
    s = [lax.ppermute(s[k - 1], "filt", Z[k]) for k in (1, 2, 3)]

    keep, give = run(
        first_kernel,
        [sds((32, HALF), F32)] * 2,
        [own] + s + [slope, xi, dw2],
        [pltpu.VMEM((32, 2 * HALF), F32)],
    )
    got = lax.ppermute(give, "space", other)
    o, yo, *s = run(
        chip_kernel,
        [sds((8, HALF), F32), sds((8, 1024), F32)] + [sds((8, HALF + 1024), BF16)] * 3,
        [keep, got, y],
        [pltpu.VMEM((32, HALF), F32), pltpu.VMEM((32, 1024), F32)],
    )
    s = [lax.ppermute(s[k - 1], "filt", X[k]) for k in (1, 2, 3)]
    part, yt = run(sum_kernel, [sds((8, HALF), BF16), sds((2, 16, 8, W), F32)], [o, yo] + s)
    y_out = jnp.transpose(yt, (2, 0, 1, 3)).astype(BF16)[None]

    q = [part] + [lax.ppermute(part, "space", [(i, i ^ (2 * k)) for i in range(8)]) for k in (1, 2, 3)]
    q = [v.astype(F32) for v in q]
    part = ((q[0] + q[1]) + (q[2] + q[3])).astype(BF16)
    part = part.astype(F32) + lax.ppermute(part, "sample", [(0, 1), (1, 0)]).astype(F32)
    got = lax.ppermute(part, "space", other)
    dw1, dw2 = run(last_kernel, [sds((27, 8, 64), F32), sds((27, 8, 128), F32)], [part, got])
    return y_out, jnp.transpose(dw1, (0, 2, 1)), jnp.transpose(dw2, (0, 2, 1))


def solution(mesh):
    placed = (
        P("sample", None, "space", None, None),
        P(None, None, "filt"),
        P(None, None, "filt"),
        P("sample", "filt", "space", None, None),
    )
    return jax.shard_map(
        local,
        mesh=mesh,
        in_specs=placed,
        out_specs=(
            P("sample", "filt", "space", None, None),
            P(None, None, "filt"),
            P(None, None, "filt"),
        ),
        check_vma=False,
    )
```

time: 104 us -> 78.4 us (0.75); the launches traced: 102 us -> 78.1 us
  waiting for transfers between devices: 34 us -> 18.9 us
  Pallas kernels: 19.9 us -> 8.67 us
  starting transfers between devices: 39.4 us -> 45.2 us
  local copies, waits for them, and re-layouts: 8.3 us -> 4.49 us
    ppermute x6 -> x10, starting transfers between devices: 11.4 us -> 25.4 us  [the longest x1 5.07 us: local(): got = lax.ppermute(part, 'space', other)]
    pallas_call x8 -> x13, Pallas kernels: 19.9 us -> 8.67 us  [run(): pl.pallas_call(kernel, out_shape=outs, in_specs=[VMEM] * len(args), out_s...]
    ppermute x6 -> x10, waiting for transfers between devices: 16.5 us -> 9.24 us  [the longest x3 3.48 us: local(): c = [w0] + [lax.ppermute(w0, 'filt', Z[k]) for k in (1, 2, 3)]]
    ppermute x3, waiting for transfers between devices: 7.27 us -> 1.59 us  [local(): b = [b[0]] + [lax.ppermute(b[k], 'filt', X[k]) for k in (1, 2, 3)]]
    unnamed x9 -> x7, local copies, waits for them, and re-layouts: 6.91 us -> 3.1 us
    ppermute x1, starting transfers between devices: 2.96 us -> 0.8 us  [local(): gn = lax.ppermute(gs0, 'space', down)]
    ppermute x1, starting transfers between devices: 3.09 us -> 0.96 us  [local(): gp = lax.ppermute(gs1, 'space', up)]
    ppermute x3, waiting for transfers between devices: 5.28 us -> 3.21 us  [local(): s = [lax.ppermute(s[k - 1], 'filt', X[k]) for k in (1, 2, 3)]]
  transfers between devices with their start and end apart: 22 -> 26, of which waited for: 14 -> 14; matrix products, arithmetic and copies ran while one was open for 3% -> 1% of each run, Pallas kernels for 3% -> 7%
where the time goes in v2:
time: 78.4 us; the launch traced here: 78.1 us
  starting transfers between devices  45.2 us (58%)
  waiting for transfers between devices  18.9 us (24%)
  Pallas kernels  8.67 us (11%)
  local copies, waits for them, and re-layouts  4.49 us (6%)
  between operations  0.82 us (1%)
    pallas_call x13, Pallas kernels, run(): pl.pallas_call(kernel, out_shape=outs, in_specs=[VMEM] * len(args), out_s...  8.67 us
    ppermute x1, starting transfers between devices, local(): got = lax.ppermute(part, 'space', other)  5.07 us
    ppermute x1, starting transfers between devices, local(): lax.ppermute(part, 'sample', [(0, 1), (1, 0)]).astype(F32)  4.7 us
    ppermute x1, starting transfers between devices, local(): got = lax.ppermute(give, 'space', other)  4.32 us
    ppermute x3, starting transfers between devices, local(): c = [w0] + [lax.ppermute(w0, 'filt', Z[k]) for k in (1, 2, 3)]  4.1 us
    ppermute x3, starting transfers between devices, local(): s = [lax.ppermute(s[k - 1], 'filt', X[k]) for k in (1, 2, 3)]  3.94 us
    ppermute x3, starting transfers between devices, local(): b = [b[0]] + [lax.ppermute(b[k], 'filt', X[k]) for k in (1, 2, 3)]  3.88 us
    ppermute x1, starting transfers between devices, local(): w1got = lax.ppermute(w1, 'space', other)  3.86 us
  transfers between devices with their start and end apart: 26, of which 14 were waited for; matrix products, arithmetic and copies ran while one was open for 1% of the time, Pallas kernels for 7%

profile of v2, /device:TPU:1, one launch (start us, length us, event | category | flops | bytes accessed | tf_op | source)
XLA Modules:
  0.0 78.1 jit_solution(11834404882904658504)
XLA Ops:
  1.5 1.3 %pad_dynamic-slice_fusion = bf16[2,10,64,128]{3,1,0,2:T(8,128)(2,1)S(1)} fusion(s32[]{:T(128)S(6)} %select_n.3, bf16[2,16,64,128]{3,1,0,2:T(8,128)(2,1)} %bitcast.19), kind=kLoop, calls=%fused_computation | loop fusion | bytes 851972 | tf_op jit(solution)/shard_map/dynamic_slice | solution.py:302
  2.9 3.3 %collective-permute-start.11 = (bf16[20,64,128]{2,1,0:T(8,128)(2,1)S(1)}, bf16[20,64,128]{2,1,0:T(8,128)(2,1)S(1)}, u32[]{:S(2)}, u32[]{:S(2)}) collective-permute-start(bf16[20,64,128]{2,1,0:T(8,128)(2,1)S(1)} %bitcast.13), channel_id=1, source_target_pairs={{16,0},{32,16},{48,32},{64,48},{80,64},{96,80},{112,96},{0,112},{1... | collective-permute-start | bytes 983048 | tf_op jit(solution)/shard_map/ppermute | solution.py:304
  6.2 3.8 %collective-permute-start.2 = (bf16[8,896]{1,0:T(8,128)(2,1)S(1)}, bf16[8,896]{1,0:T(8,128)(2,1)S(1)}, u32[]{:S(2)}, u32[]{:S(2)}) collective-permute-start(bf16[8,896]{1,0:T(8,128)(2,1)S(1)} %shard_map.68.b0), channel_id=1, source_target_pairs={{0,12},{1,13},{2,14},{3,15},{4,8},{5,9},{6,10},{7,11},{8,4},{9,5},... | collective-permute-start | bytes 43016 | tf_op jit(solution)/shard_map/ppermute | solution.py:298
  11.1 2.7 %collective-permute-done.1.b2 = bf16[8,896]{1,0:T(8,128)(2,1)S(1)} collective-permute-done((bf16[8,896]{1,0:T(8,128)(2,1)S(1)}, bf16[8,896]{1,0:T(8,128)(2,1)S(1)}, u32[]{:S(2)}, u32[]{:S(2)}) %collective-permute-start.1) | collective-permute-done | bytes 14368 | tf_op jit(solution)/shard_map/ppermute | solution.py:298
  13.8 2.5 %collective-permute-start.5 = (bf16[32,896]{1,0:T(8,128)(2,1)S(1)}, bf16[32,896]{1,0:T(8,128)(2,1)S(1)}, u32[]{:S(2)}, u32[]{:S(2)}) collective-permute-start(bf16[32,896]{1,0:T(8,128)(2,1)S(1)} %shard_map.69.c0), channel_id=1, source_target_pairs={{0,3},{1,2},{2,1},{3,0},{4,7},{5,6},{6,5},{7,4},{8,11},{9,10},{10,... | collective-permute-start | bytes 172040 | tf_op jit(solution)/shard_map/ppermute | solution.py:307
  18.9 2.0 %collective-permute-done.4.c2 = bf16[32,896]{1,0:T(8,128)(2,1)S(1)} collective-permute-done((bf16[32,896]{1,0:T(8,128)(2,1)S(1)}, bf16[32,896]{1,0:T(8,128)(2,1)S(1)}, u32[]{:S(2)}, u32[]{:S(2)}) %collective-permute-start.4) | collective-permute-done | bytes 57376 | tf_op jit(solution)/shard_map/ppermute | solution.py:307
  20.9 3.9 %collective-permute-start.9 = (bf16[128,896]{1,0:T(8,128)(2,1)S(1)}, bf16[128,896]{1,0:T(8,128)(2,1)S(1)}, u32[]{:S(2)}, u32[]{:S(2)}) collective-permute-start(bf16[128,896]{1,0:T(8,128)(2,1)S(1)} %shard_map.70.own_ref), channel_id=1, source_target_pairs={{0,16},{16,0},{32,48},{48,32},{64,80},{80,64},{96,112},{112,96},{1... | collective-permute-start | bytes 688136 | tf_op jit(solution)/shard_map/ppermute | solution.py:316
  24.9 2.3 %collective-permute-start.7 = (bf16[8,4992]{1,0:T(8,128)(2,1)S(1)}, bf16[8,4992]{1,0:T(8,128)(2,1)S(1)}, u32[]{:S(2)}, u32[]{:S(2)}) collective-permute-start(bf16[8,4992]{1,0:T(8,128)(2,1)S(1)} %get-tuple-element.60), channel_id=1, source_target_pairs={{0,2},{1,3},{2,0},{3,1},{4,6},{5,7},{6,4},{7,5},{8,10},{9,11},{10,... | collective-permute-start | bytes 239624 | tf_op jit(solution)/shard_map/ppermute | solution.py:319
  27.2 1.5 %collective-permute-start.8 = (bf16[8,4992]{1,0:T(8,128)(2,1)S(1)}, bf16[8,4992]{1,0:T(8,128)(2,1)S(1)}, u32[]{:S(2)}, u32[]{:S(2)}) collective-permute-start(bf16[8,4992]{1,0:T(8,128)(2,1)S(1)} %get-tuple-element.61), channel_id=1, source_target_pairs={{0,3},{1,2},{2,1},{3,0},{4,7},{5,6},{6,5},{7,4},{8,11},{9,10},{10,... | collective-permute-start | bytes 239624 | tf_op jit(solution)/shard_map/ppermute | solution.py:319
  29.3 2.3 %shard_map.72 = (f32[32,1024]{1,0:T(8,128)S(1)}, bf16[32,384,128]{2,1,0:T(8,128)(2,1)S(1)}) custom-call(bf16[128,896]{1,0:T(8,128)(2,1)S(1)} %shard_map.70.own_ref, bf16[128,896]{1,0:T(8,128)(2,1)S(1)} %collective-permute-done.9.got_ref, bf16[60,192,128]{2,1,0:T(8,128)(2,1)S(1)} %shard_map.71.xi_ref), custom_call_target="tpu_custom_call" | custom-call | flops 4000000000 | bytes 100000 | tf_op jit(solution)/shard_map/pallas_call | solution.py:21
  31.6 1.6 %collective-permute-done.8.b3 = bf16[8,4992]{1,0:T(8,128)(2,1)S(1)} collective-permute-done((bf16[8,4992]{1,0:T(8,128)(2,1)S(1)}, bf16[8,4992]{1,0:T(8,128)(2,1)S(1)}, u32[]{:S(2)}, u32[]{:S(2)}) %collective-permute-start.8) | collective-permute-done | bytes 79904 | tf_op jit(solution)/shard_map/ppermute | solution.py:319
  35.8 1.8 %collective-permute-done.13.gn_ref = bf16[6,32,128]{2,1,0:T(8,128)(2,1)S(1)} collective-permute-done((bf16[6,32,128]{2,1,0:T(8,128)(2,1)S(1)}, bf16[6,32,128]{2,1,0:T(8,128)(2,1)S(1)}, u32[]{:S(2)}, u32[]{:S(2)}) %collective-permute-start.13) | collective-permute-done | bytes 49184 | tf_op jit(solution)/shard_map/ppermute | solution.py:335
  38.3 1.8 %collective-permute-start.15 = (bf16[32,1024]{1,0:T(8,128)(2,1)S(1)}, bf16[32,1024]{1,0:T(8,128)(2,1)S(1)}, u32[]{:S(2)}, u32[]{:S(2)}) collective-permute-start(bf16[32,1024]{1,0:T(8,128)(2,1)S(1)} %get-tuple-element.70), channel_id=1, source_target_pairs={{0,8},{1,9},{2,10},{3,11},{4,12},{5,13},{6,14},{7,15},{8,0},{9,1},... | collective-permute-start | bytes 196616 | tf_op jit(solution)/shard_map/ppermute | solution.py:344
  40.1 1.7 %collective-permute-start.16 = (bf16[32,1024]{1,0:T(8,128)(2,1)S(1)}, bf16[32,1024]{1,0:T(8,128)(2,1)S(1)}, u32[]{:S(2)}, u32[]{:S(2)}) collective-permute-start(bf16[32,1024]{1,0:T(8,128)(2,1)S(1)} %get-tuple-element.71), channel_id=1, source_target_pairs={{0,12},{1,13},{2,14},{3,15},{4,8},{5,9},{6,10},{7,11},{8,4},{9,5},... | collective-permute-start | bytes 196616 | tf_op jit(solution)/shard_map/ppermute | solution.py:344
  41.8 2.1 %shard_map.75.dw2_ref = f32[32,3456]{1,0:T(8,128)S(1)} custom-call(bf16[32,384,128]{2,1,0:T(8,128)(2,1)S(1)} %get-tuple-element.64.xa_ref, bf16[6,32,128]{2,1,0:T(8,128)(2,1)S(1)} %get-tuple-element.65.gs0_ref, bf16[6,32,128]{2,1,0:T(8,128)(2,1)S(1)} %get-tuple-element.66.gs1_ref), custom_call_target="tpu_custom_call" | custom-call | flops 2500000000 | bytes 100000 | tf_op jit(solution)/shard_map/pallas_call | solution.py:21
  46.3 4.3 %collective-permute-start.17 = (f32[32,2688]{1,0:T(8,128)S(1)}, f32[32,2688]{1,0:T(8,128)S(1)}, u32[]{:S(2)}, u32[]{:S(2)}) collective-permute-start(f32[32,2688]{1,0:T(8,128)S(1)} %get-tuple-element.74), channel_id=1, source_target_pairs={{0,16},{16,0},{32,48},{48,32},{64,80},{80,64},{96,112},{112,96},{1... | collective-permute-start | bytes 1032200 | tf_op jit(solution)/shard_map/ppermute | solution.py:352
  50.6 1.3 %collective-permute-done.17.got_ref = f32[32,2688]{1,0:T(8,128)S(1)} collective-permute-done((f32[32,2688]{1,0:T(8,128)S(1)}, f32[32,2688]{1,0:T(8,128)S(1)}, u32[]{:S(2)}, u32[]{:S(2)}) %collective-permute-start.17) | collective-permute-done | bytes 344096 | tf_op jit(solution)/shard_map/ppermute | solution.py:352
  52.1 2.8 %collective-permute-start.19 = (bf16[8,3712]{1,0:T(8,128)(2,1)S(1)}, bf16[8,3712]{1,0:T(8,128)(2,1)S(1)}, u32[]{:S(2)}, u32[]{:S(2)}) collective-permute-start(bf16[8,3712]{1,0:T(8,128)(2,1)S(1)} %get-tuple-element.79), channel_id=1, source_target_pairs={{0,2},{1,3},{2,0},{3,1},{4,6},{5,7},{6,4},{7,5},{8,10},{9,11},{10,... | collective-permute-start | bytes 178184 | tf_op jit(solution)/shard_map/ppermute | solution.py:359
  55.9 1.6 %collective-permute-done.19.r2 = bf16[8,3712]{1,0:T(8,128)(2,1)S(1)} collective-permute-done((bf16[8,3712]{1,0:T(8,128)(2,1)S(1)}, bf16[8,3712]{1,0:T(8,128)(2,1)S(1)}, u32[]{:S(2)}, u32[]{:S(2)}) %collective-permute-start.19) | collective-permute-done | bytes 59424 | tf_op jit(solution)/shard_map/ppermute | solution.py:359
  57.6 1.6 %collective-permute-done.20.r3 = bf16[8,3712]{1,0:T(8,128)(2,1)S(1)} collective-permute-done((bf16[8,3712]{1,0:T(8,128)(2,1)S(1)}, bf16[8,3712]{1,0:T(8,128)(2,1)S(1)}, u32[]{:S(2)}, u32[]{:S(2)}) %collective-permute-start.20) | collective-permute-done | bytes 59424 | tf_op jit(solution)/shard_map/ppermute | solution.py:359
  60.0 2.6 %collective-permute-start.21 = (bf16[8,2688]{1,0:T(8,128)(2,1)S(1)}, bf16[8,2688]{1,0:T(8,128)(2,1)S(1)}, u32[]{:S(2)}, u32[]{:S(2)}) collective-permute-start(bf16[8,2688]{1,0:T(8,128)(2,1)S(1)} %get-tuple-element.82), channel_id=1, source_target_pairs={{0,32},{16,48},{32,0},{48,16},{64,96},{80,112},{96,64},{112,80},{1... | collective-permute-start | bytes 129032 | tf_op jit(solution)/shard_map/ppermute | solution.py:363
  64.4 4.7 %collective-permute-start.24 = (bf16[8,2688]{1,0:T(8,128)(2,1)S(1)}, bf16[8,2688]{1,0:T(8,128)(2,1)S(1)}, u32[]{:S(2)}, u32[]{:S(2)}) collective-permute-start(bf16[8,2688]{1,0:T(8,128)(2,1)S(1)} %add_convert_fusion), channel_id=1, source_target_pairs={{0,128},{128,0},{1,129},{129,1},{2,130},{130,2},{3,131},{131,3},{4... | collective-permute-start | bytes 129032 | tf_op jit(solution)/shard_map/ppermute | solution.py:366
  69.1 2.2 %collective-permute-done.24 = bf16[8,2688]{1,0:T(8,128)(2,1)S(1)} collective-permute-done((bf16[8,2688]{1,0:T(8,128)(2,1)S(1)}, bf16[8,2688]{1,0:T(8,128)(2,1)S(1)}, u32[]{:S(2)}, u32[]{:S(2)}) %collective-permute-start.24) | collective-permute-done | bytes 43040 | tf_op jit(solution)/shard_map/ppermute | solution.py:366
  71.3 5.1 %collective-permute-start.25 = (f32[8,2688]{1,0:T(8,128)S(1)}, f32[8,2688]{1,0:T(8,128)S(1)}, u32[]{:S(2)}, u32[]{:S(2)}) collective-permute-start(f32[8,2688]{1,0:T(8,128)S(1)} %convert_add_fusion.own_ref), channel_id=1, source_target_pairs={{0,16},{16,0},{32,48},{48,32},{64,80},{80,64},{96,112},{112,96},{1... | collective-permute-start | bytes 258056 | tf_op jit(solution)/shard_map/ppermute | solution.py:367
  (53 shorter events, 16.6 us)
Async XLA Ops:
  2.9 24.3 %collective-permute-start.11 = (bf16[20,64,128]{2,1,0:T(8,128)(2,1)S(1)}, bf16[20,64,128]{2,1,0:T(8,128)(2,1)S(1)}, u32[]{:S(2)}, u32[]{:S(2)}) collective-permute-start(bf16[20,64,128]{2,1,0:T(8,128)(2,1)S(1)} %bitcast.13), channel_id=1, source_target_pairs={{16,0},{32,16},{48,32},{64,48},{80,64},{96,80},{112,96},{0,112},{1... | collective-permute-start | bytes 983048 | tf_op jit(solution)/shard_map/ppermute | solution.py:304
  6.2 22.5 %collective-permute-start.10 = (bf16[20,64,128]{2,1,0:T(8,128)(2,1)S(1)}, bf16[20,64,128]{2,1,0:T(8,128)(2,1)S(1)}, u32[]{:S(2)}, u32[]{:S(2)}) collective-permute-start(bf16[20,64,128]{2,1,0:T(8,128)(2,1)S(1)} %bitcast.14), channel_id=1, source_target_pairs={{0,16},{16,32},{32,48},{48,64},{64,80},{80,96},{96,112},{112,0},{1... | collective-permute-start | bytes 983048 | tf_op jit(solution)/shard_map/ppermute | solution.py:303
  6.2 4.9 %collective-permute-start.2 = (bf16[8,896]{1,0:T(8,128)(2,1)S(1)}, bf16[8,896]{1,0:T(8,128)(2,1)S(1)}, u32[]{:S(2)}, u32[]{:S(2)}) collective-permute-start(bf16[8,896]{1,0:T(8,128)(2,1)S(1)} %shard_map.68.b0), channel_id=1, source_target_pairs={{0,12},{1,13},{2,14},{3,15},{4,8},{5,9},{6,10},{7,11},{8,4},{9,5},... | collective-permute-start | bytes 43016 | tf_op jit(solution)/shard_map/ppermute | solution.py:298
  10.0 3.8 %collective-permute-start.1 = (bf16[8,896]{1,0:T(8,128)(2,1)S(1)}, bf16[8,896]{1,0:T(8,128)(2,1)S(1)}, u32[]{:S(2)}, u32[]{:S(2)}) collective-permute-start(bf16[8,896]{1,0:T(8,128)(2,1)S(1)} %shard_map.68.b0), channel_id=1, source_target_pairs={{0,8},{1,9},{2,10},{3,11},{4,12},{5,13},{6,14},{7,15},{8,0},{9,1},... | collective-permute-start | bytes 43016 | tf_op jit(solution)/shard_map/ppermute | solution.py:298
  10.0 3.8 %collective-permute-start = (bf16[8,896]{1,0:T(8,128)(2,1)S(1)}, bf16[8,896]{1,0:T(8,128)(2,1)S(1)}, u32[]{:S(2)}, u32[]{:S(2)}) collective-permute-start(bf16[8,896]{1,0:T(8,128)(2,1)S(1)} %shard_map.68.b0), channel_id=1, source_target_pairs={{0,4},{1,5},{2,6},{3,7},{4,0},{5,1},{6,2},{7,3},{8,12},{9,13},{10,... | collective-permute-start | bytes 43016 | tf_op jit(solution)/shard_map/ppermute | solution.py:298
  13.8 5.0 %collective-permute-start.5 = (bf16[32,896]{1,0:T(8,128)(2,1)S(1)}, bf16[32,896]{1,0:T(8,128)(2,1)S(1)}, u32[]{:S(2)}, u32[]{:S(2)}) collective-permute-start(bf16[32,896]{1,0:T(8,128)(2,1)S(1)} %shard_map.69.c0), channel_id=1, source_target_pairs={{0,3},{1,2},{2,1},{3,0},{4,7},{5,6},{6,5},{7,4},{8,11},{9,10},{10,... | collective-permute-start | bytes 172040 | tf_op jit(solution)/shard_map/ppermute | solution.py:307
  16.3 4.6 %collective-permute-start.4 = (bf16[32,896]{1,0:T(8,128)(2,1)S(1)}, bf16[32,896]{1,0:T(8,128)(2,1)S(1)}, u32[]{:S(2)}, u32[]{:S(2)}) collective-permute-start(bf16[32,896]{1,0:T(8,128)(2,1)S(1)} %shard_map.69.c0), channel_id=1, source_target_pairs={{0,2},{1,3},{2,0},{3,1},{4,6},{5,7},{6,4},{7,5},{8,10},{9,11},{10,... | collective-permute-start | bytes 172040 | tf_op jit(solution)/shard_map/ppermute | solution.py:307
  16.9 4.0 %collective-permute-start.3 = (bf16[32,896]{1,0:T(8,128)(2,1)S(1)}, bf16[32,896]{1,0:T(8,128)(2,1)S(1)}, u32[]{:S(2)}, u32[]{:S(2)}) collective-permute-start(bf16[32,896]{1,0:T(8,128)(2,1)S(1)} %shard_map.69.c0), channel_id=1, source_target_pairs={{0,1},{1,0},{2,3},{3,2},{4,5},{5,4},{6,7},{7,6},{8,9},{9,8},{10,11... | collective-permute-start | bytes 172040 | tf_op jit(solution)/shard_map/ppermute | solution.py:307
  20.9 8.3 %collective-permute-start.9 = (bf16[128,896]{1,0:T(8,128)(2,1)S(1)}, bf16[128,896]{1,0:T(8,128)(2,1)S(1)}, u32[]{:S(2)}, u32[]{:S(2)}) collective-permute-start(bf16[128,896]{1,0:T(8,128)(2,1)S(1)} %shard_map.70.own_ref), channel_id=1, source_target_pairs={{0,16},{16,0},{32,48},{48,32},{64,80},{80,64},{96,112},{112,96},{1... | collective-permute-start | bytes 688136 | tf_op jit(solution)/shard_map/ppermute | solution.py:316
  24.8 6.8 %collective-permute-start.6 = (bf16[8,4992]{1,0:T(8,128)(2,1)S(1)}, bf16[8,4992]{1,0:T(8,128)(2,1)S(1)}, u32[]{:S(2)}, u32[]{:S(2)}) collective-permute-start(bf16[8,4992]{1,0:T(8,128)(2,1)S(1)} %get-tuple-element.59), channel_id=1, source_target_pairs={{0,1},{1,0},{2,3},{3,2},{4,5},{5,4},{6,7},{7,6},{8,9},{9,8},{10,11... | collective-permute-start | bytes 239624 | tf_op jit(solution)/shard_map/ppermute | solution.py:319
  24.9 6.8 %collective-permute-start.7 = (bf16[8,4992]{1,0:T(8,128)(2,1)S(1)}, bf16[8,4992]{1,0:T(8,128)(2,1)S(1)}, u32[]{:S(2)}, u32[]{:S(2)}) collective-permute-start(bf16[8,4992]{1,0:T(8,128)(2,1)S(1)} %get-tuple-element.60), channel_id=1, source_target_pairs={{0,2},{1,3},{2,0},{3,1},{4,6},{5,7},{6,4},{7,5},{8,10},{9,11},{10,... | collective-permute-start | bytes 239624 | tf_op jit(solution)/shard_map/ppermute | solution.py:319
  27.2 6.0 %collective-permute-start.8 = (bf16[8,4992]{1,0:T(8,128)(2,1)S(1)}, bf16[8,4992]{1,0:T(8,128)(2,1)S(1)}, u32[]{:S(2)}, u32[]{:S(2)}) collective-permute-start(bf16[8,4992]{1,0:T(8,128)(2,1)S(1)} %get-tuple-element.61), channel_id=1, source_target_pairs={{0,3},{1,2},{2,1},{3,0},{4,7},{5,6},{6,5},{7,4},{8,11},{9,10},{10,... | collective-permute-start | bytes 239624 | tf_op jit(solution)/shard_map/ppermute | solution.py:319
  38.2 5.8 %collective-permute-start.14 = (bf16[32,1024]{1,0:T(8,128)(2,1)S(1)}, bf16[32,1024]{1,0:T(8,128)(2,1)S(1)}, u32[]{:S(2)}, u32[]{:S(2)}) collective-permute-start(bf16[32,1024]{1,0:T(8,128)(2,1)S(1)} %get-tuple-element.69), channel_id=1, source_target_pairs={{0,4},{1,5},{2,6},{3,7},{4,0},{5,1},{6,2},{7,3},{8,12},{9,13},{10,... | collective-permute-start | bytes 196616 | tf_op jit(solution)/shard_map/ppermute | solution.py:344
  38.3 5.7 %collective-permute-start.15 = (bf16[32,1024]{1,0:T(8,128)(2,1)S(1)}, bf16[32,1024]{1,0:T(8,128)(2,1)S(1)}, u32[]{:S(2)}, u32[]{:S(2)}) collective-permute-start(bf16[32,1024]{1,0:T(8,128)(2,1)S(1)} %get-tuple-element.70), channel_id=1, source_target_pairs={{0,8},{1,9},{2,10},{3,11},{4,12},{5,13},{6,14},{7,15},{8,0},{9,1},... | collective-permute-start | bytes 196616 | tf_op jit(solution)/shard_map/ppermute | solution.py:344
  40.1 5.0 %collective-permute-start.16 = (bf16[32,1024]{1,0:T(8,128)(2,1)S(1)}, bf16[32,1024]{1,0:T(8,128)(2,1)S(1)}, u32[]{:S(2)}, u32[]{:S(2)}) collective-permute-start(bf16[32,1024]{1,0:T(8,128)(2,1)S(1)} %get-tuple-element.71), channel_id=1, source_target_pairs={{0,12},{1,13},{2,14},{3,15},{4,8},{5,9},{6,10},{7,11},{8,4},{9,5},... | collective-permute-start | bytes 196616 | tf_op jit(solution)/shard_map/ppermute | solution.py:344
  46.3 5.6 %collective-permute-start.17 = (f32[32,2688]{1,0:T(8,128)S(1)}, f32[32,2688]{1,0:T(8,128)S(1)}, u32[]{:S(2)}, u32[]{:S(2)}) collective-permute-start(f32[32,2688]{1,0:T(8,128)S(1)} %get-tuple-element.74), channel_id=1, source_target_pairs={{0,16},{16,0},{32,48},{48,32},{64,80},{80,64},{96,112},{112,96},{1... | collective-permute-start | bytes 1032200 | tf_op jit(solution)/shard_map/ppermute | solution.py:352
  52.0 3.9 %collective-permute-start.18 = (bf16[8,3712]{1,0:T(8,128)(2,1)S(1)}, bf16[8,3712]{1,0:T(8,128)(2,1)S(1)}, u32[]{:S(2)}, u32[]{:S(2)}) collective-permute-start(bf16[8,3712]{1,0:T(8,128)(2,1)S(1)} %get-tuple-element.78), channel_id=1, source_target_pairs={{0,1},{1,0},{2,3},{3,2},{4,5},{5,4},{6,7},{7,6},{8,9},{9,8},{10,11... | collective-permute-start | bytes 178184 | tf_op jit(solution)/shard_map/ppermute | solution.py:359
  52.1 5.5 %collective-permute-start.19 = (bf16[8,3712]{1,0:T(8,128)(2,1)S(1)}, bf16[8,3712]{1,0:T(8,128)(2,1)S(1)}, u32[]{:S(2)}, u32[]{:S(2)}) collective-permute-start(bf16[8,3712]{1,0:T(8,128)(2,1)S(1)} %get-tuple-element.79), channel_id=1, source_target_pairs={{0,2},{1,3},{2,0},{3,1},{4,6},{5,7},{6,4},{7,5},{8,10},{9,11},{10,... | collective-permute-start | bytes 178184 | tf_op jit(solution)/shard_map/ppermute | solution.py:359
  54.9 4.3 %collective-permute-start.20 = (bf16[8,3712]{1,0:T(8,128)(2,1)S(1)}, bf16[8,3712]{1,0:T(8,128)(2,1)S(1)}, u32[]{:S(2)}, u32[]{:S(2)}) collective-permute-start(bf16[8,3712]{1,0:T(8,128)(2,1)S(1)} %get-tuple-element.80), channel_id=1, source_target_pairs={{0,3},{1,2},{2,1},{3,0},{4,7},{5,6},{6,5},{7,4},{8,11},{9,10},{10,... | collective-permute-start | bytes 178184 | tf_op jit(solution)/shard_map/ppermute | solution.py:359
  59.2 4.2 %collective-permute-start.23 = (bf16[8,2688]{1,0:T(8,128)(2,1)S(1)}, bf16[8,2688]{1,0:T(8,128)(2,1)S(1)}, u32[]{:S(2)}, u32[]{:S(2)}) collective-permute-start(bf16[8,2688]{1,0:T(8,128)(2,1)S(1)} %get-tuple-element.82), channel_id=1, source_target_pairs={{0,96},{16,112},{32,64},{48,80},{64,32},{80,48},{96,0},{112,16},{1... | collective-permute-start | bytes 129032 | tf_op jit(solution)/shard_map/ppermute | solution.py:363
  59.5 4.4 %collective-permute-start.22 = (bf16[8,2688]{1,0:T(8,128)(2,1)S(1)}, bf16[8,2688]{1,0:T(8,128)(2,1)S(1)}, u32[]{:S(2)}, u32[]{:S(2)}) collective-permute-start(bf16[8,2688]{1,0:T(8,128)(2,1)S(1)} %get-tuple-element.82), channel_id=1, source_target_pairs={{0,64},{16,80},{32,96},{48,112},{64,0},{80,16},{96,32},{112,48},{1... | collective-permute-start | bytes 129032 | tf_op jit(solution)/shard_map/ppermute | solution.py:363
  60.0 4.4 %collective-permute-start.21 = (bf16[8,2688]{1,0:T(8,128)(2,1)S(1)}, bf16[8,2688]{1,0:T(8,128)(2,1)S(1)}, u32[]{:S(2)}, u32[]{:S(2)}) collective-permute-start(bf16[8,2688]{1,0:T(8,128)(2,1)S(1)} %get-tuple-element.82), channel_id=1, source_target_pairs={{0,32},{16,48},{32,0},{48,16},{64,96},{80,112},{96,64},{112,80},{1... | collective-permute-start | bytes 129032 | tf_op jit(solution)/shard_map/ppermute | solution.py:363
  64.4 6.9 %collective-permute-start.24 = (bf16[8,2688]{1,0:T(8,128)(2,1)S(1)}, bf16[8,2688]{1,0:T(8,128)(2,1)S(1)}, u32[]{:S(2)}, u32[]{:S(2)}) collective-permute-start(bf16[8,2688]{1,0:T(8,128)(2,1)S(1)} %add_convert_fusion), channel_id=1, source_target_pairs={{0,128},{128,0},{1,129},{129,1},{2,130},{130,2},{3,131},{131,3},{4... | collective-permute-start | bytes 129032 | tf_op jit(solution)/shard_map/ppermute | solution.py:366
  71.3 6.0 %collective-permute-start.25 = (f32[8,2688]{1,0:T(8,128)S(1)}, f32[8,2688]{1,0:T(8,128)S(1)}, u32[]{:S(2)}, u32[]{:S(2)}) collective-permute-start(f32[8,2688]{1,0:T(8,128)S(1)} %convert_add_fusion.own_ref), channel_id=1, source_target_pairs={{0,16},{16,0},{32,48},{48,32},{64,80},{80,64},{96,112},{112,96},{1... | collective-permute-start | bytes 258056 | tf_op jit(solution)/shard_map/ppermute | solution.py:367
  (5 other events, 8.7 us)

commit v3 on v2

--- a/solution.py
+++ b/solution.py
@@ -10,7 +10,6 @@
 W = 128
 K1, K2 = 27 * 64, 27 * 128
 K1P = 1792
-K1H = 896
 HALF = 2688
 KB = 896
 VMEM = pl.BlockSpec(memory_space=pltpu.VMEM)
@@ -65,16 +64,17 @@
     return 0.5 * jnp.tanh(0.5 * v) + 0.5
 
 
-def pack_first_kernel(w1_ref, out, acc):
+def pack_first_kernel(w1_ref, out):
+    w1 = [w1_ref[t].astype(F32) for t in range(27)]
+    out[...] = jnp.concatenate(w1 + [jnp.zeros((8, K1P - K1), F32)], axis=1).astype(BF16)
+
+
+def prepare_kernel(w2_ref, g_ref, b0, b1, b2, b3, rows_ref, acc):
+    x, _ = split()
     core = lax.rem(lax.axis_index("space"), 2)
-    w1 = [w1_ref[t].astype(F32) for t in range(27)]
-    acc[...] = jnp.concatenate(w1 + [jnp.zeros((8, K1P - K1), F32)], axis=1)
-    out[...] = acc[:, pl.ds(pl.multiple_of(core * K1H, W), K1H)].astype(BF16)
-
-
-def pack_second_kernel(w2_ref, g_ref, b0, b1, b2, b3, rows_ref):
-    x, _ = split()
-    w2 = [w2_ref[t].astype(F32) for t in range(27)]
+    for t in range(27):
+        acc[:, t * W : (t + 1) * W] = w2_ref[t].astype(F32)
+    w2 = acc[:, pl.ds(pl.multiple_of(core * (13 * W), W), K1P)]
     for d in range(2):
         t = jnp.swapaxes(g_ref[:, d].astype(F32), 0, 1)
         rows_ref[d, 0] = jnp.zeros((8, W), F32)
@@ -83,23 +83,31 @@
     for k, out in enumerate((b0, b1, b2, b3)):
         h0 = xor(x, k) * 4
         parts = [rows_ref[d, h0 + h] for d in range(2) for h in range(6)]
-        out[...] = jnp.concatenate(w2 + parts, axis=1).astype(BF16)
-
-
-def stack_kernel(b0, b1, b2, b3, w1_ref, acc):
+        out[...] = jnp.concatenate([w2] + parts, axis=1).astype(BF16)
+
+
+def pack_kernel(w0_ref, p1_ref, p2_ref, a0, a1, a2, a3, b0, b1, b2, b3):
     _, zl = split()
+    core = lax.rem(lax.axis_index("space"), 2)
+    w0, p1, p2 = w0_ref[...], p1_ref[...], p2_ref[...]
+    same, other = jnp.where(core == 0, w0, p1), jnp.where(core == 0, p1, p2)
+    even = lax.rem(zl, 2) == 0
+    low, high = jnp.where(even, same, other), jnp.where(even, other, same)
+    for a, b in zip((a0, a1, a2, a3), (b0, b1, b2, b3)):
+        b[:, :K1P] = low
+        b[:, K1P : 2 * K1P] = high
+        b[:, 2 * K1P :] = a[...]
+
+
+def order_kernel(b0, b1, b2, b3, half_ref, go_ref, acc, acc_go):
+    x, _ = split()
     for k, b in enumerate((b0, b1, b2, b3)):
-        acc[rows8(xor(zl, k)), :] = b[...].astype(F32)
-    w1_ref[...] = acc[...].astype(BF16)
-
-
-def order_kernel(c0, c1, c2, c3, w1_ref, acc):
-    x, _ = split()
-    for k, c in enumerate((c0, c1, c2, c3)):
-        v = c[...].astype(F32)
-        for z in range(4):
-            acc[rows8(z * 4 + xor(x, k)), :] = v[z * 8 : z * 8 + 8]
-    w1_ref[...] = acc[...].astype(BF16)
+        v = b[...].astype(F32)
+        for j in range(3):
+            acc[rows8(j * 4 + xor(x, k)), :] = v[:, j * K1P : (j + 1) * K1P]
+        acc_go[rows8(xor(x, k)), :] = v[:, 3 * K1P :]
+    half_ref[...] = acc[...].astype(BF16)
+    go_ref[...] = acc_go[...].astype(BF16)
 
 
 def widen_kernel(xo_ref, xp_ref, xn_ref, xi_ref):
@@ -116,9 +124,9 @@
 def conv_first_kernel(own_ref, got_ref, xi_ref, slope_ref, xa_ref, zs):
     x, zl = split()
     p = lax.axis_index("space")
-    own, got = own_ref[...], got_ref[...]
-    first = lax.rem(p, 2) == 0
-    w1 = jnp.concatenate([jnp.where(first, own, got), jnp.where(first, got, own)], axis=1)[:, :K1]
+    own, got = own_ref[:64], got_ref[:64]
+    first = lax.rem(lax.div(zl, 2) + p, 2) == 0
+    w1 = jnp.concatenate([jnp.where(first, own, got), jnp.where(first, got, own)], axis=0)[:, :K1]
 
     for i in range(16):
         dd, hh = i // 4, i % 4 * 2
@@ -150,11 +158,12 @@
             slope_ref[:, (d * 4 + h) * W : (d * 4 + h + 1) * W] = q * (1.0 + v * (1.0 - q))
 
 
-def conv_second_kernel(b0, b1, b2, b3, xa_ref, y_ref, gs0_ref, gs1_ref, w2b_ref, acc, w2_ref):
-    x, _ = split()
-    for k, b in enumerate((b0, b1, b2, b3)):
-        acc[rows8(xor(x, k)), :] = b[...].astype(F32)
-    w2_ref[...] = acc[:, :K2].astype(BF16)
+def conv_second_kernel(own_ref, got_ref, go_ref, xa_ref, y_ref, gs0_ref, gs1_ref, w2b_ref, acc, w2_ref):
+    first = lax.rem(lax.axis_index("space"), 2) == 0
+    own, got = own_ref[64:], got_ref[64:]
+    w2_ref[:, : 14 * W] = jnp.where(first, own, got)
+    w2_ref[:, 14 * W :] = jnp.where(first, got, own)[:, W:]
+    acc[...] = w2_ref[...].astype(F32)
     for j in range(7):
         taps = [acc[:, t * W : (t + 1) * W] if t < 27 else jnp.zeros((32, W), F32) for t in range(4 * j, 4 * j + 4)]
         w2b_ref[:, j * W : (j + 1) * W] = jnp.concatenate(taps, axis=0).T.astype(BF16)
@@ -179,7 +188,7 @@
             if 1 <= hh <= 4:
                 at = (d * 4 + hh - 1) * W
                 y_ref[:, at : at + W] = (v * q).astype(BF16)
-            g = acc[:, K2 + (d * 6 + hh) * W : K2 + (d * 6 + hh + 1) * W]
+            g = go_ref[:, (d * 6 + hh) * W : (d * 6 + hh + 1) * W].astype(F32)
             gs = (g * (q * (1.0 + v * (1.0 - q)))).astype(BF16)
             (gs0_ref if d == 0 else gs1_ref)[hh] = gs
 
@@ -289,47 +298,53 @@
     other = [(i, i ^ 1) for i in range(8)]
     x = lax.rem(lax.axis_index("filt"), 4)
 
-    (w0,) = run(
-        pack_first_kernel,
-        [sds((8, K1H), BF16)],
-        [jnp.transpose(w_first, (0, 2, 1))],
-        [pltpu.VMEM((8, K1P), F32)],
-    )
-    c = [w0] + [lax.ppermute(w0, "filt", Z[k]) for k in (1, 2, 3)]
-    act_in, w0 = lax.optimization_barrier((act_in, w0))
+    (w0,) = run(pack_first_kernel, [sds((8, K1P), BF16)], [jnp.transpose(w_first, (0, 2, 1))])
+    joint = ("space", "filt")
+
+    def zed(k0, k1):
+        return [(p * 16 + f, p * 16 + (f ^ (4 * (k1 if p % 2 else k0)))) for p in range(8) for f in range(16)]
+
+    p1 = lax.ppermute(w0, joint, zed(1, 2))
+    p2 = lax.ppermute(w0, joint, zed(0, 3))
+
     w_second, grad_out, w0 = lax.optimization_barrier((w_second, grad_out, w0))
+    act_in, p1 = lax.optimization_barrier((act_in, p1))
     rows = jnp.pad(jnp.transpose(act_in[0], (1, 2, 0, 3)), ((0, 0), (3, 3), (0, 0), (0, 0)))
     xo = lax.dynamic_slice_in_dim(rows, x * 4, 10, axis=1).reshape(20, 64, W)
+    a = run(
+        prepare_kernel,
+        [sds((8, K1P + 12 * W), BF16)] * 4,
+        [jnp.transpose(w_second, (0, 2, 1)), grad_out[0]],
+        [pltpu.VMEM((2, 18, 8, W), F32), pltpu.VMEM((8, K2), F32)],
+        10**9,
+    )
     xp = lax.ppermute(xo, "space", up)
     xn = lax.ppermute(xo, "space", down)
 
-    (w1,) = run(stack_kernel, [sds((32, K1H), BF16)], c, [pltpu.VMEM((32, K1H), F32)])
-    c = [w1] + [lax.ppermute(w1, "filt", X[k]) for k in (1, 2, 3)]
-    b = run(
-        pack_second_kernel,
-        [sds((8, K2 + 12 * W), BF16)] * 4,
-        [jnp.transpose(w_second, (0, 2, 1)), grad_out[0]],
-        [pltpu.VMEM((2, 18, 8, W), F32)],
-    )
-    b, c = lax.optimization_barrier((b, c))
-    (w1,) = run(order_kernel, [sds((128, K1H), BF16)], c, [pltpu.VMEM((128, K1H), F32)])
-    w1got = lax.ppermute(w1, "space", other)
-
-    b, w1 = lax.optimization_barrier((b, w1))
+    a, p1, p2 = lax.optimization_barrier((a, p1, p2))
+    b = run(pack_kernel, [sds((8, 3 * K1P + 12 * W), BF16)] * 4, [w0, p1, p2] + list(a))
     b = [b[0]] + [lax.ppermute(b[k], "filt", X[k]) for k in (1, 2, 3)]
+    half, go = run(
+        order_kernel,
+        [sds((96, K1P), BF16), sds((32, 12 * W), BF16)],
+        b,
+        [pltpu.VMEM((96, K1P), F32), pltpu.VMEM((32, 12 * W), F32)],
+    )
+    half_got = lax.ppermute(half, "space", other)
+
     (xi,) = run(widen_kernel, [sds((60, 192, W), BF16)], [xo, xp, xn], flops=8 * 10**8)
     slope, xa = run(
         conv_first_kernel,
         [sds((32, 1024), F32), sds((32, 384, W), BF16)],
-        [w1, w1got, xi],
+        [half, half_got, xi],
         [pltpu.VMEM((32, 128, W), F32)],
         4 * 10**9,
     )
     y, gs0, gs1, w2b = run(
         conv_second_kernel,
         [sds((32, 1024), BF16), sds((6, 32, W), BF16), sds((6, 32, W), BF16), sds((128, KB), BF16)],
-        b + [xa],
-        [pltpu.VMEM((32, K2 + 12 * W), F32), pltpu.VMEM((32, K2), BF16)],
+        [half, half_got, go, xa],
+        [pltpu.VMEM((32, K2), F32), pltpu.VMEM((32, K2), BF16)],
     )
     gp = lax.ppermute(gs1, "space", up)
     gn = lax.ppermute(gs0, "space", down)
@@ -341,6 +356,7 @@
         [gs0, gs1, gp, gn, w2b],
         [pltpu.VMEM((24, 96, W), BF16), pltpu.VMEM((128, 1024), F32)],
     )
+    s, dw2 = lax.optimization_barrier((s, dw2))
     s = [lax.ppermute(s[k - 1], "filt", Z[k]) for k in (1, 2, 3)]
 
     keep, give = run(

time: 78.4 us -> 73.9 us (0.943)
  starting transfers between devices: 45.2 us -> 42.7 us
  local copies, waits for them, and re-layouts: 4.49 us -> 3.44 us
  waiting for transfers between devices: 18.9 us -> 17.9 us
    ppermute x7 -> x3, starting transfers between devices: 11.3 us -> 7.26 us  [the longest x1 7.07 us: local(): p2 = lax.ppermute(w0, joint, zed(0, 3))]
    ppermute x7 -> x3, waiting for transfers between devices: 5.48 us -> 1.89 us  [the longest x1 1.88 us: local(): p1 = lax.ppermute(w0, joint, zed(1, 2))]
    ppermute x1, starting transfers between devices: 0.8 us -> 4.35 us  [local(): gn = lax.ppermute(gs0, 'space', down)]
    ppermute x1, starting transfers between devices: 3.25 us -> 0.02 us  [local(): xn = lax.ppermute(xo, 'space', down)]
    ppermute x1, waiting for transfers between devices: 0.01 us -> 2.04 us  [local(): xn = lax.ppermute(xo, 'space', down)]
    ppermute x1, waiting for transfers between devices: 1.77 us -> 0.01 us  [local(): gn = lax.ppermute(gs0, 'space', down)]
    ppermute x1, starting transfers between devices: 0.01 us -> 1.73 us  [local(): xp = lax.ppermute(xo, 'space', up)]
    ppermute x3, waiting for transfers between devices: 1.17 us -> 2.85 us  [local(): s = [lax.ppermute(s[k - 1], 'filt', Z[k]) for k in (1, 2, 3)]]
  transfers between devices with their start and end apart: 26 -> 22, of which waited for: 14 -> 14; matrix products, arithmetic and copies ran while one was open for 1% -> 1% of each run, Pallas kernels for 7% -> 4%
where the time goes in v3:
time: 73.9 us; the launch traced here: 73.6 us
  starting transfers between devices  42.7 us (58%)
  waiting for transfers between devices  17.9 us (24%)
  Pallas kernels  8.7 us (12%)
  local copies, waits for them, and re-layouts  3.44 us (5%)
  between operations  0.82 us (1%)
    pallas_call x13, Pallas kernels, run(): pl.pallas_call(kernel, out_shape=outs, in_specs=[VMEM] * len(args), out_s...  8.7 us
    ppermute x1, starting transfers between devices, local(): p2 = lax.ppermute(w0, joint, zed(0, 3))  7.07 us
    ppermute x1, starting transfers between devices, local(): lax.ppermute(part, 'sample', [(0, 1), (1, 0)]).astype(F32)  5.07 us
    ppermute x1, starting transfers between devices, local(): got = lax.ppermute(part, 'space', other)  4.75 us
    ppermute x1, starting transfers between devices, local(): got = lax.ppermute(give, 'space', other)  4.63 us
    ppermute x1, starting transfers between devices, local(): gn = lax.ppermute(gs0, 'space', down)  4.35 us
    ppermute x3, starting transfers between devices, local(): b = [b[0]] + [lax.ppermute(b[k], 'filt', X[k]) for k in (1, 2, 3)]  3.95 us
    ppermute x3, starting transfers between devices, local(): s = [lax.ppermute(s[k - 1], 'filt', X[k]) for k in (1, 2, 3)]  3.94 us
  transfers between devices with their start and end apart: 22, of which 14 were waited for; matrix products, arithmetic and copies ran while one was open for 1% of the time, Pallas kernels for 4%

profile of v3, /device:TPU:1, one launch (start us, length us, event | category | flops | bytes accessed | tf_op | source)
XLA Modules:
  0.0 73.6 jit_solution(3802420783517866682)
XLA Ops:
  1.5 7.1 %collective-permute-start.1 = (bf16[8,1792]{1,0:T(8,128)(2,1)S(1)}, bf16[8,1792]{1,0:T(8,128)(2,1)S(1)}, u32[]{:S(2)}, u32[]{:S(2)}) collective-permute-start(bf16[8,1792]{1,0:T(8,128)(2,1)S(1)} %shard_map.67.w0_ref), channel_id=1, source_target_pairs={{0,0},{1,1},{2,2},{3,3},{4,4},{5,5},{6,6},{7,7},{8,8},{9,9},{10,10... | collective-permute-start | bytes 86024 | tf_op jit(solution)/shard_map/ppermute | solution.py:308
  10.4 1.9 %collective-permute-done.p1_ref = bf16[8,1792]{1,0:T(8,128)(2,1)S(1)} collective-permute-done((bf16[8,1792]{1,0:T(8,128)(2,1)S(1)}, bf16[8,1792]{1,0:T(8,128)(2,1)S(1)}, u32[]{:S(2)}, u32[]{:S(2)}) %collective-permute-start) | collective-permute-done | bytes 28704 | tf_op jit(solution)/shard_map/ppermute | solution.py:307
  12.4 1.3 %collective-permute-start.2 = (bf16[8,6912]{1,0:T(8,128)(2,1)S(1)}, bf16[8,6912]{1,0:T(8,128)(2,1)S(1)}, u32[]{:S(2)}, u32[]{:S(2)}) collective-permute-start(bf16[8,6912]{1,0:T(8,128)(2,1)S(1)} %get-tuple-element.64), channel_id=1, source_target_pairs={{0,1},{1,0},{2,3},{3,2},{4,5},{5,4},{6,7},{7,6},{8,9},{9,8},{10,11... | collective-permute-start | bytes 331784 | tf_op jit(solution)/shard_map/ppermute | solution.py:326
  13.7 2.5 %collective-permute-start.3 = (bf16[8,6912]{1,0:T(8,128)(2,1)S(1)}, bf16[8,6912]{1,0:T(8,128)(2,1)S(1)}, u32[]{:S(2)}, u32[]{:S(2)}) collective-permute-start(bf16[8,6912]{1,0:T(8,128)(2,1)S(1)} %get-tuple-element.65), channel_id=1, source_target_pairs={{0,2},{1,3},{2,0},{3,1},{4,6},{5,7},{6,4},{7,5},{8,10},{9,11},{10,... | collective-permute-start | bytes 331784 | tf_op jit(solution)/shard_map/ppermute | solution.py:326
  16.7 1.7 %collective-permute-start.6 = (bf16[20,64,128]{2,1,0:T(8,128)(2,1)S(1)}, bf16[20,64,128]{2,1,0:T(8,128)(2,1)S(1)}, u32[]{:S(2)}, u32[]{:S(2)}) collective-permute-start(bf16[20,64,128]{2,1,0:T(8,128)(2,1)S(1)} %bitcast.14), channel_id=1, source_target_pairs={{0,16},{16,32},{32,48},{48,64},{64,80},{80,96},{96,112},{112,0},{1... | collective-permute-start | bytes 983048 | tf_op jit(solution)/shard_map/ppermute | solution.py:321
  18.4 1.0 %collective-permute-done.3.b2 = bf16[8,6912]{1,0:T(8,128)(2,1)S(1)} collective-permute-done((bf16[8,6912]{1,0:T(8,128)(2,1)S(1)}, bf16[8,6912]{1,0:T(8,128)(2,1)S(1)}, u32[]{:S(2)}, u32[]{:S(2)}) %collective-permute-start.3) | collective-permute-done | bytes 110624 | tf_op jit(solution)/shard_map/ppermute | solution.py:326
  19.4 1.5 %collective-permute-done.4.b3 = bf16[8,6912]{1,0:T(8,128)(2,1)S(1)} collective-permute-done((bf16[8,6912]{1,0:T(8,128)(2,1)S(1)}, bf16[8,6912]{1,0:T(8,128)(2,1)S(1)}, u32[]{:S(2)}, u32[]{:S(2)}) %collective-permute-start.4) | collective-permute-done | bytes 110624 | tf_op jit(solution)/shard_map/ppermute | solution.py:326
  21.1 2.0 %collective-permute-done.7.xn_ref = bf16[20,64,128]{2,1,0:T(8,128)(2,1)S(1)} collective-permute-done((bf16[20,64,128]{2,1,0:T(8,128)(2,1)S(1)}, bf16[20,64,128]{2,1,0:T(8,128)(2,1)S(1)}, u32[]{:S(2)}, u32[]{:S(2)}) %collective-permute-start.7) | collective-permute-done | bytes 327712 | tf_op jit(solution)/shard_map/ppermute | solution.py:322
  23.8 2.3 %shard_map.72 = (f32[32,1024]{1,0:T(8,128)S(1)}, bf16[32,384,128]{2,1,0:T(8,128)(2,1)S(1)}) custom-call(bf16[96,1792]{1,0:T(8,128)(2,1)S(1)} %get-tuple-element.67.own_ref, bf16[96,1792]{1,0:T(8,128)(2,1)S(1)} %collective-permute-done.5.got_ref, bf16[60,192,128]{2,1,0:T(8,128)(2,1)S(1)} %shard_map.71.xi_ref), custom_call_target="tpu_custom_call" | custom-call | flops 4000000000 | bytes 100000 | tf_op jit(solution)/shard_map/pallas_call | solution.py:20
  26.9 4.3 %collective-permute-start.9 = (bf16[6,32,128]{2,1,0:T(8,128)(2,1)S(1)}, bf16[6,32,128]{2,1,0:T(8,128)(2,1)S(1)}, u32[]{:S(2)}, u32[]{:S(2)}) collective-permute-start(bf16[6,32,128]{2,1,0:T(8,128)(2,1)S(1)} %get-tuple-element.71.gs0_ref), channel_id=1, source_target_pairs={{16,0},{32,16},{48,32},{64,48},{80,64},{96,80},{112,96},{0,112},{1... | collective-permute-start | bytes 147464 | tf_op jit(solution)/shard_map/ppermute | solution.py:350
  31.3 2.1 %shard_map.75.dw2_ref = f32[32,3456]{1,0:T(8,128)S(1)} custom-call(bf16[32,384,128]{2,1,0:T(8,128)(2,1)S(1)} %get-tuple-element.70.xa_ref, bf16[6,32,128]{2,1,0:T(8,128)(2,1)S(1)} %get-tuple-element.71.gs0_ref, bf16[6,32,128]{2,1,0:T(8,128)(2,1)S(1)} %get-tuple-element.72.gs1_ref), custom_call_target="tpu_custom_call" | custom-call | flops 2500000000 | bytes 100000 | tf_op jit(solution)/shard_map/pallas_call | solution.py:20
  34.1 1.1 %collective-permute-start.11 = (bf16[32,1024]{1,0:T(8,128)(2,1)S(1)}, bf16[32,1024]{1,0:T(8,128)(2,1)S(1)}, u32[]{:S(2)}, u32[]{:S(2)}) collective-permute-start(bf16[32,1024]{1,0:T(8,128)(2,1)S(1)} %get-tuple-element.79), channel_id=1, source_target_pairs={{0,8},{1,9},{2,10},{3,11},{4,12},{5,13},{6,14},{7,15},{8,0},{9,1},... | collective-permute-start | bytes 196616 | tf_op jit(solution)/shard_map/ppermute | solution.py:360
  35.2 2.5 %collective-permute-start.12 = (bf16[32,1024]{1,0:T(8,128)(2,1)S(1)}, bf16[32,1024]{1,0:T(8,128)(2,1)S(1)}, u32[]{:S(2)}, u32[]{:S(2)}) collective-permute-start(bf16[32,1024]{1,0:T(8,128)(2,1)S(1)} %get-tuple-element.80), channel_id=1, source_target_pairs={{0,12},{1,13},{2,14},{3,15},{4,8},{5,9},{6,10},{7,11},{8,4},{9,5},... | collective-permute-start | bytes 196616 | tf_op jit(solution)/shard_map/ppermute | solution.py:360
  38.2 2.3 %collective-permute-done.12.r3 = bf16[32,1024]{1,0:T(8,128)(2,1)S(1)} collective-permute-done((bf16[32,1024]{1,0:T(8,128)(2,1)S(1)}, bf16[32,1024]{1,0:T(8,128)(2,1)S(1)}, u32[]{:S(2)}, u32[]{:S(2)}) %collective-permute-start.12) | collective-permute-done | bytes 65568 | tf_op jit(solution)/shard_map/ppermute | solution.py:360
  40.5 1.1 %shard_map.76 = (f32[32,2688]{1,0:T(8,128)S(1)}, f32[32,2688]{1,0:T(8,128)S(1)}) custom-call(f32[32,1024]{1,0:T(8,128)S(1)} %get-tuple-element.74.own_ref, bf16[32,1024]{1,0:T(8,128)(2,1)S(1)} %collective-permute-done.10.r1, bf16[32,1024]{1,0:T(8,128)(2,1)S(1)} %collective-permute-done.11.r2, bf16[32,1024]{1,0:T(8,128)(2,1)S(1)} %collective-permute-done.12.r3, ...), custom_call_target="tpu_custom_call" | custom-call | flops 100000000 | bytes 100000 | tf_op jit(solution)/shard_map/pallas_call | solution.py:20
  41.7 4.6 %collective-permute-start.13 = (f32[32,2688]{1,0:T(8,128)S(1)}, f32[32,2688]{1,0:T(8,128)S(1)}, u32[]{:S(2)}, u32[]{:S(2)}) collective-permute-start(f32[32,2688]{1,0:T(8,128)S(1)} %get-tuple-element.84), channel_id=1, source_target_pairs={{0,16},{16,0},{32,48},{48,32},{64,80},{80,64},{96,112},{112,96},{1... | collective-permute-start | bytes 1032200 | tf_op jit(solution)/shard_map/ppermute | solution.py:368
  46.3 1.3 %collective-permute-done.13.got_ref = f32[32,2688]{1,0:T(8,128)S(1)} collective-permute-done((f32[32,2688]{1,0:T(8,128)S(1)}, f32[32,2688]{1,0:T(8,128)S(1)}, u32[]{:S(2)}, u32[]{:S(2)}) %collective-permute-start.13) | collective-permute-done | bytes 344096 | tf_op jit(solution)/shard_map/ppermute | solution.py:368
  47.8 3.0 %collective-permute-start.15 = (bf16[8,3712]{1,0:T(8,128)(2,1)S(1)}, bf16[8,3712]{1,0:T(8,128)(2,1)S(1)}, u32[]{:S(2)}, u32[]{:S(2)}) collective-permute-start(bf16[8,3712]{1,0:T(8,128)(2,1)S(1)} %get-tuple-element.89), channel_id=1, source_target_pairs={{0,2},{1,3},{2,0},{3,1},{4,6},{5,7},{6,4},{7,5},{8,10},{9,11},{10,... | collective-permute-start | bytes 178184 | tf_op jit(solution)/shard_map/ppermute | solution.py:375
  51.6 1.9 %collective-permute-done.15.r2 = bf16[8,3712]{1,0:T(8,128)(2,1)S(1)} collective-permute-done((bf16[8,3712]{1,0:T(8,128)(2,1)S(1)}, bf16[8,3712]{1,0:T(8,128)(2,1)S(1)}, u32[]{:S(2)}, u32[]{:S(2)}) %collective-permute-start.15) | collective-permute-done | bytes 59424 | tf_op jit(solution)/shard_map/ppermute | solution.py:375
  53.5 1.6 %collective-permute-done.16.r3 = bf16[8,3712]{1,0:T(8,128)(2,1)S(1)} collective-permute-done((bf16[8,3712]{1,0:T(8,128)(2,1)S(1)}, bf16[8,3712]{1,0:T(8,128)(2,1)S(1)}, u32[]{:S(2)}, u32[]{:S(2)}) %collective-permute-start.16) | collective-permute-done | bytes 59424 | tf_op jit(solution)/shard_map/ppermute | solution.py:375
  55.8 2.6 %collective-permute-start.17 = (bf16[8,2688]{1,0:T(8,128)(2,1)S(1)}, bf16[8,2688]{1,0:T(8,128)(2,1)S(1)}, u32[]{:S(2)}, u32[]{:S(2)}) collective-permute-start(bf16[8,2688]{1,0:T(8,128)(2,1)S(1)} %get-tuple-element.92), channel_id=1, source_target_pairs={{0,32},{16,48},{32,0},{48,16},{64,96},{80,112},{96,64},{112,80},{1... | collective-permute-start | bytes 129032 | tf_op jit(solution)/shard_map/ppermute | solution.py:379
  60.3 5.1 %collective-permute-start.20 = (bf16[8,2688]{1,0:T(8,128)(2,1)S(1)}, bf16[8,2688]{1,0:T(8,128)(2,1)S(1)}, u32[]{:S(2)}, u32[]{:S(2)}) collective-permute-start(bf16[8,2688]{1,0:T(8,128)(2,1)S(1)} %add_convert_fusion), channel_id=1, source_target_pairs={{0,128},{128,0},{1,129},{129,1},{2,130},{130,2},{3,131},{131,3},{4... | collective-permute-start | bytes 129032 | tf_op jit(solution)/shard_map/ppermute | solution.py:382
  65.4 1.8 %collective-permute-done.20 = bf16[8,2688]{1,0:T(8,128)(2,1)S(1)} collective-permute-done((bf16[8,2688]{1,0:T(8,128)(2,1)S(1)}, bf16[8,2688]{1,0:T(8,128)(2,1)S(1)}, u32[]{:S(2)}, u32[]{:S(2)}) %collective-permute-start.20) | collective-permute-done | bytes 43040 | tf_op jit(solution)/shard_map/ppermute | solution.py:382
  67.2 4.7 %collective-permute-start.21 = (f32[8,2688]{1,0:T(8,128)S(1)}, f32[8,2688]{1,0:T(8,128)S(1)}, u32[]{:S(2)}, u32[]{:S(2)}) collective-permute-start(f32[8,2688]{1,0:T(8,128)S(1)} %convert_add_fusion.own_ref), channel_id=1, source_target_pairs={{0,16},{16,0},{32,48},{48,32},{64,80},{80,64},{96,112},{112,96},{1... | collective-permute-start | bytes 258056 | tf_op jit(solution)/shard_map/ppermute | solution.py:383
  (47 shorter events, 11.5 us)
Async XLA Ops:
  1.5 10.8 %collective-permute-start.1 = (bf16[8,1792]{1,0:T(8,128)(2,1)S(1)}, bf16[8,1792]{1,0:T(8,128)(2,1)S(1)}, u32[]{:S(2)}, u32[]{:S(2)}) collective-permute-start(bf16[8,1792]{1,0:T(8,128)(2,1)S(1)} %shard_map.67.w0_ref), channel_id=1, source_target_pairs={{0,0},{1,1},{2,2},{3,3},{4,4},{5,5},{6,6},{7,7},{8,8},{9,9},{10,10... | collective-permute-start | bytes 86024 | tf_op jit(solution)/shard_map/ppermute | solution.py:308
  8.6 3.7 %collective-permute-start = (bf16[8,1792]{1,0:T(8,128)(2,1)S(1)}, bf16[8,1792]{1,0:T(8,128)(2,1)S(1)}, u32[]{:S(2)}, u32[]{:S(2)}) collective-permute-start(bf16[8,1792]{1,0:T(8,128)(2,1)S(1)} %shard_map.67.w0_ref), channel_id=1, source_target_pairs={{0,4},{1,5},{2,6},{3,7},{4,0},{5,1},{6,2},{7,3},{8,12},{9,13},{10,... | collective-permute-start | bytes 86024 | tf_op jit(solution)/shard_map/ppermute | solution.py:307
  8.7 0.8 %copy-start = (bf16[1,8,2,16,128]{4,3,2,1,0:T(8,128)(2,1)S(1)}, bf16[1,8,2,16,128]{4,3,2,1,0:T(8,128)(2,1)}, u32[]{:S(2)}) copy-start(bf16[1,8,2,16,128]{4,3,2,1,0:T(8,128)(2,1)} %param.7) | copy-start | bytes 196612
  10.4 5.9 %copy-start.3 = (bf16[1,64,2,16,128]{4,3,2,1,0:T(8,128)(2,1)S(1)}, bf16[1,64,2,16,128]{4,3,2,1,0:T(8,128)(2,1)}, u32[]{:S(2)}) copy-start(bf16[1,64,2,16,128]{4,3,2,1,0:T(8,128)(2,1)} %param.4) | copy-start | bytes 1572868
  12.4 6.1 %collective-permute-start.2 = (bf16[8,6912]{1,0:T(8,128)(2,1)S(1)}, bf16[8,6912]{1,0:T(8,128)(2,1)S(1)}, u32[]{:S(2)}, u32[]{:S(2)}) collective-permute-start(bf16[8,6912]{1,0:T(8,128)(2,1)S(1)} %get-tuple-element.64), channel_id=1, source_target_pairs={{0,1},{1,0},{2,3},{3,2},{4,5},{5,4},{6,7},{7,6},{8,9},{9,8},{10,11... | collective-permute-start | bytes 331784 | tf_op jit(solution)/shard_map/ppermute | solution.py:326
  13.7 5.8 %collective-permute-start.3 = (bf16[8,6912]{1,0:T(8,128)(2,1)S(1)}, bf16[8,6912]{1,0:T(8,128)(2,1)S(1)}, u32[]{:S(2)}, u32[]{:S(2)}) collective-permute-start(bf16[8,6912]{1,0:T(8,128)(2,1)S(1)} %get-tuple-element.65), channel_id=1, source_target_pairs={{0,2},{1,3},{2,0},{3,1},{4,6},{5,7},{6,4},{7,5},{8,10},{9,11},{10,... | collective-permute-start | bytes 331784 | tf_op jit(solution)/shard_map/ppermute | solution.py:326
  16.1 4.8 %collective-permute-start.4 = (bf16[8,6912]{1,0:T(8,128)(2,1)S(1)}, bf16[8,6912]{1,0:T(8,128)(2,1)S(1)}, u32[]{:S(2)}, u32[]{:S(2)}) collective-permute-start(bf16[8,6912]{1,0:T(8,128)(2,1)S(1)} %get-tuple-element.66), channel_id=1, source_target_pairs={{0,3},{1,2},{2,1},{3,0},{4,7},{5,6},{6,5},{7,4},{8,11},{9,10},{10,... | collective-permute-start | bytes 331784 | tf_op jit(solution)/shard_map/ppermute | solution.py:326
  16.7 6.5 %collective-permute-start.7 = (bf16[20,64,128]{2,1,0:T(8,128)(2,1)S(1)}, bf16[20,64,128]{2,1,0:T(8,128)(2,1)S(1)}, u32[]{:S(2)}, u32[]{:S(2)}) collective-permute-start(bf16[20,64,128]{2,1,0:T(8,128)(2,1)S(1)} %bitcast.13), channel_id=1, source_target_pairs={{16,0},{32,16},{48,32},{64,48},{80,64},{96,80},{112,96},{0,112},{1... | collective-permute-start | bytes 983048 | tf_op jit(solution)/shard_map/ppermute | solution.py:322
  16.7 6.5 %collective-permute-start.6 = (bf16[20,64,128]{2,1,0:T(8,128)(2,1)S(1)}, bf16[20,64,128]{2,1,0:T(8,128)(2,1)S(1)}, u32[]{:S(2)}, u32[]{:S(2)}) collective-permute-start(bf16[20,64,128]{2,1,0:T(8,128)(2,1)S(1)} %bitcast.14), channel_id=1, source_target_pairs={{0,16},{16,32},{32,48},{48,64},{64,80},{80,96},{96,112},{112,0},{1... | collective-permute-start | bytes 983048 | tf_op jit(solution)/shard_map/ppermute | solution.py:321
  21.0 2.7 %collective-permute-start.5 = (bf16[96,1792]{1,0:T(8,128)(2,1)S(1)}, bf16[96,1792]{1,0:T(8,128)(2,1)S(1)}, u32[]{:S(2)}, u32[]{:S(2)}) collective-permute-start(bf16[96,1792]{1,0:T(8,128)(2,1)S(1)} %get-tuple-element.67.own_ref), channel_id=1, source_target_pairs={{0,16},{16,0},{32,48},{48,32},{64,80},{80,64},{96,112},{112,96},{1... | collective-permute-start | bytes 1032200 | tf_op jit(solution)/shard_map/ppermute | solution.py:333
  26.9 6.5 %collective-permute-start.9 = (bf16[6,32,128]{2,1,0:T(8,128)(2,1)S(1)}, bf16[6,32,128]{2,1,0:T(8,128)(2,1)S(1)}, u32[]{:S(2)}, u32[]{:S(2)}) collective-permute-start(bf16[6,32,128]{2,1,0:T(8,128)(2,1)S(1)} %get-tuple-element.71.gs0_ref), channel_id=1, source_target_pairs={{16,0},{32,16},{48,32},{64,48},{80,64},{96,80},{112,96},{0,112},{1... | collective-permute-start | bytes 147464 | tf_op jit(solution)/shard_map/ppermute | solution.py:350
  31.3 2.2 %collective-permute-start.8 = (bf16[6,32,128]{2,1,0:T(8,128)(2,1)S(1)}, bf16[6,32,128]{2,1,0:T(8,128)(2,1)S(1)}, u32[]{:S(2)}, u32[]{:S(2)}) collective-permute-start(bf16[6,32,128]{2,1,0:T(8,128)(2,1)S(1)} %get-tuple-element.72.gs1_ref), channel_id=1, source_target_pairs={{0,16},{16,32},{32,48},{48,64},{64,80},{80,96},{96,112},{112,0},{1... | collective-permute-start | bytes 147464 | tf_op jit(solution)/shard_map/ppermute | solution.py:349
  34.0 3.6 %collective-permute-start.10 = (bf16[32,1024]{1,0:T(8,128)(2,1)S(1)}, bf16[32,1024]{1,0:T(8,128)(2,1)S(1)}, u32[]{:S(2)}, u32[]{:S(2)}) collective-permute-start(bf16[32,1024]{1,0:T(8,128)(2,1)S(1)} %get-tuple-element.78), channel_id=1, source_target_pairs={{0,4},{1,5},{2,6},{3,7},{4,0},{5,1},{6,2},{7,3},{8,12},{9,13},{10,... | collective-permute-start | bytes 196616 | tf_op jit(solution)/shard_map/ppermute | solution.py:360
  34.1 4.1 %collective-permute-start.11 = (bf16[32,1024]{1,0:T(8,128)(2,1)S(1)}, bf16[32,1024]{1,0:T(8,128)(2,1)S(1)}, u32[]{:S(2)}, u32[]{:S(2)}) collective-permute-start(bf16[32,1024]{1,0:T(8,128)(2,1)S(1)} %get-tuple-element.79), channel_id=1, source_target_pairs={{0,8},{1,9},{2,10},{3,11},{4,12},{5,13},{6,14},{7,15},{8,0},{9,1},... | collective-permute-start | bytes 196616 | tf_op jit(solution)/shard_map/ppermute | solution.py:360
  35.2 5.3 %collective-permute-start.12 = (bf16[32,1024]{1,0:T(8,128)(2,1)S(1)}, bf16[32,1024]{1,0:T(8,128)(2,1)S(1)}, u32[]{:S(2)}, u32[]{:S(2)}) collective-permute-start(bf16[32,1024]{1,0:T(8,128)(2,1)S(1)} %get-tuple-element.80), channel_id=1, source_target_pairs={{0,12},{1,13},{2,14},{3,15},{4,8},{5,9},{6,10},{7,11},{8,4},{9,5},... | collective-permute-start | bytes 196616 | tf_op jit(solution)/shard_map/ppermute | solution.py:360
  41.7 5.9 %collective-permute-start.13 = (f32[32,2688]{1,0:T(8,128)S(1)}, f32[32,2688]{1,0:T(8,128)S(1)}, u32[]{:S(2)}, u32[]{:S(2)}) collective-permute-start(f32[32,2688]{1,0:T(8,128)S(1)} %get-tuple-element.84), channel_id=1, source_target_pairs={{0,16},{16,0},{32,48},{48,32},{64,80},{80,64},{96,112},{112,96},{1... | collective-permute-start | bytes 1032200 | tf_op jit(solution)/shard_map/ppermute | solution.py:368
  47.7 4.0 %collective-permute-start.14 = (bf16[8,3712]{1,0:T(8,128)(2,1)S(1)}, bf16[8,3712]{1,0:T(8,128)(2,1)S(1)}, u32[]{:S(2)}, u32[]{:S(2)}) collective-permute-start(bf16[8,3712]{1,0:T(8,128)(2,1)S(1)} %get-tuple-element.88), channel_id=1, source_target_pairs={{0,1},{1,0},{2,3},{3,2},{4,5},{5,4},{6,7},{7,6},{8,9},{9,8},{10,11... | collective-permute-start | bytes 178184 | tf_op jit(solution)/shard_map/ppermute | solution.py:375
  47.8 5.7 %collective-permute-start.15 = (bf16[8,3712]{1,0:T(8,128)(2,1)S(1)}, bf16[8,3712]{1,0:T(8,128)(2,1)S(1)}, u32[]{:S(2)}, u32[]{:S(2)}) collective-permute-start(bf16[8,3712]{1,0:T(8,128)(2,1)S(1)} %get-tuple-element.89), channel_id=1, source_target_pairs={{0,2},{1,3},{2,0},{3,1},{4,6},{5,7},{6,4},{7,5},{8,10},{9,11},{10,... | collective-permute-start | bytes 178184 | tf_op jit(solution)/shard_map/ppermute | solution.py:375
  50.8 4.3 %collective-permute-start.16 = (bf16[8,3712]{1,0:T(8,128)(2,1)S(1)}, bf16[8,3712]{1,0:T(8,128)(2,1)S(1)}, u32[]{:S(2)}, u32[]{:S(2)}) collective-permute-start(bf16[8,3712]{1,0:T(8,128)(2,1)S(1)} %get-tuple-element.90), channel_id=1, source_target_pairs={{0,3},{1,2},{2,1},{3,0},{4,7},{5,6},{6,5},{7,4},{8,11},{9,10},{10,... | collective-permute-start | bytes 178184 | tf_op jit(solution)/shard_map/ppermute | solution.py:375
  55.1 4.2 %collective-permute-start.19 = (bf16[8,2688]{1,0:T(8,128)(2,1)S(1)}, bf16[8,2688]{1,0:T(8,128)(2,1)S(1)}, u32[]{:S(2)}, u32[]{:S(2)}) collective-permute-start(bf16[8,2688]{1,0:T(8,128)(2,1)S(1)} %get-tuple-element.92), channel_id=1, source_target_pairs={{0,96},{16,112},{32,64},{48,80},{64,32},{80,48},{96,0},{112,16},{1... | collective-permute-start | bytes 129032 | tf_op jit(solution)/shard_map/ppermute | solution.py:379
  55.3 4.4 %collective-permute-start.18 = (bf16[8,2688]{1,0:T(8,128)(2,1)S(1)}, bf16[8,2688]{1,0:T(8,128)(2,1)S(1)}, u32[]{:S(2)}, u32[]{:S(2)}) collective-permute-start(bf16[8,2688]{1,0:T(8,128)(2,1)S(1)} %get-tuple-element.92), channel_id=1, source_target_pairs={{0,64},{16,80},{32,96},{48,112},{64,0},{80,16},{96,32},{112,48},{1... | collective-permute-start | bytes 129032 | tf_op jit(solution)/shard_map/ppermute | solution.py:379
  55.8 4.5 %collective-permute-start.17 = (bf16[8,2688]{1,0:T(8,128)(2,1)S(1)}, bf16[8,2688]{1,0:T(8,128)(2,1)S(1)}, u32[]{:S(2)}, u32[]{:S(2)}) collective-permute-start(bf16[8,2688]{1,0:T(8,128)(2,1)S(1)} %get-tuple-element.92), channel_id=1, source_target_pairs={{0,32},{16,48},{32,0},{48,16},{64,96},{80,112},{96,64},{112,80},{1... | collective-permute-start | bytes 129032 | tf_op jit(solution)/shard_map/ppermute | solution.py:379
  60.3 6.9 %collective-permute-start.20 = (bf16[8,2688]{1,0:T(8,128)(2,1)S(1)}, bf16[8,2688]{1,0:T(8,128)(2,1)S(1)}, u32[]{:S(2)}, u32[]{:S(2)}) collective-permute-start(bf16[8,2688]{1,0:T(8,128)(2,1)S(1)} %add_convert_fusion), channel_id=1, source_target_pairs={{0,128},{128,0},{1,129},{129,1},{2,130},{130,2},{3,131},{131,3},{4... | collective-permute-start | bytes 129032 | tf_op jit(solution)/shard_map/ppermute | solution.py:382
  67.2 5.7 %collective-permute-start.21 = (f32[8,2688]{1,0:T(8,128)S(1)}, f32[8,2688]{1,0:T(8,128)S(1)}, u32[]{:S(2)}, u32[]{:S(2)}) collective-permute-start(f32[8,2688]{1,0:T(8,128)S(1)} %convert_add_fusion.own_ref), channel_id=1, source_target_pairs={{0,16},{16,0},{32,48},{48,32},{64,80},{80,64},{96,112},{112,96},{1... | collective-permute-start | bytes 258056 | tf_op jit(solution)/shard_map/ppermute | solution.py:383
  (2 other events, 1.6 us)

commit v4 on v3

--- a/solution.py
+++ b/solution.py
@@ -58,6 +58,17 @@
     left = jnp.where(lane == 0, 0.0, pltpu.roll(x, 1, 1))
     right = jnp.where(lane == W - 1, 0.0, pltpu.roll(x, W - 1, 1))
     return left, x, right
+
+
+def height_taps(row):
+    zero = jnp.zeros((32, W), BF16)
+    taps = []
+    for b in range(3):
+        cells = []
+        for d in range(2):
+            cells += [zero] * b + [row(d, h) for h in range(4)] + [zero] * (2 - b)
+        taps.append(jnp.concatenate(cells, axis=1))
+    return jnp.concatenate(taps, axis=0)
 
 
 def logistic(v):
@@ -110,18 +121,30 @@
     go_ref[...] = acc_go[...].astype(BF16)
 
 
-def widen_kernel(xo_ref, xp_ref, xn_ref, xi_ref):
+def widen(v, out, r):
+    for k, part in enumerate(shifted(v)):
+        out[r, k * 64 : (k + 1) * 64] = part.astype(BF16)
+
+
+def widen_own_kernel(xo_ref, own_ref):
+    for r in range(20):
+        widen(xo_ref[r].astype(F32), own_ref, r)
+
+
+def widen_rim_kernel(xp_ref, xn_ref, rim_ref):
     p = lax.axis_index("space")
-    for base, ref, inside in ((0, xp_ref, p > 0), (20, xo_ref, None), (40, xn_ref, p < 7)):
+    for base, ref, inside in ((0, xp_ref, p > 0), (20, xn_ref, p < 7)):
         for r in range(20):
-            v = ref[r].astype(F32)
-            a, b, c = shifted(v if inside is None else jnp.where(inside, v, 0.0))
-            xi_ref[base + r, 0:64] = a.astype(BF16)
-            xi_ref[base + r, 64:128] = b.astype(BF16)
-            xi_ref[base + r, 128:192] = c.astype(BF16)
-
-
-def conv_first_kernel(own_ref, got_ref, xi_ref, slope_ref, xa_ref, zs):
+            widen(jnp.where(inside, ref[r].astype(F32), 0.0), rim_ref, base + r)
+
+
+def input_row(own_ref, rim_ref, layer, height):
+    if 2 <= layer <= 3:
+        return own_ref[(layer - 2) * 10 + height]
+    return rim_ref[(layer if layer < 2 else layer - 2) * 10 + height]
+
+
+def conv_first_kernel(own_ref, got_ref, xo_ref, xr_ref, slope_ref, xa_ref, zs):
     x, zl = split()
     p = lax.axis_index("space")
     own, got = own_ref[:64], got_ref[:64]
@@ -134,7 +157,7 @@
         for j in range(2):
             cols.append(
                 jnp.concatenate(
-                    [xi_ref[(dd + a) * 10 + hh + j + b] for a in range(3) for b in range(3)], axis=0
+                    [input_row(xo_ref, xr_ref, dd + a, hh + j + b) for a in range(3) for b in range(3)], axis=0
                 )
             )
         z = jnp.dot(w1, jnp.concatenate(cols, axis=1), preferred_element_type=F32)
@@ -194,14 +217,13 @@
 
 
 def second_kernel(xa_ref, gs0_ref, gs1_ref, dw_ref):
-    gs = jnp.concatenate([(gs0_ref, gs1_ref)[d][h + 1] for d in range(2) for h in range(4)], axis=1)
+    left = height_taps(lambda d, h: (gs0_ref, gs1_ref)[d][h + 1])
     for a in range(3):
+        col = jnp.concatenate([xa_ref[(d + a) * 8 + h + 1] for d in range(2) for h in range(6)], axis=1)
+        dw = lax.dot_general(left, col, NT, preferred_element_type=F32)
         for b in range(3):
-            col = jnp.concatenate(
-                [xa_ref[(d + a) * 8 + h + 1 + b] for d in range(2) for h in range(4)], axis=1
-            )
             at = (a * 3 + b) * 384
-            dw_ref[:, at : at + 384] = lax.dot_general(gs, col, NT, preferred_element_type=F32)
+            dw_ref[:, at : at + 384] = dw[b * 32 : (b + 1) * 32]
 
 
 def back_kernel(gs0_ref, gs1_ref, gp_ref, gn_ref, w2b_ref, own_ref, s1, s2, s3, g3, acc):
@@ -235,22 +257,22 @@
         out[...] = acc[rows32(xor(zl, k + 1)), :].astype(BF16)
 
 
-def first_kernel(own_ref, r1, r2, r3, slope_ref, xi_ref, dw2_ref, keep_ref, give_ref, acc):
+def first_kernel(own_ref, r1, r2, r3, slope_ref, xo_ref, xr_ref, dw2_ref, keep_ref, give_ref, acc):
     core = lax.rem(lax.axis_index("space"), 2)
     back = (own_ref[...] + r1[...].astype(F32)) + (r2[...].astype(F32) + r3[...].astype(F32))
     gf = (back * slope_ref[...]).astype(BF16)
-    parts = []
-    for a in range(3):
-        col = jnp.concatenate(
-            [
-                jnp.concatenate(
-                    [xi_ref[(d + 1 + a) * 10 + h + 2 + b] for d in range(2) for h in range(4)], axis=1
-                )
-                for b in range(3)
-            ],
-            axis=0,
-        )
-        parts.append(lax.dot_general(gf, col, NT, preferred_element_type=F32))
+    left = height_taps(lambda d, h: gf[:, (d * 4 + h) * W : (d * 4 + h + 1) * W])
+    col = jnp.concatenate(
+        [
+            jnp.concatenate(
+                [input_row(xo_ref, xr_ref, d + 1 + a, h + 2) for d in range(2) for h in range(6)], axis=1
+            )
+            for a in range(3)
+        ],
+        axis=0,
+    )
+    dw = lax.dot_general(left, col, NT, preferred_element_type=F32)
+    parts = [dw[b * 32 : (b + 1) * 32] for b in range(3)]
     acc[:, :K2] = dw2_ref[...]
     acc[:, K2:] = jnp.concatenate(parts + [jnp.zeros((32, 2 * HALF - K2 - K1), F32)], axis=1)
     keep_ref[...] = acc[:, lanes(core)]
@@ -286,8 +308,10 @@
     both = [jnp.where(core == 0, own, got), jnp.where(core == 0, got, own)]
     both = jnp.concatenate(both, axis=1) * (1.0 / 256.0)
     for t in range(27):
+        a, b, c = t // 9, t // 3 % 3, t % 3
+        at = K2 + b * 576 + a * 192 + c * 64
         dw2_ref[t] = both[:, t * W : (t + 1) * W]
-        dw1_ref[t] = both[:, K2 + t * 64 : K2 + (t + 1) * 64]
+        dw1_ref[t] = both[:, at : at + 64]
 
 
 def local(act_in, w_first, w_second, grad_out):
@@ -332,11 +356,12 @@
     )
     half_got = lax.ppermute(half, "space", other)
 
-    (xi,) = run(widen_kernel, [sds((60, 192, W), BF16)], [xo, xp, xn], flops=8 * 10**8)
+    (xw,) = run(widen_own_kernel, [sds((20, 192, W), BF16)], [xo], flops=3 * 10**8)
+    (xr,) = run(widen_rim_kernel, [sds((40, 192, W), BF16)], [xp, xn], flops=6 * 10**8)
     slope, xa = run(
         conv_first_kernel,
         [sds((32, 1024), F32), sds((32, 384, W), BF16)],
-        [half, half_got, xi],
+        [half, half_got, xw, xr],
         [pltpu.VMEM((32, 128, W), F32)],
         4 * 10**9,
     )
@@ -362,7 +387,7 @@
     keep, give = run(
         first_kernel,
         [sds((32, HALF), F32)] * 2,
-        [own] + s + [slope, xi, dw2],
+        [own] + s + [slope, xw, xr, dw2],
         [pltpu.VMEM((32, 2 * HALF), F32)],
     )
     got = lax.ppermute(give, "space", other)

time: 73.9 us -> 73.3 us (level)
  Pallas kernels: 8.7 us -> 7.39 us
  starting transfers between devices: 42.7 us -> 43.8 us
    pallas_call x13 -> x14, Pallas kernels: 8.7 us -> 7.39 us  [run(): pl.pallas_call(kernel, out_shape=outs, in_specs=[VMEM] * len(args), out_s...]
    ppermute x1, starting transfers between devices: 4.63 us -> 5.8 us  [local(): got = lax.ppermute(give, 'space', other)]
  transfers between devices with their start and end apart: 22 -> 22, of which waited for: 14 -> 15; matrix products, arithmetic and copies ran while one was open for 1% -> 1% of each run, Pallas kernels for 4% -> 3%
where the time goes in v4:
time: 73.3 us; the launch traced here: 73.1 us
  starting transfers between devices  43.8 us (60%)
  waiting for transfers between devices  17.6 us (24%)
  Pallas kernels  7.39 us (10%)
  local copies, waits for them, and re-layouts  3.44 us (5%)
  between operations  0.82 us (1%)
    pallas_call x14, Pallas kernels, run(): pl.pallas_call(kernel, out_shape=outs, in_specs=[VMEM] * len(args), out_s...  7.39 us
    ppermute x1, starting transfers between devices, local(): p2 = lax.ppermute(w0, joint, zed(0, 3))  7.07 us
    ppermute x1, starting transfers between devices, local(): got = lax.ppermute(give, 'space', other)  5.8 us
    ppermute x1, starting transfers between devices, local(): lax.ppermute(part, 'sample', [(0, 1), (1, 0)]).astype(F32)  5.07 us
    ppermute x1, starting transfers between devices, local(): got = lax.ppermute(part, 'space', other)  4.75 us
    ppermute x1, starting transfers between devices, local(): gn = lax.ppermute(gs0, 'space', down)  4.35 us
    ppermute x3, starting transfers between devices, local(): b = [b[0]] + [lax.ppermute(b[k], 'filt', X[k]) for k in (1, 2, 3)]  3.95 us
    ppermute x3, starting transfers between devices, local(): s = [lax.ppermute(s[k - 1], 'filt', X[k]) for k in (1, 2, 3)]  3.94 us
  transfers between devices with their start and end apart: 22, of which 15 were waited for; matrix products, arithmetic and copies ran while one was open for 1% of the time, Pallas kernels for 3%

profile of v4, /device:TPU:1, one launch (start us, length us, event | category | flops | bytes accessed | tf_op | source)
XLA Modules:
  0.0 73.1 jit_solution(15498555050244645934)
XLA Ops:
  1.5 7.1 %collective-permute-start.1 = (bf16[8,1792]{1,0:T(8,128)(2,1)S(1)}, bf16[8,1792]{1,0:T(8,128)(2,1)S(1)}, u32[]{:S(2)}, u32[]{:S(2)}) collective-permute-start(bf16[8,1792]{1,0:T(8,128)(2,1)S(1)} %shard_map.67.w0_ref), channel_id=1, source_target_pairs={{0,0},{1,1},{2,2},{3,3},{4,4},{5,5},{6,6},{7,7},{8,8},{9,9},{10,10... | collective-permute-start | bytes 86024 | tf_op jit(solution)/shard_map/ppermute | solution.py:332
  10.4 1.9 %collective-permute-done.p1_ref = bf16[8,1792]{1,0:T(8,128)(2,1)S(1)} collective-permute-done((bf16[8,1792]{1,0:T(8,128)(2,1)S(1)}, bf16[8,1792]{1,0:T(8,128)(2,1)S(1)}, u32[]{:S(2)}, u32[]{:S(2)}) %collective-permute-start) | collective-permute-done | bytes 28704 | tf_op jit(solution)/shard_map/ppermute | solution.py:331
  12.4 1.3 %collective-permute-start.2 = (bf16[8,6912]{1,0:T(8,128)(2,1)S(1)}, bf16[8,6912]{1,0:T(8,128)(2,1)S(1)}, u32[]{:S(2)}, u32[]{:S(2)}) collective-permute-start(bf16[8,6912]{1,0:T(8,128)(2,1)S(1)} %get-tuple-element.64), channel_id=1, source_target_pairs={{0,1},{1,0},{2,3},{3,2},{4,5},{5,4},{6,7},{7,6},{8,9},{9,8},{10,11... | collective-permute-start | bytes 331784 | tf_op jit(solution)/shard_map/ppermute | solution.py:350
  13.7 2.5 %collective-permute-start.3 = (bf16[8,6912]{1,0:T(8,128)(2,1)S(1)}, bf16[8,6912]{1,0:T(8,128)(2,1)S(1)}, u32[]{:S(2)}, u32[]{:S(2)}) collective-permute-start(bf16[8,6912]{1,0:T(8,128)(2,1)S(1)} %get-tuple-element.65), channel_id=1, source_target_pairs={{0,2},{1,3},{2,0},{3,1},{4,6},{5,7},{6,4},{7,5},{8,10},{9,11},{10,... | collective-permute-start | bytes 331784 | tf_op jit(solution)/shard_map/ppermute | solution.py:350
  16.7 1.7 %collective-permute-start.6 = (bf16[20,64,128]{2,1,0:T(8,128)(2,1)S(1)}, bf16[20,64,128]{2,1,0:T(8,128)(2,1)S(1)}, u32[]{:S(2)}, u32[]{:S(2)}) collective-permute-start(bf16[20,64,128]{2,1,0:T(8,128)(2,1)S(1)} %bitcast.14), channel_id=1, source_target_pairs={{0,16},{16,32},{32,48},{48,64},{64,80},{80,96},{96,112},{112,0},{1... | collective-permute-start | bytes 983048 | tf_op jit(solution)/shard_map/ppermute | solution.py:345
  18.4 1.0 %collective-permute-done.3.b2 = bf16[8,6912]{1,0:T(8,128)(2,1)S(1)} collective-permute-done((bf16[8,6912]{1,0:T(8,128)(2,1)S(1)}, bf16[8,6912]{1,0:T(8,128)(2,1)S(1)}, u32[]{:S(2)}, u32[]{:S(2)}) %collective-permute-start.3) | collective-permute-done | bytes 110624 | tf_op jit(solution)/shard_map/ppermute | solution.py:350
  19.4 1.5 %collective-permute-done.4.b3 = bf16[8,6912]{1,0:T(8,128)(2,1)S(1)} collective-permute-done((bf16[8,6912]{1,0:T(8,128)(2,1)S(1)}, bf16[8,6912]{1,0:T(8,128)(2,1)S(1)}, u32[]{:S(2)}, u32[]{:S(2)}) %collective-permute-start.4) | collective-permute-done | bytes 110624 | tf_op jit(solution)/shard_map/ppermute | solution.py:350
  21.4 1.8 %collective-permute-done.7.xn_ref = bf16[20,64,128]{2,1,0:T(8,128)(2,1)S(1)} collective-permute-done((bf16[20,64,128]{2,1,0:T(8,128)(2,1)S(1)}, bf16[20,64,128]{2,1,0:T(8,128)(2,1)S(1)}, u32[]{:S(2)}, u32[]{:S(2)}) %collective-permute-start.7) | collective-permute-done | bytes 327712 | tf_op jit(solution)/shard_map/ppermute | solution.py:346
  23.6 2.3 %shard_map.73 = (f32[32,1024]{1,0:T(8,128)S(1)}, bf16[32,384,128]{2,1,0:T(8,128)(2,1)S(1)}) custom-call(bf16[96,1792]{1,0:T(8,128)(2,1)S(1)} %get-tuple-element.67.own_ref, bf16[96,1792]{1,0:T(8,128)(2,1)S(1)} %collective-permute-done.5.got_ref, bf16[20,192,128]{2,1,0:T(8,128)(2,1)S(1)} %shard_map.71.xo_ref, bf16[40,192,128]{2,1,0:T(8,128)(2,1)S(1)} %shard_map.72.xr_ref), custom_call_target="tpu_custom_call" | custom-call | flops 4000000000 | bytes 100000 | tf_op jit(solution)/shard_map/pallas_call | solution.py:20
  26.8 4.3 %collective-permute-start.9 = (bf16[6,32,128]{2,1,0:T(8,128)(2,1)S(1)}, bf16[6,32,128]{2,1,0:T(8,128)(2,1)S(1)}, u32[]{:S(2)}, u32[]{:S(2)}) collective-permute-start(bf16[6,32,128]{2,1,0:T(8,128)(2,1)S(1)} %get-tuple-element.71.gs0_ref), channel_id=1, source_target_pairs={{16,0},{32,16},{48,32},{64,48},{80,64},{96,80},{112,96},{0,112},{1... | collective-permute-start | bytes 147464 | tf_op jit(solution)/shard_map/ppermute | solution.py:375
  31.1 1.1 %shard_map.76.dw2_ref = f32[32,3456]{1,0:T(8,128)S(1)} custom-call(bf16[32,384,128]{2,1,0:T(8,128)(2,1)S(1)} %get-tuple-element.70.xa_ref, bf16[6,32,128]{2,1,0:T(8,128)(2,1)S(1)} %get-tuple-element.71.gs0_ref, bf16[6,32,128]{2,1,0:T(8,128)(2,1)S(1)} %get-tuple-element.72.gs1_ref), custom_call_target="tpu_custom_call" | custom-call | flops 2500000000 | bytes 100000 | tf_op jit(solution)/shard_map/pallas_call | solution.py:20
  33.0 1.4 %collective-permute-start.11 = (bf16[32,1024]{1,0:T(8,128)(2,1)S(1)}, bf16[32,1024]{1,0:T(8,128)(2,1)S(1)}, u32[]{:S(2)}, u32[]{:S(2)}) collective-permute-start(bf16[32,1024]{1,0:T(8,128)(2,1)S(1)} %get-tuple-element.79), channel_id=1, source_target_pairs={{0,8},{1,9},{2,10},{3,11},{4,12},{5,13},{6,14},{7,15},{8,0},{9,1},... | collective-permute-start | bytes 196616 | tf_op jit(solution)/shard_map/ppermute | solution.py:385
  34.4 2.1 %collective-permute-start.12 = (bf16[32,1024]{1,0:T(8,128)(2,1)S(1)}, bf16[32,1024]{1,0:T(8,128)(2,1)S(1)}, u32[]{:S(2)}, u32[]{:S(2)}) collective-permute-start(bf16[32,1024]{1,0:T(8,128)(2,1)S(1)} %get-tuple-element.80), channel_id=1, source_target_pairs={{0,12},{1,13},{2,14},{3,15},{4,8},{5,9},{6,10},{7,11},{8,4},{9,5},... | collective-permute-start | bytes 196616 | tf_op jit(solution)/shard_map/ppermute | solution.py:385
  37.1 2.2 %collective-permute-done.12.r3 = bf16[32,1024]{1,0:T(8,128)(2,1)S(1)} collective-permute-done((bf16[32,1024]{1,0:T(8,128)(2,1)S(1)}, bf16[32,1024]{1,0:T(8,128)(2,1)S(1)}, u32[]{:S(2)}, u32[]{:S(2)}) %collective-permute-start.12) | collective-permute-done | bytes 65568 | tf_op jit(solution)/shard_map/ppermute | solution.py:385
  40.1 5.8 %collective-permute-start.13 = (f32[32,2688]{1,0:T(8,128)S(1)}, f32[32,2688]{1,0:T(8,128)S(1)}, u32[]{:S(2)}, u32[]{:S(2)}) collective-permute-start(f32[32,2688]{1,0:T(8,128)S(1)} %get-tuple-element.84), channel_id=1, source_target_pairs={{0,16},{16,0},{32,48},{48,32},{64,80},{80,64},{96,112},{112,96},{1... | collective-permute-start | bytes 1032200 | tf_op jit(solution)/shard_map/ppermute | solution.py:393
  45.9 1.3 %collective-permute-done.13.got_ref = f32[32,2688]{1,0:T(8,128)S(1)} collective-permute-done((f32[32,2688]{1,0:T(8,128)S(1)}, f32[32,2688]{1,0:T(8,128)S(1)}, u32[]{:S(2)}, u32[]{:S(2)}) %collective-permute-start.13) | collective-permute-done | bytes 344096 | tf_op jit(solution)/shard_map/ppermute | solution.py:393
  47.4 2.9 %collective-permute-start.15 = (bf16[8,3712]{1,0:T(8,128)(2,1)S(1)}, bf16[8,3712]{1,0:T(8,128)(2,1)S(1)}, u32[]{:S(2)}, u32[]{:S(2)}) collective-permute-start(bf16[8,3712]{1,0:T(8,128)(2,1)S(1)} %get-tuple-element.89), channel_id=1, source_target_pairs={{0,2},{1,3},{2,0},{3,1},{4,6},{5,7},{6,4},{7,5},{8,10},{9,11},{10,... | collective-permute-start | bytes 178184 | tf_op jit(solution)/shard_map/ppermute | solution.py:400
  50.2 1.0 %collective-permute-start.16 = (bf16[8,3712]{1,0:T(8,128)(2,1)S(1)}, bf16[8,3712]{1,0:T(8,128)(2,1)S(1)}, u32[]{:S(2)}, u32[]{:S(2)}) collective-permute-start(bf16[8,3712]{1,0:T(8,128)(2,1)S(1)} %get-tuple-element.90), channel_id=1, source_target_pairs={{0,3},{1,2},{2,1},{3,0},{4,7},{5,6},{6,5},{7,4},{8,11},{9,10},{10,... | collective-permute-start | bytes 178184 | tf_op jit(solution)/shard_map/ppermute | solution.py:400
  51.2 1.7 %collective-permute-done.15.r2 = bf16[8,3712]{1,0:T(8,128)(2,1)S(1)} collective-permute-done((bf16[8,3712]{1,0:T(8,128)(2,1)S(1)}, bf16[8,3712]{1,0:T(8,128)(2,1)S(1)}, u32[]{:S(2)}, u32[]{:S(2)}) %collective-permute-start.15) | collective-permute-done | bytes 59424 | tf_op jit(solution)/shard_map/ppermute | solution.py:400
  52.9 1.6 %collective-permute-done.16.r3 = bf16[8,3712]{1,0:T(8,128)(2,1)S(1)} collective-permute-done((bf16[8,3712]{1,0:T(8,128)(2,1)S(1)}, bf16[8,3712]{1,0:T(8,128)(2,1)S(1)}, u32[]{:S(2)}, u32[]{:S(2)}) %collective-permute-start.16) | collective-permute-done | bytes 59424 | tf_op jit(solution)/shard_map/ppermute | solution.py:400
  55.3 2.6 %collective-permute-start.17 = (bf16[8,2688]{1,0:T(8,128)(2,1)S(1)}, bf16[8,2688]{1,0:T(8,128)(2,1)S(1)}, u32[]{:S(2)}, u32[]{:S(2)}) collective-permute-start(bf16[8,2688]{1,0:T(8,128)(2,1)S(1)} %get-tuple-element.92), channel_id=1, source_target_pairs={{0,32},{16,48},{32,0},{48,16},{64,96},{80,112},{96,64},{112,80},{1... | collective-permute-start | bytes 129032 | tf_op jit(solution)/shard_map/ppermute | solution.py:404
  59.8 5.1 %collective-permute-start.20 = (bf16[8,2688]{1,0:T(8,128)(2,1)S(1)}, bf16[8,2688]{1,0:T(8,128)(2,1)S(1)}, u32[]{:S(2)}, u32[]{:S(2)}) collective-permute-start(bf16[8,2688]{1,0:T(8,128)(2,1)S(1)} %add_convert_fusion), channel_id=1, source_target_pairs={{0,128},{128,0},{1,129},{129,1},{2,130},{130,2},{3,131},{131,3},{4... | collective-permute-start | bytes 129032 | tf_op jit(solution)/shard_map/ppermute | solution.py:407
  64.8 1.8 %collective-permute-done.20 = bf16[8,2688]{1,0:T(8,128)(2,1)S(1)} collective-permute-done((bf16[8,2688]{1,0:T(8,128)(2,1)S(1)}, bf16[8,2688]{1,0:T(8,128)(2,1)S(1)}, u32[]{:S(2)}, u32[]{:S(2)}) %collective-permute-start.20) | collective-permute-done | bytes 43040 | tf_op jit(solution)/shard_map/ppermute | solution.py:407
  66.7 4.7 %collective-permute-start.21 = (f32[8,2688]{1,0:T(8,128)S(1)}, f32[8,2688]{1,0:T(8,128)S(1)}, u32[]{:S(2)}, u32[]{:S(2)}) collective-permute-start(f32[8,2688]{1,0:T(8,128)S(1)} %convert_add_fusion.own_ref), channel_id=1, source_target_pairs={{0,16},{16,0},{32,48},{48,32},{64,80},{80,64},{96,112},{112,96},{1... | collective-permute-start | bytes 258056 | tf_op jit(solution)/shard_map/ppermute | solution.py:408
  (48 shorter events, 11.6 us)
Async XLA Ops:
  1.5 10.8 %collective-permute-start.1 = (bf16[8,1792]{1,0:T(8,128)(2,1)S(1)}, bf16[8,1792]{1,0:T(8,128)(2,1)S(1)}, u32[]{:S(2)}, u32[]{:S(2)}) collective-permute-start(bf16[8,1792]{1,0:T(8,128)(2,1)S(1)} %shard_map.67.w0_ref), channel_id=1, source_target_pairs={{0,0},{1,1},{2,2},{3,3},{4,4},{5,5},{6,6},{7,7},{8,8},{9,9},{10,10... | collective-permute-start | bytes 86024 | tf_op jit(solution)/shard_map/ppermute | solution.py:332
  8.6 3.7 %collective-permute-start = (bf16[8,1792]{1,0:T(8,128)(2,1)S(1)}, bf16[8,1792]{1,0:T(8,128)(2,1)S(1)}, u32[]{:S(2)}, u32[]{:S(2)}) collective-permute-start(bf16[8,1792]{1,0:T(8,128)(2,1)S(1)} %shard_map.67.w0_ref), channel_id=1, source_target_pairs={{0,4},{1,5},{2,6},{3,7},{4,0},{5,1},{6,2},{7,3},{8,12},{9,13},{10,... | collective-permute-start | bytes 86024 | tf_op jit(solution)/shard_map/ppermute | solution.py:331
  8.7 0.8 %copy-start = (bf16[1,8,2,16,128]{4,3,2,1,0:T(8,128)(2,1)S(1)}, bf16[1,8,2,16,128]{4,3,2,1,0:T(8,128)(2,1)}, u32[]{:S(2)}) copy-start(bf16[1,8,2,16,128]{4,3,2,1,0:T(8,128)(2,1)} %param.7) | copy-start | bytes 196612
  10.4 5.9 %copy-start.3 = (bf16[1,64,2,16,128]{4,3,2,1,0:T(8,128)(2,1)S(1)}, bf16[1,64,2,16,128]{4,3,2,1,0:T(8,128)(2,1)}, u32[]{:S(2)}) copy-start(bf16[1,64,2,16,128]{4,3,2,1,0:T(8,128)(2,1)} %param.4) | copy-start | bytes 1572868
  12.4 6.1 %collective-permute-start.2 = (bf16[8,6912]{1,0:T(8,128)(2,1)S(1)}, bf16[8,6912]{1,0:T(8,128)(2,1)S(1)}, u32[]{:S(2)}, u32[]{:S(2)}) collective-permute-start(bf16[8,6912]{1,0:T(8,128)(2,1)S(1)} %get-tuple-element.64), channel_id=1, source_target_pairs={{0,1},{1,0},{2,3},{3,2},{4,5},{5,4},{6,7},{7,6},{8,9},{9,8},{10,11... | collective-permute-start | bytes 331784 | tf_op jit(solution)/shard_map/ppermute | solution.py:350
  13.7 5.8 %collective-permute-start.3 = (bf16[8,6912]{1,0:T(8,128)(2,1)S(1)}, bf16[8,6912]{1,0:T(8,128)(2,1)S(1)}, u32[]{:S(2)}, u32[]{:S(2)}) collective-permute-start(bf16[8,6912]{1,0:T(8,128)(2,1)S(1)} %get-tuple-element.65), channel_id=1, source_target_pairs={{0,2},{1,3},{2,0},{3,1},{4,6},{5,7},{6,4},{7,5},{8,10},{9,11},{10,... | collective-permute-start | bytes 331784 | tf_op jit(solution)/shard_map/ppermute | solution.py:350
  16.1 4.8 %collective-permute-start.4 = (bf16[8,6912]{1,0:T(8,128)(2,1)S(1)}, bf16[8,6912]{1,0:T(8,128)(2,1)S(1)}, u32[]{:S(2)}, u32[]{:S(2)}) collective-permute-start(bf16[8,6912]{1,0:T(8,128)(2,1)S(1)} %get-tuple-element.66), channel_id=1, source_target_pairs={{0,3},{1,2},{2,1},{3,0},{4,7},{5,6},{6,5},{7,4},{8,11},{9,10},{10,... | collective-permute-start | bytes 331784 | tf_op jit(solution)/shard_map/ppermute | solution.py:350
  16.7 6.5 %collective-permute-start.7 = (bf16[20,64,128]{2,1,0:T(8,128)(2,1)S(1)}, bf16[20,64,128]{2,1,0:T(8,128)(2,1)S(1)}, u32[]{:S(2)}, u32[]{:S(2)}) collective-permute-start(bf16[20,64,128]{2,1,0:T(8,128)(2,1)S(1)} %bitcast.13), channel_id=1, source_target_pairs={{16,0},{32,16},{48,32},{64,48},{80,64},{96,80},{112,96},{0,112},{1... | collective-permute-start | bytes 983048 | tf_op jit(solution)/shard_map/ppermute | solution.py:346
  16.7 6.5 %collective-permute-start.6 = (bf16[20,64,128]{2,1,0:T(8,128)(2,1)S(1)}, bf16[20,64,128]{2,1,0:T(8,128)(2,1)S(1)}, u32[]{:S(2)}, u32[]{:S(2)}) collective-permute-start(bf16[20,64,128]{2,1,0:T(8,128)(2,1)S(1)} %bitcast.14), channel_id=1, source_target_pairs={{0,16},{16,32},{32,48},{48,64},{64,80},{80,96},{96,112},{112,0},{1... | collective-permute-start | bytes 983048 | tf_op jit(solution)/shard_map/ppermute | solution.py:345
  21.0 2.6 %collective-permute-start.5 = (bf16[96,1792]{1,0:T(8,128)(2,1)S(1)}, bf16[96,1792]{1,0:T(8,128)(2,1)S(1)}, u32[]{:S(2)}, u32[]{:S(2)}) collective-permute-start(bf16[96,1792]{1,0:T(8,128)(2,1)S(1)} %get-tuple-element.67.own_ref), channel_id=1, source_target_pairs={{0,16},{16,0},{32,48},{48,32},{64,80},{80,64},{96,112},{112,96},{1... | collective-permute-start | bytes 1032200 | tf_op jit(solution)/shard_map/ppermute | solution.py:357
  26.8 5.5 %collective-permute-start.9 = (bf16[6,32,128]{2,1,0:T(8,128)(2,1)S(1)}, bf16[6,32,128]{2,1,0:T(8,128)(2,1)S(1)}, u32[]{:S(2)}, u32[]{:S(2)}) collective-permute-start(bf16[6,32,128]{2,1,0:T(8,128)(2,1)S(1)} %get-tuple-element.71.gs0_ref), channel_id=1, source_target_pairs={{16,0},{32,16},{48,32},{64,48},{80,64},{96,80},{112,96},{0,112},{1... | collective-permute-start | bytes 147464 | tf_op jit(solution)/shard_map/ppermute | solution.py:375
  31.1 1.2 %collective-permute-start.8 = (bf16[6,32,128]{2,1,0:T(8,128)(2,1)S(1)}, bf16[6,32,128]{2,1,0:T(8,128)(2,1)S(1)}, u32[]{:S(2)}, u32[]{:S(2)}) collective-permute-start(bf16[6,32,128]{2,1,0:T(8,128)(2,1)S(1)} %get-tuple-element.72.gs1_ref), channel_id=1, source_target_pairs={{0,16},{16,32},{32,48},{48,64},{64,80},{80,96},{96,112},{112,0},{1... | collective-permute-start | bytes 147464 | tf_op jit(solution)/shard_map/ppermute | solution.py:374
  32.9 3.6 %collective-permute-start.10 = (bf16[32,1024]{1,0:T(8,128)(2,1)S(1)}, bf16[32,1024]{1,0:T(8,128)(2,1)S(1)}, u32[]{:S(2)}, u32[]{:S(2)}) collective-permute-start(bf16[32,1024]{1,0:T(8,128)(2,1)S(1)} %get-tuple-element.78), channel_id=1, source_target_pairs={{0,4},{1,5},{2,6},{3,7},{4,0},{5,1},{6,2},{7,3},{8,12},{9,13},{10,... | collective-permute-start | bytes 196616 | tf_op jit(solution)/shard_map/ppermute | solution.py:385
  33.0 4.1 %collective-permute-start.11 = (bf16[32,1024]{1,0:T(8,128)(2,1)S(1)}, bf16[32,1024]{1,0:T(8,128)(2,1)S(1)}, u32[]{:S(2)}, u32[]{:S(2)}) collective-permute-start(bf16[32,1024]{1,0:T(8,128)(2,1)S(1)} %get-tuple-element.79), channel_id=1, source_target_pairs={{0,8},{1,9},{2,10},{3,11},{4,12},{5,13},{6,14},{7,15},{8,0},{9,1},... | collective-permute-start | bytes 196616 | tf_op jit(solution)/shard_map/ppermute | solution.py:385
  34.4 4.9 %collective-permute-start.12 = (bf16[32,1024]{1,0:T(8,128)(2,1)S(1)}, bf16[32,1024]{1,0:T(8,128)(2,1)S(1)}, u32[]{:S(2)}, u32[]{:S(2)}) collective-permute-start(bf16[32,1024]{1,0:T(8,128)(2,1)S(1)} %get-tuple-element.80), channel_id=1, source_target_pairs={{0,12},{1,13},{2,14},{3,15},{4,8},{5,9},{6,10},{7,11},{8,4},{9,5},... | collective-permute-start | bytes 196616 | tf_op jit(solution)/shard_map/ppermute | solution.py:385
  40.1 7.1 %collective-permute-start.13 = (f32[32,2688]{1,0:T(8,128)S(1)}, f32[32,2688]{1,0:T(8,128)S(1)}, u32[]{:S(2)}, u32[]{:S(2)}) collective-permute-start(f32[32,2688]{1,0:T(8,128)S(1)} %get-tuple-element.84), channel_id=1, source_target_pairs={{0,16},{16,0},{32,48},{48,32},{64,80},{80,64},{96,112},{112,96},{1... | collective-permute-start | bytes 1032200 | tf_op jit(solution)/shard_map/ppermute | solution.py:393
  47.3 4.0 %collective-permute-start.14 = (bf16[8,3712]{1,0:T(8,128)(2,1)S(1)}, bf16[8,3712]{1,0:T(8,128)(2,1)S(1)}, u32[]{:S(2)}, u32[]{:S(2)}) collective-permute-start(bf16[8,3712]{1,0:T(8,128)(2,1)S(1)} %get-tuple-element.88), channel_id=1, source_target_pairs={{0,1},{1,0},{2,3},{3,2},{4,5},{5,4},{6,7},{7,6},{8,9},{9,8},{10,11... | collective-permute-start | bytes 178184 | tf_op jit(solution)/shard_map/ppermute | solution.py:400
  47.4 5.5 %collective-permute-start.15 = (bf16[8,3712]{1,0:T(8,128)(2,1)S(1)}, bf16[8,3712]{1,0:T(8,128)(2,1)S(1)}, u32[]{:S(2)}, u32[]{:S(2)}) collective-permute-start(bf16[8,3712]{1,0:T(8,128)(2,1)S(1)} %get-tuple-element.89), channel_id=1, source_target_pairs={{0,2},{1,3},{2,0},{3,1},{4,6},{5,7},{6,4},{7,5},{8,10},{9,11},{10,... | collective-permute-start | bytes 178184 | tf_op jit(solution)/shard_map/ppermute | solution.py:400
  50.2 4.3 %collective-permute-start.16 = (bf16[8,3712]{1,0:T(8,128)(2,1)S(1)}, bf16[8,3712]{1,0:T(8,128)(2,1)S(1)}, u32[]{:S(2)}, u32[]{:S(2)}) collective-permute-start(bf16[8,3712]{1,0:T(8,128)(2,1)S(1)} %get-tuple-element.90), channel_id=1, source_target_pairs={{0,3},{1,2},{2,1},{3,0},{4,7},{5,6},{6,5},{7,4},{8,11},{9,10},{10,... | collective-permute-start | bytes 178184 | tf_op jit(solution)/shard_map/ppermute | solution.py:400
  54.5 4.2 %collective-permute-start.19 = (bf16[8,2688]{1,0:T(8,128)(2,1)S(1)}, bf16[8,2688]{1,0:T(8,128)(2,1)S(1)}, u32[]{:S(2)}, u32[]{:S(2)}) collective-permute-start(bf16[8,2688]{1,0:T(8,128)(2,1)S(1)} %get-tuple-element.92), channel_id=1, source_target_pairs={{0,96},{16,112},{32,64},{48,80},{64,32},{80,48},{96,0},{112,16},{1... | collective-permute-start | bytes 129032 | tf_op jit(solution)/shard_map/ppermute | solution.py:404
  54.6 4.5 %collective-permute-start.18 = (bf16[8,2688]{1,0:T(8,128)(2,1)S(1)}, bf16[8,2688]{1,0:T(8,128)(2,1)S(1)}, u32[]{:S(2)}, u32[]{:S(2)}) collective-permute-start(bf16[8,2688]{1,0:T(8,128)(2,1)S(1)} %get-tuple-element.92), channel_id=1, source_target_pairs={{0,64},{16,80},{32,96},{48,112},{64,0},{80,16},{96,32},{112,48},{1... | collective-permute-start | bytes 129032 | tf_op jit(solution)/shard_map/ppermute | solution.py:404
  55.3 4.5 %collective-permute-start.17 = (bf16[8,2688]{1,0:T(8,128)(2,1)S(1)}, bf16[8,2688]{1,0:T(8,128)(2,1)S(1)}, u32[]{:S(2)}, u32[]{:S(2)}) collective-permute-start(bf16[8,2688]{1,0:T(8,128)(2,1)S(1)} %get-tuple-element.92), channel_id=1, source_target_pairs={{0,32},{16,48},{32,0},{48,16},{64,96},{80,112},{96,64},{112,80},{1... | collective-permute-start | bytes 129032 | tf_op jit(solution)/shard_map/ppermute | solution.py:404
  59.8 6.9 %collective-permute-start.20 = (bf16[8,2688]{1,0:T(8,128)(2,1)S(1)}, bf16[8,2688]{1,0:T(8,128)(2,1)S(1)}, u32[]{:S(2)}, u32[]{:S(2)}) collective-permute-start(bf16[8,2688]{1,0:T(8,128)(2,1)S(1)} %add_convert_fusion), channel_id=1, source_target_pairs={{0,128},{128,0},{1,129},{129,1},{2,130},{130,2},{3,131},{131,3},{4... | collective-permute-start | bytes 129032 | tf_op jit(solution)/shard_map/ppermute | solution.py:407
  66.7 5.7 %collective-permute-start.21 = (f32[8,2688]{1,0:T(8,128)S(1)}, f32[8,2688]{1,0:T(8,128)S(1)}, u32[]{:S(2)}, u32[]{:S(2)}) collective-permute-start(f32[8,2688]{1,0:T(8,128)S(1)} %convert_add_fusion.own_ref), channel_id=1, source_target_pairs={{0,16},{16,0},{32,48},{48,32},{64,80},{80,64},{96,112},{112,96},{1... | collective-permute-start | bytes 258056 | tf_op jit(solution)/shard_map/ppermute | solution.py:408
  (2 other events, 1.6 us)

commit v5 on v4

--- a/solution.py
+++ b/solution.py
@@ -131,11 +131,13 @@
         widen(xo_ref[r].astype(F32), own_ref, r)
 
 
-def widen_rim_kernel(xp_ref, xn_ref, rim_ref):
+def widen_rim_kernel(chip_ref, next_ref, rim_ref):
     p = lax.axis_index("space")
-    for base, ref, inside in ((0, xp_ref, p > 0), (20, xn_ref, p < 7)):
-        for r in range(20):
-            widen(jnp.where(inside, ref[r].astype(F32), 0.0), rim_ref, base + r)
+    first = lax.rem(p, 2) == 0
+    for r in range(20):
+        chip, far = chip_ref[r].astype(F32), next_ref[r].astype(F32)
+        widen(jnp.where(p > 0, jnp.where(first, far, chip), 0.0), rim_ref, r)
+        widen(jnp.where(p < 7, jnp.where(first, chip, far), 0.0), rim_ref, 20 + r)
 
 
 def input_row(own_ref, rim_ref, layer, height):
@@ -181,7 +183,9 @@
             slope_ref[:, (d * 4 + h) * W : (d * 4 + h + 1) * W] = q * (1.0 + v * (1.0 - q))
 
 
-def conv_second_kernel(own_ref, got_ref, go_ref, xa_ref, y_ref, gs0_ref, gs1_ref, w2b_ref, acc, w2_ref):
+def conv_second_kernel(
+    own_ref, got_ref, go_ref, xa_ref, y_ref, gs0_ref, gs1_ref, chip_ref, next_ref, w2b_ref, acc, w2_ref
+):
     first = lax.rem(lax.axis_index("space"), 2) == 0
     own, got = own_ref[64:], got_ref[64:]
     w2_ref[:, : 14 * W] = jnp.where(first, own, got)
@@ -214,6 +218,9 @@
             g = go_ref[:, (d * 6 + hh) * W : (d * 6 + hh + 1) * W].astype(F32)
             gs = (g * (q * (1.0 + v * (1.0 - q)))).astype(BF16)
             (gs0_ref if d == 0 else gs1_ref)[hh] = gs
+    for hh in range(6):
+        chip_ref[hh] = jnp.where(first, gs1_ref[hh], gs0_ref[hh])
+        next_ref[hh] = jnp.where(first, gs0_ref[hh], gs1_ref[hh])
 
 
 def second_kernel(xa_ref, gs0_ref, gs1_ref, dw_ref):
@@ -226,14 +233,21 @@
             dw_ref[:, at : at + 384] = dw[b * 32 : (b + 1) * 32]
 
 
-def back_kernel(gs0_ref, gs1_ref, gp_ref, gn_ref, w2b_ref, own_ref, s1, s2, s3, g3, acc):
+def back_kernel(gs0_ref, gs1_ref, chip_ref, next_ref, w2b_ref, own_ref, s1, s2, s3, g3, acc):
     _, zl = split()
     p = lax.axis_index("space")
-    sides = ((gp_ref, p > 0), (gs0_ref, None), (gs1_ref, None), (gn_ref, p < 7))
-    for d, (ref, inside) in enumerate(sides):
+    first = lax.rem(p, 2) == 0
+    for d in range(4):
         for h in range(6):
-            v = ref[h].astype(F32)
-            before, mid, after = shifted(v if inside is None else jnp.where(inside, v, 0.0))
+            if d == 0:
+                v = jnp.where(first, next_ref[h].astype(F32), chip_ref[h].astype(F32))
+                v = jnp.where(p > 0, v, 0.0)
+            elif d == 3:
+                v = jnp.where(first, chip_ref[h].astype(F32), next_ref[h].astype(F32))
+                v = jnp.where(p < 7, v, 0.0)
+            else:
+                v = (gs0_ref, gs1_ref)[d - 1][h].astype(F32)
+            before, mid, after = shifted(v)
             g3[d * 6 + h, 0:32] = after.astype(BF16)
             g3[d * 6 + h, 32:64] = mid.astype(BF16)
             g3[d * 6 + h, 64:96] = before.astype(BF16)
@@ -317,8 +331,7 @@
 def local(act_in, w_first, w_second, grad_out):
     X = [[(z * 4 + x, z * 4 + (x ^ k)) for z in range(4) for x in range(4)] for k in range(4)]
     Z = [[(z * 4 + x, (z ^ k) * 4 + x) for z in range(4) for x in range(4)] for k in range(4)]
-    up = [(i, (i + 1) % 8) for i in range(8)]
-    down = [((i + 1) % 8, i) for i in range(8)]
+    across = [(i, (i + 1) % 8 if i % 2 else (i + 7) % 8) for i in range(8)]
     other = [(i, i ^ 1) for i in range(8)]
     x = lax.rem(lax.axis_index("filt"), 4)
 
@@ -342,8 +355,8 @@
         [pltpu.VMEM((2, 18, 8, W), F32), pltpu.VMEM((8, K2), F32)],
         10**9,
     )
-    xp = lax.ppermute(xo, "space", up)
-    xn = lax.ppermute(xo, "space", down)
+    xchip = lax.ppermute(xo, "space", other)
+    xnext = lax.ppermute(xo, "space", across)
 
     a, p1, p2 = lax.optimization_barrier((a, p1, p2))
     b = run(pack_kernel, [sds((8, 3 * K1P + 12 * W), BF16)] * 4, [w0, p1, p2] + list(a))
@@ -357,7 +370,7 @@
     half_got = lax.ppermute(half, "space", other)
 
     (xw,) = run(widen_own_kernel, [sds((20, 192, W), BF16)], [xo], flops=3 * 10**8)
-    (xr,) = run(widen_rim_kernel, [sds((40, 192, W), BF16)], [xp, xn], flops=6 * 10**8)
+    (xr,) = run(widen_rim_kernel, [sds((40, 192, W), BF16)], [xchip, xnext], flops=6 * 10**8)
     slope, xa = run(
         conv_first_kernel,
         [sds((32, 1024), F32), sds((32, 384, W), BF16)],
@@ -365,20 +378,20 @@
         [pltpu.VMEM((32, 128, W), F32)],
         4 * 10**9,
     )
-    y, gs0, gs1, w2b = run(
+    y, gs0, gs1, gchip, gnext, w2b = run(
         conv_second_kernel,
-        [sds((32, 1024), BF16), sds((6, 32, W), BF16), sds((6, 32, W), BF16), sds((128, KB), BF16)],
+        [sds((32, 1024), BF16)] + [sds((6, 32, W), BF16)] * 4 + [sds((128, KB), BF16)],
         [half, half_got, go, xa],
         [pltpu.VMEM((32, K2), F32), pltpu.VMEM((32, K2), BF16)],
     )
-    gp = lax.ppermute(gs1, "space", up)
-    gn = lax.ppermute(gs0, "space", down)
+    gchip = lax.ppermute(gchip, "space", other)
+    gnext = lax.ppermute(gnext, "space", across)
     (dw2,) = run(second_kernel, [sds((32, K2), F32)], [xa, gs0, gs1], flops=25 * 10**8)
 
     own, *s = run(
         back_kernel,
         [sds((32, 1024), F32)] + [sds((32, 1024), BF16)] * 3,
-        [gs0, gs1, gp, gn, w2b],
+        [gs0, gs1, gchip, gnext, w2b],
         [pltpu.VMEM((24, 96, W), BF16), pltpu.VMEM((128, 1024), F32)],
     )
     s, dw2 = lax.optimization_barrier((s, dw2))

time: 73.3 us -> 72.8 us (level)
  starting transfers between devices: 43.8 us -> 39.2 us
  waiting for transfers between devices: 17.6 us -> 21.6 us
    ppermute x1, starting transfers between devices: 5.8 us -> 2.77 us  [local(): got = lax.ppermute(give, 'space', other)]
    ppermute x4, waiting for transfers between devices: 1.88 us -> 3.94 us  [the longest x1 2.07 us: local(): gnext = lax.ppermute(gnext, 'space', across)]
    ppermute x3, waiting for transfers between devices: 1.87 us -> 3.7 us  [local(): lax.ppermute(part, 'space', [(i, i ^ 2 * k) for i in range(8)])]
    ppermute x4, starting transfers between devices: 6.1 us -> 4.69 us  [the longest x1 3.12 us: local(): xchip = lax.ppermute(xo, 'space', other)]
    ppermute x3, waiting for transfers between devices: 2.5 us -> 1.34 us  [local(): b = [b[0]] + [lax.ppermute(b[k], 'filt', X[k]) for k in (1, 2, 3)]]
    ppermute x3, waiting for transfers between devices: 2.8 us -> 3.81 us  [local(): s = [lax.ppermute(s[k - 1], 'filt', Z[k]) for k in (1, 2, 3)]]
  transfers between devices with their start and end apart: 22 -> 22, of which waited for: 15 -> 13; matrix products, arithmetic and copies ran while one was open for 1% -> 1% of each run, Pallas kernels for 3% -> 3%
where the time goes in v5:
time: 72.8 us; the launch traced here: 72.6 us
  starting transfers between devices  39.2 us (54%)
  waiting for transfers between devices  21.6 us (30%)
  Pallas kernels  7.43 us (10%)
  local copies, waits for them, and re-layouts  3.44 us (5%)
  between operations  0.81 us (1%)
    pallas_call x14, Pallas kernels, run(): pl.pallas_call(kernel, out_shape=outs, in_specs=[VMEM] * len(args), out_s...  7.43 us
    ppermute x1, starting transfers between devices, local(): p2 = lax.ppermute(w0, joint, zed(0, 3))  7.07 us
    ppermute x1, starting transfers between devices, local(): got = lax.ppermute(part, 'space', other)  4.88 us
    ppermute x1, starting transfers between devices, local(): lax.ppermute(part, 'sample', [(0, 1), (1, 0)]).astype(F32)  4.58 us
    ppermute x3, starting transfers between devices, local(): b = [b[0]] + [lax.ppermute(b[k], 'filt', X[k]) for k in (1, 2, 3)]  3.95 us
    ppermute x3, starting transfers between devices, local(): s = [lax.ppermute(s[k - 1], 'filt', X[k]) for k in (1, 2, 3)]  3.94 us
    ppermute x3, waiting for transfers between devices, local(): s = [lax.ppermute(s[k - 1], 'filt', Z[k]) for k in (1, 2, 3)]  3.81 us
    ppermute x3, waiting for transfers between devices, local(): lax.ppermute(part, 'space', [(i, i ^ 2 * k) for i in range(8)])  3.7 us
  transfers between devices with their start and end apart: 22, of which 13 were waited for; matrix products, arithmetic and copies ran while one was open for 1% of the time, Pallas kernels for 3%

profile of v5, /device:TPU:1, one launch (start us, length us, event | category | flops | bytes accessed | tf_op | source)
XLA Modules:
  0.0 72.6 jit_solution(7124321239149392605)
XLA Ops:
  1.5 7.1 %collective-permute-start.1 = (bf16[8,1792]{1,0:T(8,128)(2,1)S(1)}, bf16[8,1792]{1,0:T(8,128)(2,1)S(1)}, u32[]{:S(2)}, u32[]{:S(2)}) collective-permute-start(bf16[8,1792]{1,0:T(8,128)(2,1)S(1)} %shard_map.67.w0_ref), channel_id=1, source_target_pairs={{0,0},{1,1},{2,2},{3,3},{4,4},{5,5},{6,6},{7,7},{8,8},{9,9},{10,10... | collective-permute-start | bytes 86024 | tf_op jit(solution)/shard_map/ppermute | solution.py:345
  10.4 1.9 %collective-permute-done.p1_ref = bf16[8,1792]{1,0:T(8,128)(2,1)S(1)} collective-permute-done((bf16[8,1792]{1,0:T(8,128)(2,1)S(1)}, bf16[8,1792]{1,0:T(8,128)(2,1)S(1)}, u32[]{:S(2)}, u32[]{:S(2)}) %collective-permute-start) | collective-permute-done | bytes 28704 | tf_op jit(solution)/shard_map/ppermute | solution.py:344
  12.4 1.3 %collective-permute-start.2 = (bf16[8,6912]{1,0:T(8,128)(2,1)S(1)}, bf16[8,6912]{1,0:T(8,128)(2,1)S(1)}, u32[]{:S(2)}, u32[]{:S(2)}) collective-permute-start(bf16[8,6912]{1,0:T(8,128)(2,1)S(1)} %get-tuple-element.66), channel_id=1, source_target_pairs={{0,1},{1,0},{2,3},{3,2},{4,5},{5,4},{6,7},{7,6},{8,9},{9,8},{10,11... | collective-permute-start | bytes 331784 | tf_op jit(solution)/shard_map/ppermute | solution.py:363
  13.7 2.5 %collective-permute-start.3 = (bf16[8,6912]{1,0:T(8,128)(2,1)S(1)}, bf16[8,6912]{1,0:T(8,128)(2,1)S(1)}, u32[]{:S(2)}, u32[]{:S(2)}) collective-permute-start(bf16[8,6912]{1,0:T(8,128)(2,1)S(1)} %get-tuple-element.67), channel_id=1, source_target_pairs={{0,2},{1,3},{2,0},{3,1},{4,6},{5,7},{6,4},{7,5},{8,10},{9,11},{10,... | collective-permute-start | bytes 331784 | tf_op jit(solution)/shard_map/ppermute | solution.py:363
  16.8 3.1 %collective-permute-start.6 = (bf16[20,64,128]{2,1,0:T(8,128)(2,1)S(1)}, bf16[20,64,128]{2,1,0:T(8,128)(2,1)S(1)}, u32[]{:S(2)}, u32[]{:S(2)}) collective-permute-start(bf16[20,64,128]{2,1,0:T(8,128)(2,1)S(1)} %bitcast.14), channel_id=1, source_target_pairs={{0,16},{16,0},{32,48},{48,32},{64,80},{80,64},{96,112},{112,96},{1... | collective-permute-start | bytes 983048 | tf_op jit(solution)/shard_map/ppermute | solution.py:358
  19.9 1.3 %collective-permute-done.4.b3 = bf16[8,6912]{1,0:T(8,128)(2,1)S(1)} collective-permute-done((bf16[8,6912]{1,0:T(8,128)(2,1)S(1)}, bf16[8,6912]{1,0:T(8,128)(2,1)S(1)}, u32[]{:S(2)}, u32[]{:S(2)}) %collective-permute-start.4) | collective-permute-done | bytes 110624 | tf_op jit(solution)/shard_map/ppermute | solution.py:363
  21.7 1.9 %collective-permute-done.7.next_ref = bf16[20,64,128]{2,1,0:T(8,128)(2,1)S(1)} collective-permute-done((bf16[20,64,128]{2,1,0:T(8,128)(2,1)S(1)}, bf16[20,64,128]{2,1,0:T(8,128)(2,1)S(1)}, u32[]{:S(2)}, u32[]{:S(2)}) %collective-permute-start.7) | collective-permute-done | bytes 327712 | tf_op jit(solution)/shard_map/ppermute | solution.py:359
  24.0 2.3 %shard_map.73 = (f32[32,1024]{1,0:T(8,128)S(1)}, bf16[32,384,128]{2,1,0:T(8,128)(2,1)S(1)}) custom-call(bf16[96,1792]{1,0:T(8,128)(2,1)S(1)} %get-tuple-element.69.own_ref, bf16[96,1792]{1,0:T(8,128)(2,1)S(1)} %collective-permute-done.5.got_ref, bf16[20,192,128]{2,1,0:T(8,128)(2,1)S(1)} %shard_map.71.xo_ref, bf16[40,192,128]{2,1,0:T(8,128)(2,1)S(1)} %shard_map.72.xr_ref), custom_call_target="tpu_custom_call" | custom-call | flops 4000000000 | bytes 100000 | tf_op jit(solution)/shard_map/pallas_call | solution.py:20
  27.2 1.2 %collective-permute-start.8 = (bf16[6,32,128]{2,1,0:T(8,128)(2,1)S(1)}, bf16[6,32,128]{2,1,0:T(8,128)(2,1)S(1)}, u32[]{:S(2)}, u32[]{:S(2)}) collective-permute-start(bf16[6,32,128]{2,1,0:T(8,128)(2,1)S(1)} %get-tuple-element.75), channel_id=1, source_target_pairs={{0,16},{16,0},{32,48},{48,32},{64,80},{80,64},{96,112},{112,96},{1... | collective-permute-start | bytes 147464 | tf_op jit(solution)/shard_map/ppermute | solution.py:387
  29.8 2.1 %collective-permute-done.9.next_ref = bf16[6,32,128]{2,1,0:T(8,128)(2,1)S(1)} collective-permute-done((bf16[6,32,128]{2,1,0:T(8,128)(2,1)S(1)}, bf16[6,32,128]{2,1,0:T(8,128)(2,1)S(1)}, u32[]{:S(2)}, u32[]{:S(2)}) %collective-permute-start.9) | collective-permute-done | bytes 49184 | tf_op jit(solution)/shard_map/ppermute | solution.py:388
  32.5 2.0 %collective-permute-start.11 = (bf16[32,1024]{1,0:T(8,128)(2,1)S(1)}, bf16[32,1024]{1,0:T(8,128)(2,1)S(1)}, u32[]{:S(2)}, u32[]{:S(2)}) collective-permute-start(bf16[32,1024]{1,0:T(8,128)(2,1)S(1)} %get-tuple-element.83), channel_id=1, source_target_pairs={{0,8},{1,9},{2,10},{3,11},{4,12},{5,13},{6,14},{7,15},{8,0},{9,1},... | collective-permute-start | bytes 196616 | tf_op jit(solution)/shard_map/ppermute | solution.py:398
  34.6 1.5 %collective-permute-start.12 = (bf16[32,1024]{1,0:T(8,128)(2,1)S(1)}, bf16[32,1024]{1,0:T(8,128)(2,1)S(1)}, u32[]{:S(2)}, u32[]{:S(2)}) collective-permute-start(bf16[32,1024]{1,0:T(8,128)(2,1)S(1)} %get-tuple-element.84), channel_id=1, source_target_pairs={{0,12},{1,13},{2,14},{3,15},{4,8},{5,9},{6,10},{7,11},{8,4},{9,5},... | collective-permute-start | bytes 196616 | tf_op jit(solution)/shard_map/ppermute | solution.py:398
  36.7 3.2 %collective-permute-done.12.r3 = bf16[32,1024]{1,0:T(8,128)(2,1)S(1)} collective-permute-done((bf16[32,1024]{1,0:T(8,128)(2,1)S(1)}, bf16[32,1024]{1,0:T(8,128)(2,1)S(1)}, u32[]{:S(2)}, u32[]{:S(2)}) %collective-permute-start.12) | collective-permute-done | bytes 65568 | tf_op jit(solution)/shard_map/ppermute | solution.py:398
  40.7 2.8 %collective-permute-start.13 = (f32[32,2688]{1,0:T(8,128)S(1)}, f32[32,2688]{1,0:T(8,128)S(1)}, u32[]{:S(2)}, u32[]{:S(2)}) collective-permute-start(f32[32,2688]{1,0:T(8,128)S(1)} %get-tuple-element.88), channel_id=1, source_target_pairs={{0,16},{16,0},{32,48},{48,32},{64,80},{80,64},{96,112},{112,96},{1... | collective-permute-start | bytes 1032200 | tf_op jit(solution)/shard_map/ppermute | solution.py:406
  43.4 1.3 %collective-permute-done.13.got_ref = f32[32,2688]{1,0:T(8,128)S(1)} collective-permute-done((f32[32,2688]{1,0:T(8,128)S(1)}, f32[32,2688]{1,0:T(8,128)S(1)}, u32[]{:S(2)}, u32[]{:S(2)}) %collective-permute-start.13) | collective-permute-done | bytes 344096 | tf_op jit(solution)/shard_map/ppermute | solution.py:406
  44.9 2.6 %collective-permute-start.15 = (bf16[8,3712]{1,0:T(8,128)(2,1)S(1)}, bf16[8,3712]{1,0:T(8,128)(2,1)S(1)}, u32[]{:S(2)}, u32[]{:S(2)}) collective-permute-start(bf16[8,3712]{1,0:T(8,128)(2,1)S(1)} %get-tuple-element.93), channel_id=1, source_target_pairs={{0,2},{1,3},{2,0},{3,1},{4,6},{5,7},{6,4},{7,5},{8,10},{9,11},{10,... | collective-permute-start | bytes 178184 | tf_op jit(solution)/shard_map/ppermute | solution.py:413
  47.5 1.2 %collective-permute-start.16 = (bf16[8,3712]{1,0:T(8,128)(2,1)S(1)}, bf16[8,3712]{1,0:T(8,128)(2,1)S(1)}, u32[]{:S(2)}, u32[]{:S(2)}) collective-permute-start(bf16[8,3712]{1,0:T(8,128)(2,1)S(1)} %get-tuple-element.94), channel_id=1, source_target_pairs={{0,3},{1,2},{2,1},{3,0},{4,7},{5,6},{6,5},{7,4},{8,11},{9,10},{10,... | collective-permute-start | bytes 178184 | tf_op jit(solution)/shard_map/ppermute | solution.py:413
  48.7 1.5 %collective-permute-done.15.r2 = bf16[8,3712]{1,0:T(8,128)(2,1)S(1)} collective-permute-done((bf16[8,3712]{1,0:T(8,128)(2,1)S(1)}, bf16[8,3712]{1,0:T(8,128)(2,1)S(1)}, u32[]{:S(2)}, u32[]{:S(2)}) %collective-permute-start.15) | collective-permute-done | bytes 59424 | tf_op jit(solution)/shard_map/ppermute | solution.py:413
  50.2 1.6 %collective-permute-done.16.r3 = bf16[8,3712]{1,0:T(8,128)(2,1)S(1)} collective-permute-done((bf16[8,3712]{1,0:T(8,128)(2,1)S(1)}, bf16[8,3712]{1,0:T(8,128)(2,1)S(1)}, u32[]{:S(2)}, u32[]{:S(2)}) %collective-permute-start.16) | collective-permute-done | bytes 59424 | tf_op jit(solution)/shard_map/ppermute | solution.py:413
  51.8 2.9 %collective-permute-start.19 = (bf16[8,2688]{1,0:T(8,128)(2,1)S(1)}, bf16[8,2688]{1,0:T(8,128)(2,1)S(1)}, u32[]{:S(2)}, u32[]{:S(2)}) collective-permute-start(bf16[8,2688]{1,0:T(8,128)(2,1)S(1)} %get-tuple-element.96), channel_id=1, source_target_pairs={{0,96},{16,112},{32,64},{48,80},{64,32},{80,48},{96,0},{112,16},{1... | collective-permute-start | bytes 129032 | tf_op jit(solution)/shard_map/ppermute | solution.py:417
  56.1 3.0 %collective-permute-done.18 = bf16[8,2688]{1,0:T(8,128)(2,1)S(1)} collective-permute-done((bf16[8,2688]{1,0:T(8,128)(2,1)S(1)}, bf16[8,2688]{1,0:T(8,128)(2,1)S(1)}, u32[]{:S(2)}, u32[]{:S(2)}) %collective-permute-start.18) | collective-permute-done | bytes 43040 | tf_op jit(solution)/shard_map/ppermute | solution.py:417
  59.1 4.6 %collective-permute-start.20 = (bf16[8,2688]{1,0:T(8,128)(2,1)S(1)}, bf16[8,2688]{1,0:T(8,128)(2,1)S(1)}, u32[]{:S(2)}, u32[]{:S(2)}) collective-permute-start(bf16[8,2688]{1,0:T(8,128)(2,1)S(1)} %add_convert_fusion), channel_id=1, source_target_pairs={{0,128},{128,0},{1,129},{129,1},{2,130},{130,2},{3,131},{131,3},{4... | collective-permute-start | bytes 129032 | tf_op jit(solution)/shard_map/ppermute | solution.py:420
  63.7 2.3 %collective-permute-done.20 = bf16[8,2688]{1,0:T(8,128)(2,1)S(1)} collective-permute-done((bf16[8,2688]{1,0:T(8,128)(2,1)S(1)}, bf16[8,2688]{1,0:T(8,128)(2,1)S(1)}, u32[]{:S(2)}, u32[]{:S(2)}) %collective-permute-start.20) | collective-permute-done | bytes 43040 | tf_op jit(solution)/shard_map/ppermute | solution.py:420
  66.0 4.9 %collective-permute-start.21 = (f32[8,2688]{1,0:T(8,128)S(1)}, f32[8,2688]{1,0:T(8,128)S(1)}, u32[]{:S(2)}, u32[]{:S(2)}) collective-permute-start(f32[8,2688]{1,0:T(8,128)S(1)} %convert_add_fusion.own_ref), channel_id=1, source_target_pairs={{0,16},{16,0},{32,48},{48,32},{64,80},{80,64},{96,112},{112,96},{1... | collective-permute-start | bytes 258056 | tf_op jit(solution)/shard_map/ppermute | solution.py:421
  (48 shorter events, 11.9 us)
Async XLA Ops:
  1.5 10.8 %collective-permute-start.1 = (bf16[8,1792]{1,0:T(8,128)(2,1)S(1)}, bf16[8,1792]{1,0:T(8,128)(2,1)S(1)}, u32[]{:S(2)}, u32[]{:S(2)}) collective-permute-start(bf16[8,1792]{1,0:T(8,128)(2,1)S(1)} %shard_map.67.w0_ref), channel_id=1, source_target_pairs={{0,0},{1,1},{2,2},{3,3},{4,4},{5,5},{6,6},{7,7},{8,8},{9,9},{10,10... | collective-permute-start | bytes 86024 | tf_op jit(solution)/shard_map/ppermute | solution.py:345
  8.6 3.7 %collective-permute-start = (bf16[8,1792]{1,0:T(8,128)(2,1)S(1)}, bf16[8,1792]{1,0:T(8,128)(2,1)S(1)}, u32[]{:S(2)}, u32[]{:S(2)}) collective-permute-start(bf16[8,1792]{1,0:T(8,128)(2,1)S(1)} %shard_map.67.w0_ref), channel_id=1, source_target_pairs={{0,4},{1,5},{2,6},{3,7},{4,0},{5,1},{6,2},{7,3},{8,12},{9,13},{10,... | collective-permute-start | bytes 86024 | tf_op jit(solution)/shard_map/ppermute | solution.py:344
  8.7 0.8 %copy-start = (bf16[1,8,2,16,128]{4,3,2,1,0:T(8,128)(2,1)S(1)}, bf16[1,8,2,16,128]{4,3,2,1,0:T(8,128)(2,1)}, u32[]{:S(2)}) copy-start(bf16[1,8,2,16,128]{4,3,2,1,0:T(8,128)(2,1)} %param.7) | copy-start | bytes 196612
  10.4 5.9 %copy-start.3 = (bf16[1,64,2,16,128]{4,3,2,1,0:T(8,128)(2,1)S(1)}, bf16[1,64,2,16,128]{4,3,2,1,0:T(8,128)(2,1)}, u32[]{:S(2)}) copy-start(bf16[1,64,2,16,128]{4,3,2,1,0:T(8,128)(2,1)} %param.4) | copy-start | bytes 1572868
  12.4 7.5 %collective-permute-start.2 = (bf16[8,6912]{1,0:T(8,128)(2,1)S(1)}, bf16[8,6912]{1,0:T(8,128)(2,1)S(1)}, u32[]{:S(2)}, u32[]{:S(2)}) collective-permute-start(bf16[8,6912]{1,0:T(8,128)(2,1)S(1)} %get-tuple-element.66), channel_id=1, source_target_pairs={{0,1},{1,0},{2,3},{3,2},{4,5},{5,4},{6,7},{7,6},{8,9},{9,8},{10,11... | collective-permute-start | bytes 331784 | tf_op jit(solution)/shard_map/ppermute | solution.py:363
  13.7 6.2 %collective-permute-start.3 = (bf16[8,6912]{1,0:T(8,128)(2,1)S(1)}, bf16[8,6912]{1,0:T(8,128)(2,1)S(1)}, u32[]{:S(2)}, u32[]{:S(2)}) collective-permute-start(bf16[8,6912]{1,0:T(8,128)(2,1)S(1)} %get-tuple-element.67), channel_id=1, source_target_pairs={{0,2},{1,3},{2,0},{3,1},{4,6},{5,7},{6,4},{7,5},{8,10},{9,11},{10,... | collective-permute-start | bytes 331784 | tf_op jit(solution)/shard_map/ppermute | solution.py:363
  16.1 5.1 %collective-permute-start.4 = (bf16[8,6912]{1,0:T(8,128)(2,1)S(1)}, bf16[8,6912]{1,0:T(8,128)(2,1)S(1)}, u32[]{:S(2)}, u32[]{:S(2)}) collective-permute-start(bf16[8,6912]{1,0:T(8,128)(2,1)S(1)} %get-tuple-element.68), channel_id=1, source_target_pairs={{0,3},{1,2},{2,1},{3,0},{4,7},{5,6},{6,5},{7,4},{8,11},{9,10},{10,... | collective-permute-start | bytes 331784 | tf_op jit(solution)/shard_map/ppermute | solution.py:363
  16.7 6.9 %collective-permute-start.7 = (bf16[20,64,128]{2,1,0:T(8,128)(2,1)S(1)}, bf16[20,64,128]{2,1,0:T(8,128)(2,1)S(1)}, u32[]{:S(2)}, u32[]{:S(2)}) collective-permute-start(bf16[20,64,128]{2,1,0:T(8,128)(2,1)S(1)} %bitcast.13), channel_id=1, source_target_pairs={{0,112},{16,32},{32,16},{48,64},{64,48},{80,96},{96,80},{112,0},{1... | collective-permute-start | bytes 983048 | tf_op jit(solution)/shard_map/ppermute | solution.py:359
  16.8 6.8 %collective-permute-start.6 = (bf16[20,64,128]{2,1,0:T(8,128)(2,1)S(1)}, bf16[20,64,128]{2,1,0:T(8,128)(2,1)S(1)}, u32[]{:S(2)}, u32[]{:S(2)}) collective-permute-start(bf16[20,64,128]{2,1,0:T(8,128)(2,1)S(1)} %bitcast.14), channel_id=1, source_target_pairs={{0,16},{16,0},{32,48},{48,32},{64,80},{80,64},{96,112},{112,96},{1... | collective-permute-start | bytes 983048 | tf_op jit(solution)/shard_map/ppermute | solution.py:358
  21.3 2.7 %collective-permute-start.5 = (bf16[96,1792]{1,0:T(8,128)(2,1)S(1)}, bf16[96,1792]{1,0:T(8,128)(2,1)S(1)}, u32[]{:S(2)}, u32[]{:S(2)}) collective-permute-start(bf16[96,1792]{1,0:T(8,128)(2,1)S(1)} %get-tuple-element.69.own_ref), channel_id=1, source_target_pairs={{0,16},{16,0},{32,48},{48,32},{64,80},{80,64},{96,112},{112,96},{1... | collective-permute-start | bytes 1032200 | tf_op jit(solution)/shard_map/ppermute | solution.py:370
  27.2 2.6 %collective-permute-start.8 = (bf16[6,32,128]{2,1,0:T(8,128)(2,1)S(1)}, bf16[6,32,128]{2,1,0:T(8,128)(2,1)S(1)}, u32[]{:S(2)}, u32[]{:S(2)}) collective-permute-start(bf16[6,32,128]{2,1,0:T(8,128)(2,1)S(1)} %get-tuple-element.75), channel_id=1, source_target_pairs={{0,16},{16,0},{32,48},{48,32},{64,80},{80,64},{96,112},{112,96},{1... | collective-permute-start | bytes 147464 | tf_op jit(solution)/shard_map/ppermute | solution.py:387
  28.4 3.5 %collective-permute-start.9 = (bf16[6,32,128]{2,1,0:T(8,128)(2,1)S(1)}, bf16[6,32,128]{2,1,0:T(8,128)(2,1)S(1)}, u32[]{:S(2)}, u32[]{:S(2)}) collective-permute-start(bf16[6,32,128]{2,1,0:T(8,128)(2,1)S(1)} %get-tuple-element.76), channel_id=1, source_target_pairs={{0,112},{16,32},{32,16},{48,64},{64,48},{80,96},{96,80},{112,0},{1... | collective-permute-start | bytes 147464 | tf_op jit(solution)/shard_map/ppermute | solution.py:388
  32.4 3.6 %collective-permute-start.10 = (bf16[32,1024]{1,0:T(8,128)(2,1)S(1)}, bf16[32,1024]{1,0:T(8,128)(2,1)S(1)}, u32[]{:S(2)}, u32[]{:S(2)}) collective-permute-start(bf16[32,1024]{1,0:T(8,128)(2,1)S(1)} %get-tuple-element.82), channel_id=1, source_target_pairs={{0,4},{1,5},{2,6},{3,7},{4,0},{5,1},{6,2},{7,3},{8,12},{9,13},{10,... | collective-permute-start | bytes 196616 | tf_op jit(solution)/shard_map/ppermute | solution.py:398
  32.5 4.1 %collective-permute-start.11 = (bf16[32,1024]{1,0:T(8,128)(2,1)S(1)}, bf16[32,1024]{1,0:T(8,128)(2,1)S(1)}, u32[]{:S(2)}, u32[]{:S(2)}) collective-permute-start(bf16[32,1024]{1,0:T(8,128)(2,1)S(1)} %get-tuple-element.83), channel_id=1, source_target_pairs={{0,8},{1,9},{2,10},{3,11},{4,12},{5,13},{6,14},{7,15},{8,0},{9,1},... | collective-permute-start | bytes 196616 | tf_op jit(solution)/shard_map/ppermute | solution.py:398
  34.6 5.3 %collective-permute-start.12 = (bf16[32,1024]{1,0:T(8,128)(2,1)S(1)}, bf16[32,1024]{1,0:T(8,128)(2,1)S(1)}, u32[]{:S(2)}, u32[]{:S(2)}) collective-permute-start(bf16[32,1024]{1,0:T(8,128)(2,1)S(1)} %get-tuple-element.84), channel_id=1, source_target_pairs={{0,12},{1,13},{2,14},{3,15},{4,8},{5,9},{6,10},{7,11},{8,4},{9,5},... | collective-permute-start | bytes 196616 | tf_op jit(solution)/shard_map/ppermute | solution.py:398
  40.7 4.0 %collective-permute-start.13 = (f32[32,2688]{1,0:T(8,128)S(1)}, f32[32,2688]{1,0:T(8,128)S(1)}, u32[]{:S(2)}, u32[]{:S(2)}) collective-permute-start(f32[32,2688]{1,0:T(8,128)S(1)} %get-tuple-element.88), channel_id=1, source_target_pairs={{0,16},{16,0},{32,48},{48,32},{64,80},{80,64},{96,112},{112,96},{1... | collective-permute-start | bytes 1032200 | tf_op jit(solution)/shard_map/ppermute | solution.py:406
  44.8 3.9 %collective-permute-start.14 = (bf16[8,3712]{1,0:T(8,128)(2,1)S(1)}, bf16[8,3712]{1,0:T(8,128)(2,1)S(1)}, u32[]{:S(2)}, u32[]{:S(2)}) collective-permute-start(bf16[8,3712]{1,0:T(8,128)(2,1)S(1)} %get-tuple-element.92), channel_id=1, source_target_pairs={{0,1},{1,0},{2,3},{3,2},{4,5},{5,4},{6,7},{7,6},{8,9},{9,8},{10,11... | collective-permute-start | bytes 178184 | tf_op jit(solution)/shard_map/ppermute | solution.py:413
  44.9 5.3 %collective-permute-start.15 = (bf16[8,3712]{1,0:T(8,128)(2,1)S(1)}, bf16[8,3712]{1,0:T(8,128)(2,1)S(1)}, u32[]{:S(2)}, u32[]{:S(2)}) collective-permute-start(bf16[8,3712]{1,0:T(8,128)(2,1)S(1)} %get-tuple-element.93), channel_id=1, source_target_pairs={{0,2},{1,3},{2,0},{3,1},{4,6},{5,7},{6,4},{7,5},{8,10},{9,11},{10,... | collective-permute-start | bytes 178184 | tf_op jit(solution)/shard_map/ppermute | solution.py:413
  47.5 4.3 %collective-permute-start.16 = (bf16[8,3712]{1,0:T(8,128)(2,1)S(1)}, bf16[8,3712]{1,0:T(8,128)(2,1)S(1)}, u32[]{:S(2)}, u32[]{:S(2)}) collective-permute-start(bf16[8,3712]{1,0:T(8,128)(2,1)S(1)} %get-tuple-element.94), channel_id=1, source_target_pairs={{0,3},{1,2},{2,1},{3,0},{4,7},{5,6},{6,5},{7,4},{8,11},{9,10},{10,... | collective-permute-start | bytes 178184 | tf_op jit(solution)/shard_map/ppermute | solution.py:413
  51.8 4.3 %collective-permute-start.19 = (bf16[8,2688]{1,0:T(8,128)(2,1)S(1)}, bf16[8,2688]{1,0:T(8,128)(2,1)S(1)}, u32[]{:S(2)}, u32[]{:S(2)}) collective-permute-start(bf16[8,2688]{1,0:T(8,128)(2,1)S(1)} %get-tuple-element.96), channel_id=1, source_target_pairs={{0,96},{16,112},{32,64},{48,80},{64,32},{80,48},{96,0},{112,16},{1... | collective-permute-start | bytes 129032 | tf_op jit(solution)/shard_map/ppermute | solution.py:417
  54.7 4.4 %collective-permute-start.18 = (bf16[8,2688]{1,0:T(8,128)(2,1)S(1)}, bf16[8,2688]{1,0:T(8,128)(2,1)S(1)}, u32[]{:S(2)}, u32[]{:S(2)}) collective-permute-start(bf16[8,2688]{1,0:T(8,128)(2,1)S(1)} %get-tuple-element.96), channel_id=1, source_target_pairs={{0,64},{16,80},{32,96},{48,112},{64,0},{80,16},{96,32},{112,48},{1... | collective-permute-start | bytes 129032 | tf_op jit(solution)/shard_map/ppermute | solution.py:417
  54.7 4.4 %collective-permute-start.17 = (bf16[8,2688]{1,0:T(8,128)(2,1)S(1)}, bf16[8,2688]{1,0:T(8,128)(2,1)S(1)}, u32[]{:S(2)}, u32[]{:S(2)}) collective-permute-start(bf16[8,2688]{1,0:T(8,128)(2,1)S(1)} %get-tuple-element.96), channel_id=1, source_target_pairs={{0,32},{16,48},{32,0},{48,16},{64,96},{80,112},{96,64},{112,80},{1... | collective-permute-start | bytes 129032 | tf_op jit(solution)/shard_map/ppermute | solution.py:417
  59.1 6.9 %collective-permute-start.20 = (bf16[8,2688]{1,0:T(8,128)(2,1)S(1)}, bf16[8,2688]{1,0:T(8,128)(2,1)S(1)}, u32[]{:S(2)}, u32[]{:S(2)}) collective-permute-start(bf16[8,2688]{1,0:T(8,128)(2,1)S(1)} %add_convert_fusion), channel_id=1, source_target_pairs={{0,128},{128,0},{1,129},{129,1},{2,130},{130,2},{3,131},{131,3},{4... | collective-permute-start | bytes 129032 | tf_op jit(solution)/shard_map/ppermute | solution.py:420
  66.0 5.8 %collective-permute-start.21 = (f32[8,2688]{1,0:T(8,128)S(1)}, f32[8,2688]{1,0:T(8,128)S(1)}, u32[]{:S(2)}, u32[]{:S(2)}) collective-permute-start(f32[8,2688]{1,0:T(8,128)S(1)} %convert_add_fusion.own_ref), channel_id=1, source_target_pairs={{0,16},{16,0},{32,48},{48,32},{64,80},{80,64},{96,112},{112,96},{1... | collective-permute-start | bytes 258056 | tf_op jit(solution)/shard_map/ppermute | solution.py:421
  (2 other events, 1.6 us)

commit v6 on v5

--- a/solution.py
+++ b/solution.py
@@ -344,8 +344,7 @@
     p1 = lax.ppermute(w0, joint, zed(1, 2))
     p2 = lax.ppermute(w0, joint, zed(0, 3))
 
-    w_second, grad_out, w0 = lax.optimization_barrier((w_second, grad_out, w0))
-    act_in, p1 = lax.optimization_barrier((act_in, p1))
+    act_in, w_second, grad_out, w0 = lax.optimization_barrier((act_in, w_second, grad_out, w0))
     rows = jnp.pad(jnp.transpose(act_in[0], (1, 2, 0, 3)), ((0, 0), (3, 3), (0, 0), (0, 0)))
     xo = lax.dynamic_slice_in_dim(rows, x * 4, 10, axis=1).reshape(20, 64, W)
     a = run(
@@ -355,6 +354,7 @@
         [pltpu.VMEM((2, 18, 8, W), F32), pltpu.VMEM((8, K2), F32)],
         10**9,
     )
+    xo, p1 = lax.optimization_barrier((xo, p1))
     xchip = lax.ppermute(xo, "space", other)
     xnext = lax.ppermute(xo, "space", across)
 

time: 72.8 us -> 72.5 us (level)
  waiting for transfers between devices: 21.6 us -> 20.3 us
  local copies, waits for them, and re-layouts: 3.44 us -> 4.49 us
    ppermute x1, waiting for transfers between devices: 1.88 us -> 0.49 us  [local(): p1 = lax.ppermute(w0, joint, zed(1, 2))]
    dynamic_slice x2, local copies, waits for them, and re-layouts: 0.34 us -> 1.39 us  [local(): xo = lax.dynamic_slice_in_dim(rows, x * 4, 10, axis=1).reshape(20, 64, W)]
    ppermute x1, waiting for transfers between devices: 2.31 us -> 1.53 us  [local(): lax.ppermute(part, 'sample', [(0, 1), (1, 0)]).astype(F32)]
    ppermute x1, starting transfers between devices: 4.58 us -> 5.34 us  [local(): lax.ppermute(part, 'sample', [(0, 1), (1, 0)]).astype(F32)]
    unnamed x9 -> x7, local copies, waits for them, and re-layouts: 3.1 us -> 3.09 us
  transfers between devices with their start and end apart: 22 -> 22, of which waited for: 13 -> 14; matrix products, arithmetic and copies ran while one was open for 1% -> 3% of each run, Pallas kernels for 3% -> 3%
where the time goes in v6:
time: 72.5 us; the launch traced here: 72.2 us
  starting transfers between devices  39.2 us (54%)
  waiting for transfers between devices  20.3 us (28%)
  Pallas kernels  7.43 us (10%)
  local copies, waits for them, and re-layouts  4.49 us (6%)
  between operations  0.8 us (1%)
    pallas_call x14, Pallas kernels, run(): pl.pallas_call(kernel, out_shape=outs, in_specs=[VMEM] * len(args), out_s...  7.43 us
    ppermute x1, starting transfers between devices, local(): p2 = lax.ppermute(w0, joint, zed(0, 3))  7.07 us
    ppermute x1, starting transfers between devices, local(): lax.ppermute(part, 'sample', [(0, 1), (1, 0)]).astype(F32)  5.34 us
    ppermute x1, starting transfers between devices, local(): got = lax.ppermute(part, 'space', other)  4.6 us
    ppermute x3, waiting for transfers between devices, local(): s = [lax.ppermute(s[k - 1], 'filt', Z[k]) for k in (1, 2, 3)]  4.5 us
    ppermute x3, starting transfers between devices, local(): b = [b[0]] + [lax.ppermute(b[k], 'filt', X[k]) for k in (1, 2, 3)]  3.95 us
    ppermute x3, starting transfers between devices, local(): s = [lax.ppermute(s[k - 1], 'filt', X[k]) for k in (1, 2, 3)]  3.94 us
    ppermute x3, waiting for transfers between devices, local(): lax.ppermute(part, 'space', [(i, i ^ 2 * k) for i in range(8)])  3.77 us
  transfers between devices with their start and end apart: 22, of which 14 were waited for; matrix products, arithmetic and copies ran while one was open for 3% of the time, Pallas kernels for 3%

profile of v6, /device:TPU:1, one launch (start us, length us, event | category | flops | bytes accessed | tf_op | source)
XLA Modules:
  0.0 72.2 jit_solution(98855622725054094)
XLA Ops:
  1.5 7.1 %collective-permute-start.1 = (bf16[8,1792]{1,0:T(8,128)(2,1)S(1)}, bf16[8,1792]{1,0:T(8,128)(2,1)S(1)}, u32[]{:S(2)}, u32[]{:S(2)}) collective-permute-start(bf16[8,1792]{1,0:T(8,128)(2,1)S(1)} %shard_map.67.w0_ref), channel_id=1, source_target_pairs={{0,0},{1,1},{2,2},{3,3},{4,4},{5,5},{6,6},{7,7},{8,8},{9,9},{10,10... | collective-permute-start | bytes 86024 | tf_op jit(solution)/shard_map/ppermute | solution.py:345
  8.7 1.3 %pad_dynamic-slice_fusion = bf16[2,10,64,128]{3,1,0,2:T(8,128)(2,1)S(1)} fusion(s32[]{:T(128)S(6)} %select_n.3, bf16[2,16,64,128]{3,1,0,2:T(8,128)(2,1)} %bitcast.19), kind=kLoop, calls=%fused_computation | loop fusion | bytes 851972 | tf_op jit(solution)/shard_map/dynamic_slice | solution.py:349
  12.4 1.3 %collective-permute-start.2 = (bf16[8,6912]{1,0:T(8,128)(2,1)S(1)}, bf16[8,6912]{1,0:T(8,128)(2,1)S(1)}, u32[]{:S(2)}, u32[]{:S(2)}) collective-permute-start(bf16[8,6912]{1,0:T(8,128)(2,1)S(1)} %get-tuple-element.68), channel_id=1, source_target_pairs={{0,1},{1,0},{2,3},{3,2},{4,5},{5,4},{6,7},{7,6},{8,9},{9,8},{10,11... | collective-permute-start | bytes 331784 | tf_op jit(solution)/shard_map/ppermute | solution.py:363
  13.7 2.5 %collective-permute-start.3 = (bf16[8,6912]{1,0:T(8,128)(2,1)S(1)}, bf16[8,6912]{1,0:T(8,128)(2,1)S(1)}, u32[]{:S(2)}, u32[]{:S(2)}) collective-permute-start(bf16[8,6912]{1,0:T(8,128)(2,1)S(1)} %get-tuple-element.69), channel_id=1, source_target_pairs={{0,2},{1,3},{2,0},{3,1},{4,6},{5,7},{6,4},{7,5},{8,10},{9,11},{10,... | collective-permute-start | bytes 331784 | tf_op jit(solution)/shard_map/ppermute | solution.py:363
  16.3 3.1 %collective-permute-start.6 = (bf16[20,64,128]{2,1,0:T(8,128)(2,1)S(1)}, bf16[20,64,128]{2,1,0:T(8,128)(2,1)S(1)}, u32[]{:S(2)}, u32[]{:S(2)}) collective-permute-start(bf16[20,64,128]{2,1,0:T(8,128)(2,1)S(1)} %bitcast.14), channel_id=1, source_target_pairs={{0,16},{16,0},{32,48},{48,32},{64,80},{80,64},{96,112},{112,96},{1... | collective-permute-start | bytes 983048 | tf_op jit(solution)/shard_map/ppermute | solution.py:358
  19.5 1.7 %collective-permute-done.4.b3 = bf16[8,6912]{1,0:T(8,128)(2,1)S(1)} collective-permute-done((bf16[8,6912]{1,0:T(8,128)(2,1)S(1)}, bf16[8,6912]{1,0:T(8,128)(2,1)S(1)}, u32[]{:S(2)}, u32[]{:S(2)}) %collective-permute-start.4) | collective-permute-done | bytes 110624 | tf_op jit(solution)/shard_map/ppermute | solution.py:363
  21.7 1.4 %collective-permute-done.7.next_ref = bf16[20,64,128]{2,1,0:T(8,128)(2,1)S(1)} collective-permute-done((bf16[20,64,128]{2,1,0:T(8,128)(2,1)S(1)}, bf16[20,64,128]{2,1,0:T(8,128)(2,1)S(1)}, u32[]{:S(2)}, u32[]{:S(2)}) %collective-permute-start.7) | collective-permute-done | bytes 327712 | tf_op jit(solution)/shard_map/ppermute | solution.py:359
  23.6 2.3 %shard_map.73 = (f32[32,1024]{1,0:T(8,128)S(1)}, bf16[32,384,128]{2,1,0:T(8,128)(2,1)S(1)}) custom-call(bf16[96,1792]{1,0:T(8,128)(2,1)S(1)} %get-tuple-element.71.own_ref, bf16[96,1792]{1,0:T(8,128)(2,1)S(1)} %collective-permute-done.5.got_ref, bf16[20,192,128]{2,1,0:T(8,128)(2,1)S(1)} %shard_map.71.xo_ref, bf16[40,192,128]{2,1,0:T(8,128)(2,1)S(1)} %shard_map.72.xr_ref), custom_call_target="tpu_custom_call" | custom-call | flops 4000000000 | bytes 100000 | tf_op jit(solution)/shard_map/pallas_call | solution.py:20
  26.7 1.2 %collective-permute-start.8 = (bf16[6,32,128]{2,1,0:T(8,128)(2,1)S(1)}, bf16[6,32,128]{2,1,0:T(8,128)(2,1)S(1)}, u32[]{:S(2)}, u32[]{:S(2)}) collective-permute-start(bf16[6,32,128]{2,1,0:T(8,128)(2,1)S(1)} %get-tuple-element.77), channel_id=1, source_target_pairs={{0,16},{16,0},{32,48},{48,32},{64,80},{80,64},{96,112},{112,96},{1... | collective-permute-start | bytes 147464 | tf_op jit(solution)/shard_map/ppermute | solution.py:387
  28.2 1.1 %shard_map.76.dw2_ref = f32[32,3456]{1,0:T(8,128)S(1)} custom-call(bf16[32,384,128]{2,1,0:T(8,128)(2,1)S(1)} %get-tuple-element.74.xa_ref, bf16[6,32,128]{2,1,0:T(8,128)(2,1)S(1)} %get-tuple-element.75.gs0_ref, bf16[6,32,128]{2,1,0:T(8,128)(2,1)S(1)} %get-tuple-element.76.gs1_ref), custom_call_target="tpu_custom_call" | custom-call | flops 2500000000 | bytes 100000 | tf_op jit(solution)/shard_map/pallas_call | solution.py:20
  29.4 2.1 %collective-permute-done.9.next_ref = bf16[6,32,128]{2,1,0:T(8,128)(2,1)S(1)} collective-permute-done((bf16[6,32,128]{2,1,0:T(8,128)(2,1)S(1)}, bf16[6,32,128]{2,1,0:T(8,128)(2,1)S(1)}, u32[]{:S(2)}, u32[]{:S(2)}) %collective-permute-start.9) | collective-permute-done | bytes 49184 | tf_op jit(solution)/shard_map/ppermute | solution.py:388
  32.1 2.5 %collective-permute-start.11 = (bf16[32,1024]{1,0:T(8,128)(2,1)S(1)}, bf16[32,1024]{1,0:T(8,128)(2,1)S(1)}, u32[]{:S(2)}, u32[]{:S(2)}) collective-permute-start(bf16[32,1024]{1,0:T(8,128)(2,1)S(1)} %get-tuple-element.85), channel_id=1, source_target_pairs={{0,8},{1,9},{2,10},{3,11},{4,12},{5,13},{6,14},{7,15},{8,0},{9,1},... | collective-permute-start | bytes 196616 | tf_op jit(solution)/shard_map/ppermute | solution.py:398
  36.2 3.9 %collective-permute-done.12.r3 = bf16[32,1024]{1,0:T(8,128)(2,1)S(1)} collective-permute-done((bf16[32,1024]{1,0:T(8,128)(2,1)S(1)}, bf16[32,1024]{1,0:T(8,128)(2,1)S(1)}, u32[]{:S(2)}, u32[]{:S(2)}) %collective-permute-start.12) | collective-permute-done | bytes 65568 | tf_op jit(solution)/shard_map/ppermute | solution.py:398
  40.9 2.5 %collective-permute-start.13 = (f32[32,2688]{1,0:T(8,128)S(1)}, f32[32,2688]{1,0:T(8,128)S(1)}, u32[]{:S(2)}, u32[]{:S(2)}) collective-permute-start(f32[32,2688]{1,0:T(8,128)S(1)} %get-tuple-element.90), channel_id=1, source_target_pairs={{0,16},{16,0},{32,48},{48,32},{64,80},{80,64},{96,112},{112,96},{1... | collective-permute-start | bytes 1032200 | tf_op jit(solution)/shard_map/ppermute | solution.py:406
  43.4 1.3 %collective-permute-done.13.got_ref = f32[32,2688]{1,0:T(8,128)S(1)} collective-permute-done((f32[32,2688]{1,0:T(8,128)S(1)}, f32[32,2688]{1,0:T(8,128)S(1)}, u32[]{:S(2)}, u32[]{:S(2)}) %collective-permute-start.13) | collective-permute-done | bytes 344096 | tf_op jit(solution)/shard_map/ppermute | solution.py:406
  44.9 2.8 %collective-permute-start.15 = (bf16[8,3712]{1,0:T(8,128)(2,1)S(1)}, bf16[8,3712]{1,0:T(8,128)(2,1)S(1)}, u32[]{:S(2)}, u32[]{:S(2)}) collective-permute-start(bf16[8,3712]{1,0:T(8,128)(2,1)S(1)} %get-tuple-element.95), channel_id=1, source_target_pairs={{0,2},{1,3},{2,0},{3,1},{4,6},{5,7},{6,4},{7,5},{8,10},{9,11},{10,... | collective-permute-start | bytes 178184 | tf_op jit(solution)/shard_map/ppermute | solution.py:413
  47.6 1.1 %collective-permute-start.16 = (bf16[8,3712]{1,0:T(8,128)(2,1)S(1)}, bf16[8,3712]{1,0:T(8,128)(2,1)S(1)}, u32[]{:S(2)}, u32[]{:S(2)}) collective-permute-start(bf16[8,3712]{1,0:T(8,128)(2,1)S(1)} %get-tuple-element.96), channel_id=1, source_target_pairs={{0,3},{1,2},{2,1},{3,0},{4,7},{5,6},{6,5},{7,4},{8,11},{9,10},{10,... | collective-permute-start | bytes 178184 | tf_op jit(solution)/shard_map/ppermute | solution.py:413
  48.7 1.6 %collective-permute-done.15.r2 = bf16[8,3712]{1,0:T(8,128)(2,1)S(1)} collective-permute-done((bf16[8,3712]{1,0:T(8,128)(2,1)S(1)}, bf16[8,3712]{1,0:T(8,128)(2,1)S(1)}, u32[]{:S(2)}, u32[]{:S(2)}) %collective-permute-start.15) | collective-permute-done | bytes 59424 | tf_op jit(solution)/shard_map/ppermute | solution.py:413
  50.3 1.6 %collective-permute-done.16.r3 = bf16[8,3712]{1,0:T(8,128)(2,1)S(1)} collective-permute-done((bf16[8,3712]{1,0:T(8,128)(2,1)S(1)}, bf16[8,3712]{1,0:T(8,128)(2,1)S(1)}, u32[]{:S(2)}, u32[]{:S(2)}) %collective-permute-start.16) | collective-permute-done | bytes 59424 | tf_op jit(solution)/shard_map/ppermute | solution.py:413
  51.9 2.6 %collective-permute-start.19 = (bf16[8,2688]{1,0:T(8,128)(2,1)S(1)}, bf16[8,2688]{1,0:T(8,128)(2,1)S(1)}, u32[]{:S(2)}, u32[]{:S(2)}) collective-permute-start(bf16[8,2688]{1,0:T(8,128)(2,1)S(1)} %get-tuple-element.98), channel_id=1, source_target_pairs={{0,96},{16,112},{32,64},{48,80},{64,32},{80,48},{96,0},{112,16},{1... | collective-permute-start | bytes 129032 | tf_op jit(solution)/shard_map/ppermute | solution.py:417
  56.1 2.9 %collective-permute-done.18 = bf16[8,2688]{1,0:T(8,128)(2,1)S(1)} collective-permute-done((bf16[8,2688]{1,0:T(8,128)(2,1)S(1)}, bf16[8,2688]{1,0:T(8,128)(2,1)S(1)}, u32[]{:S(2)}, u32[]{:S(2)}) %collective-permute-start.18) | collective-permute-done | bytes 43040 | tf_op jit(solution)/shard_map/ppermute | solution.py:417
  59.1 5.3 %collective-permute-start.20 = (bf16[8,2688]{1,0:T(8,128)(2,1)S(1)}, bf16[8,2688]{1,0:T(8,128)(2,1)S(1)}, u32[]{:S(2)}, u32[]{:S(2)}) collective-permute-start(bf16[8,2688]{1,0:T(8,128)(2,1)S(1)} %add_convert_fusion), channel_id=1, source_target_pairs={{0,128},{128,0},{1,129},{129,1},{2,130},{130,2},{3,131},{131,3},{4... | collective-permute-start | bytes 129032 | tf_op jit(solution)/shard_map/ppermute | solution.py:420
  64.4 1.5 %collective-permute-done.20 = bf16[8,2688]{1,0:T(8,128)(2,1)S(1)} collective-permute-done((bf16[8,2688]{1,0:T(8,128)(2,1)S(1)}, bf16[8,2688]{1,0:T(8,128)(2,1)S(1)}, u32[]{:S(2)}, u32[]{:S(2)}) %collective-permute-start.20) | collective-permute-done | bytes 43040 | tf_op jit(solution)/shard_map/ppermute | solution.py:420
  66.0 4.6 %collective-permute-start.21 = (f32[8,2688]{1,0:T(8,128)S(1)}, f32[8,2688]{1,0:T(8,128)S(1)}, u32[]{:S(2)}, u32[]{:S(2)}) collective-permute-start(f32[8,2688]{1,0:T(8,128)S(1)} %convert_add_fusion.own_ref), channel_id=1, source_target_pairs={{0,16},{16,0},{32,48},{48,32},{64,80},{80,64},{96,112},{112,96},{1... | collective-permute-start | bytes 258056 | tf_op jit(solution)/shard_map/ppermute | solution.py:421
  (46 shorter events, 12.2 us)
Async XLA Ops:
  0.6 0.8 %copy-start.1 = (bf16[27,64,8]{1,2,0:T(8,128)(2,1)S(1)}, bf16[27,64,8]{1,2,0:T(8,128)(2,1)}, u32[]{:S(2)}) copy-start(bf16[27,64,8]{1,2,0:T(8,128)(2,1)} %param.5) | copy-start | bytes 82948
  1.5 10.8 %collective-permute-start.1 = (bf16[8,1792]{1,0:T(8,128)(2,1)S(1)}, bf16[8,1792]{1,0:T(8,128)(2,1)S(1)}, u32[]{:S(2)}, u32[]{:S(2)}) collective-permute-start(bf16[8,1792]{1,0:T(8,128)(2,1)S(1)} %shard_map.67.w0_ref), channel_id=1, source_target_pairs={{0,0},{1,1},{2,2},{3,3},{4,4},{5,5},{6,6},{7,7},{8,8},{9,9},{10,10... | collective-permute-start | bytes 86024 | tf_op jit(solution)/shard_map/ppermute | solution.py:345
  8.6 3.7 %collective-permute-start = (bf16[8,1792]{1,0:T(8,128)(2,1)S(1)}, bf16[8,1792]{1,0:T(8,128)(2,1)S(1)}, u32[]{:S(2)}, u32[]{:S(2)}) collective-permute-start(bf16[8,1792]{1,0:T(8,128)(2,1)S(1)} %shard_map.67.w0_ref), channel_id=1, source_target_pairs={{0,4},{1,5},{2,6},{3,7},{4,0},{5,1},{6,2},{7,3},{8,12},{9,13},{10,... | collective-permute-start | bytes 86024 | tf_op jit(solution)/shard_map/ppermute | solution.py:344
  10.0 0.8 %copy-start = (bf16[1,8,2,16,128]{4,3,2,1,0:T(8,128)(2,1)S(1)}, bf16[1,8,2,16,128]{4,3,2,1,0:T(8,128)(2,1)}, u32[]{:S(2)}) copy-start(bf16[1,8,2,16,128]{4,3,2,1,0:T(8,128)(2,1)} %param.7) | copy-start | bytes 196612
  12.4 7.1 %collective-permute-start.2 = (bf16[8,6912]{1,0:T(8,128)(2,1)S(1)}, bf16[8,6912]{1,0:T(8,128)(2,1)S(1)}, u32[]{:S(2)}, u32[]{:S(2)}) collective-permute-start(bf16[8,6912]{1,0:T(8,128)(2,1)S(1)} %get-tuple-element.68), channel_id=1, source_target_pairs={{0,1},{1,0},{2,3},{3,2},{4,5},{5,4},{6,7},{7,6},{8,9},{9,8},{10,11... | collective-permute-start | bytes 331784 | tf_op jit(solution)/shard_map/ppermute | solution.py:363
  13.7 5.9 %collective-permute-start.3 = (bf16[8,6912]{1,0:T(8,128)(2,1)S(1)}, bf16[8,6912]{1,0:T(8,128)(2,1)S(1)}, u32[]{:S(2)}, u32[]{:S(2)}) collective-permute-start(bf16[8,6912]{1,0:T(8,128)(2,1)S(1)} %get-tuple-element.69), channel_id=1, source_target_pairs={{0,2},{1,3},{2,0},{3,1},{4,6},{5,7},{6,4},{7,5},{8,10},{9,11},{10,... | collective-permute-start | bytes 331784 | tf_op jit(solution)/shard_map/ppermute | solution.py:363
  16.1 5.1 %collective-permute-start.4 = (bf16[8,6912]{1,0:T(8,128)(2,1)S(1)}, bf16[8,6912]{1,0:T(8,128)(2,1)S(1)}, u32[]{:S(2)}, u32[]{:S(2)}) collective-permute-start(bf16[8,6912]{1,0:T(8,128)(2,1)S(1)} %get-tuple-element.70), channel_id=1, source_target_pairs={{0,3},{1,2},{2,1},{3,0},{4,7},{5,6},{6,5},{7,4},{8,11},{9,10},{10,... | collective-permute-start | bytes 331784 | tf_op jit(solution)/shard_map/ppermute | solution.py:363
  16.3 6.8 %collective-permute-start.7 = (bf16[20,64,128]{2,1,0:T(8,128)(2,1)S(1)}, bf16[20,64,128]{2,1,0:T(8,128)(2,1)S(1)}, u32[]{:S(2)}, u32[]{:S(2)}) collective-permute-start(bf16[20,64,128]{2,1,0:T(8,128)(2,1)S(1)} %bitcast.13), channel_id=1, source_target_pairs={{0,112},{16,32},{32,16},{48,64},{64,48},{80,96},{96,80},{112,0},{1... | collective-permute-start | bytes 983048 | tf_op jit(solution)/shard_map/ppermute | solution.py:359
  16.3 6.8 %collective-permute-start.6 = (bf16[20,64,128]{2,1,0:T(8,128)(2,1)S(1)}, bf16[20,64,128]{2,1,0:T(8,128)(2,1)S(1)}, u32[]{:S(2)}, u32[]{:S(2)}) collective-permute-start(bf16[20,64,128]{2,1,0:T(8,128)(2,1)S(1)} %bitcast.14), channel_id=1, source_target_pairs={{0,16},{16,0},{32,48},{48,32},{64,80},{80,64},{96,112},{112,96},{1... | collective-permute-start | bytes 983048 | tf_op jit(solution)/shard_map/ppermute | solution.py:358
  21.3 2.2 %collective-permute-start.5 = (bf16[96,1792]{1,0:T(8,128)(2,1)S(1)}, bf16[96,1792]{1,0:T(8,128)(2,1)S(1)}, u32[]{:S(2)}, u32[]{:S(2)}) collective-permute-start(bf16[96,1792]{1,0:T(8,128)(2,1)S(1)} %get-tuple-element.71.own_ref), channel_id=1, source_target_pairs={{0,16},{16,0},{32,48},{48,32},{64,80},{80,64},{96,112},{112,96},{1... | collective-permute-start | bytes 1032200 | tf_op jit(solution)/shard_map/ppermute | solution.py:370
  26.7 2.6 %collective-permute-start.8 = (bf16[6,32,128]{2,1,0:T(8,128)(2,1)S(1)}, bf16[6,32,128]{2,1,0:T(8,128)(2,1)S(1)}, u32[]{:S(2)}, u32[]{:S(2)}) collective-permute-start(bf16[6,32,128]{2,1,0:T(8,128)(2,1)S(1)} %get-tuple-element.77), channel_id=1, source_target_pairs={{0,16},{16,0},{32,48},{48,32},{64,80},{80,64},{96,112},{112,96},{1... | collective-permute-start | bytes 147464 | tf_op jit(solution)/shard_map/ppermute | solution.py:387
  27.9 3.5 %collective-permute-start.9 = (bf16[6,32,128]{2,1,0:T(8,128)(2,1)S(1)}, bf16[6,32,128]{2,1,0:T(8,128)(2,1)S(1)}, u32[]{:S(2)}, u32[]{:S(2)}) collective-permute-start(bf16[6,32,128]{2,1,0:T(8,128)(2,1)S(1)} %get-tuple-element.78), channel_id=1, source_target_pairs={{0,112},{16,32},{32,16},{48,64},{64,48},{80,96},{96,80},{112,0},{1... | collective-permute-start | bytes 147464 | tf_op jit(solution)/shard_map/ppermute | solution.py:388
  32.0 3.6 %collective-permute-start.10 = (bf16[32,1024]{1,0:T(8,128)(2,1)S(1)}, bf16[32,1024]{1,0:T(8,128)(2,1)S(1)}, u32[]{:S(2)}, u32[]{:S(2)}) collective-permute-start(bf16[32,1024]{1,0:T(8,128)(2,1)S(1)} %get-tuple-element.84), channel_id=1, source_target_pairs={{0,4},{1,5},{2,6},{3,7},{4,0},{5,1},{6,2},{7,3},{8,12},{9,13},{10,... | collective-permute-start | bytes 196616 | tf_op jit(solution)/shard_map/ppermute | solution.py:398
  32.1 4.1 %collective-permute-start.11 = (bf16[32,1024]{1,0:T(8,128)(2,1)S(1)}, bf16[32,1024]{1,0:T(8,128)(2,1)S(1)}, u32[]{:S(2)}, u32[]{:S(2)}) collective-permute-start(bf16[32,1024]{1,0:T(8,128)(2,1)S(1)} %get-tuple-element.85), channel_id=1, source_target_pairs={{0,8},{1,9},{2,10},{3,11},{4,12},{5,13},{6,14},{7,15},{8,0},{9,1},... | collective-permute-start | bytes 196616 | tf_op jit(solution)/shard_map/ppermute | solution.py:398
  34.6 5.6 %collective-permute-start.12 = (bf16[32,1024]{1,0:T(8,128)(2,1)S(1)}, bf16[32,1024]{1,0:T(8,128)(2,1)S(1)}, u32[]{:S(2)}, u32[]{:S(2)}) collective-permute-start(bf16[32,1024]{1,0:T(8,128)(2,1)S(1)} %get-tuple-element.86), channel_id=1, source_target_pairs={{0,12},{1,13},{2,14},{3,15},{4,8},{5,9},{6,10},{7,11},{8,4},{9,5},... | collective-permute-start | bytes 196616 | tf_op jit(solution)/shard_map/ppermute | solution.py:398
  40.9 3.8 %collective-permute-start.13 = (f32[32,2688]{1,0:T(8,128)S(1)}, f32[32,2688]{1,0:T(8,128)S(1)}, u32[]{:S(2)}, u32[]{:S(2)}) collective-permute-start(f32[32,2688]{1,0:T(8,128)S(1)} %get-tuple-element.90), channel_id=1, source_target_pairs={{0,16},{16,0},{32,48},{48,32},{64,80},{80,64},{96,112},{112,96},{1... | collective-permute-start | bytes 1032200 | tf_op jit(solution)/shard_map/ppermute | solution.py:406
  44.8 3.9 %collective-permute-start.14 = (bf16[8,3712]{1,0:T(8,128)(2,1)S(1)}, bf16[8,3712]{1,0:T(8,128)(2,1)S(1)}, u32[]{:S(2)}, u32[]{:S(2)}) collective-permute-start(bf16[8,3712]{1,0:T(8,128)(2,1)S(1)} %get-tuple-element.94), channel_id=1, source_target_pairs={{0,1},{1,0},{2,3},{3,2},{4,5},{5,4},{6,7},{7,6},{8,9},{9,8},{10,11... | collective-permute-start | bytes 178184 | tf_op jit(solution)/shard_map/ppermute | solution.py:413
  44.9 5.4 %collective-permute-start.15 = (bf16[8,3712]{1,0:T(8,128)(2,1)S(1)}, bf16[8,3712]{1,0:T(8,128)(2,1)S(1)}, u32[]{:S(2)}, u32[]{:S(2)}) collective-permute-start(bf16[8,3712]{1,0:T(8,128)(2,1)S(1)} %get-tuple-element.95), channel_id=1, source_target_pairs={{0,2},{1,3},{2,0},{3,1},{4,6},{5,7},{6,4},{7,5},{8,10},{9,11},{10,... | collective-permute-start | bytes 178184 | tf_op jit(solution)/shard_map/ppermute | solution.py:413
  47.6 4.3 %collective-permute-start.16 = (bf16[8,3712]{1,0:T(8,128)(2,1)S(1)}, bf16[8,3712]{1,0:T(8,128)(2,1)S(1)}, u32[]{:S(2)}, u32[]{:S(2)}) collective-permute-start(bf16[8,3712]{1,0:T(8,128)(2,1)S(1)} %get-tuple-element.96), channel_id=1, source_target_pairs={{0,3},{1,2},{2,1},{3,0},{4,7},{5,6},{6,5},{7,4},{8,11},{9,10},{10,... | collective-permute-start | bytes 178184 | tf_op jit(solution)/shard_map/ppermute | solution.py:413
  51.9 4.2 %collective-permute-start.19 = (bf16[8,2688]{1,0:T(8,128)(2,1)S(1)}, bf16[8,2688]{1,0:T(8,128)(2,1)S(1)}, u32[]{:S(2)}, u32[]{:S(2)}) collective-permute-start(bf16[8,2688]{1,0:T(8,128)(2,1)S(1)} %get-tuple-element.98), channel_id=1, source_target_pairs={{0,96},{16,112},{32,64},{48,80},{64,32},{80,48},{96,0},{112,16},{1... | collective-permute-start | bytes 129032 | tf_op jit(solution)/shard_map/ppermute | solution.py:417
  54.6 4.5 %collective-permute-start.18 = (bf16[8,2688]{1,0:T(8,128)(2,1)S(1)}, bf16[8,2688]{1,0:T(8,128)(2,1)S(1)}, u32[]{:S(2)}, u32[]{:S(2)}) collective-permute-start(bf16[8,2688]{1,0:T(8,128)(2,1)S(1)} %get-tuple-element.98), channel_id=1, source_target_pairs={{0,64},{16,80},{32,96},{48,112},{64,0},{80,16},{96,32},{112,48},{1... | collective-permute-start | bytes 129032 | tf_op jit(solution)/shard_map/ppermute | solution.py:417
  54.6 4.5 %collective-permute-start.17 = (bf16[8,2688]{1,0:T(8,128)(2,1)S(1)}, bf16[8,2688]{1,0:T(8,128)(2,1)S(1)}, u32[]{:S(2)}, u32[]{:S(2)}) collective-permute-start(bf16[8,2688]{1,0:T(8,128)(2,1)S(1)} %get-tuple-element.98), channel_id=1, source_target_pairs={{0,32},{16,48},{32,0},{48,16},{64,96},{80,112},{96,64},{112,80},{1... | collective-permute-start | bytes 129032 | tf_op jit(solution)/shard_map/ppermute | solution.py:417
  59.1 6.9 %collective-permute-start.20 = (bf16[8,2688]{1,0:T(8,128)(2,1)S(1)}, bf16[8,2688]{1,0:T(8,128)(2,1)S(1)}, u32[]{:S(2)}, u32[]{:S(2)}) collective-permute-start(bf16[8,2688]{1,0:T(8,128)(2,1)S(1)} %add_convert_fusion), channel_id=1, source_target_pairs={{0,128},{128,0},{1,129},{129,1},{2,130},{130,2},{3,131},{131,3},{4... | collective-permute-start | bytes 129032 | tf_op jit(solution)/shard_map/ppermute | solution.py:420
  66.0 5.5 %collective-permute-start.21 = (f32[8,2688]{1,0:T(8,128)S(1)}, f32[8,2688]{1,0:T(8,128)S(1)}, u32[]{:S(2)}, u32[]{:S(2)}) collective-permute-start(f32[8,2688]{1,0:T(8,128)S(1)} %convert_add_fusion.own_ref), channel_id=1, source_target_pairs={{0,16},{16,0},{32,48},{48,32},{64,80},{80,64},{96,112},{112,96},{1... | collective-permute-start | bytes 258056 | tf_op jit(solution)/shard_map/ppermute | solution.py:421
  (1 other events, 0.8 us)

commit v7 on v6

--- a/solution.py
+++ b/solution.py
@@ -360,7 +360,8 @@
 
     a, p1, p2 = lax.optimization_barrier((a, p1, p2))
     b = run(pack_kernel, [sds((8, 3 * K1P + 12 * W), BF16)] * 4, [w0, p1, p2] + list(a))
-    b = [b[0]] + [lax.ppermute(b[k], "filt", X[k]) for k in (1, 2, 3)]
+    far = {k: lax.ppermute(b[k], "filt", X[k]) for k in (2, 3, 1)}
+    b = [b[0], far[1], far[2], far[3]]
     half, go = run(
         order_kernel,
         [sds((96, K1P), BF16), sds((32, 12 * W), BF16)],

time: 72.5 us -> 72.5 us (level)
  no operation moved by 1% of the time
where the time goes in v7:
time: 72.5 us; the launch traced here: 72.2 us
  starting transfers between devices  39.2 us (54%)
  waiting for transfers between devices  20.3 us (28%)
  Pallas kernels  7.43 us (10%)
  local copies, waits for them, and re-layouts  4.49 us (6%)
  between operations  0.8 us (1%)
    pallas_call x14, Pallas kernels, run(): pl.pallas_call(kernel, out_shape=outs, in_specs=[VMEM] * len(args), out_s...  7.43 us
    ppermute x1, starting transfers between devices, local(): p2 = lax.ppermute(w0, joint, zed(0, 3))  7.07 us
    ppermute x1, starting transfers between devices, local(): lax.ppermute(part, 'sample', [(0, 1), (1, 0)]).astype(F32)  5.34 us
    ppermute x1, starting transfers between devices, local(): got = lax.ppermute(part, 'space', other)  4.6 us
    ppermute x3, waiting for transfers between devices, local(): s = [lax.ppermute(s[k - 1], 'filt', Z[k]) for k in (1, 2, 3)]  4.5 us
    ppermute x3, starting transfers between devices, local(): far = {k: lax.ppermute(b[k], 'filt', X[k]) for k in (2, 3, 1)}  3.95 us
    ppermute x3, starting transfers between devices, local(): s = [lax.ppermute(s[k - 1], 'filt', X[k]) for k in (1, 2, 3)]  3.94 us
    ppermute x3, waiting for transfers between devices, local(): lax.ppermute(part, 'space', [(i, i ^ 2 * k) for i in range(8)])  3.77 us
  transfers between devices with their start and end apart: 22, of which 14 were waited for; matrix products, arithmetic and copies ran while one was open for 3% of the time, Pallas kernels for 3%

profile of v7, /device:TPU:1, one launch (start us, length us, event | category | flops | bytes accessed | tf_op | source)
XLA Modules:
  0.0 72.2 jit_solution(98855622725054094)
XLA Ops:
  1.5 7.1 %collective-permute-start.1 = (bf16[8,1792]{1,0:T(8,128)(2,1)S(1)}, bf16[8,1792]{1,0:T(8,128)(2,1)S(1)}, u32[]{:S(2)}, u32[]{:S(2)}) collective-permute-start(bf16[8,1792]{1,0:T(8,128)(2,1)S(1)} %shard_map.67.w0_ref), channel_id=1, source_target_pairs={{0,0},{1,1},{2,2},{3,3},{4,4},{5,5},{6,6},{7,7},{8,8},{9,9},{10,10... | collective-permute-start | bytes 86024 | tf_op jit(solution)/shard_map/ppermute | solution.py:345
  8.7 1.3 %pad_dynamic-slice_fusion = bf16[2,10,64,128]{3,1,0,2:T(8,128)(2,1)S(1)} fusion(s32[]{:T(128)S(6)} %select_n.3, bf16[2,16,64,128]{3,1,0,2:T(8,128)(2,1)} %bitcast.19), kind=kLoop, calls=%fused_computation | loop fusion | bytes 851972 | tf_op jit(solution)/shard_map/dynamic_slice | solution.py:349
  12.4 1.3 %collective-permute-start.2 = (bf16[8,6912]{1,0:T(8,128)(2,1)S(1)}, bf16[8,6912]{1,0:T(8,128)(2,1)S(1)}, u32[]{:S(2)}, u32[]{:S(2)}) collective-permute-start(bf16[8,6912]{1,0:T(8,128)(2,1)S(1)} %get-tuple-element.68), channel_id=1, source_target_pairs={{0,1},{1,0},{2,3},{3,2},{4,5},{5,4},{6,7},{7,6},{8,9},{9,8},{10,11... | collective-permute-start | bytes 331784 | tf_op jit(solution)/shard_map/ppermute | solution.py:363
  13.7 2.5 %collective-permute-start.3 = (bf16[8,6912]{1,0:T(8,128)(2,1)S(1)}, bf16[8,6912]{1,0:T(8,128)(2,1)S(1)}, u32[]{:S(2)}, u32[]{:S(2)}) collective-permute-start(bf16[8,6912]{1,0:T(8,128)(2,1)S(1)} %get-tuple-element.69), channel_id=1, source_target_pairs={{0,2},{1,3},{2,0},{3,1},{4,6},{5,7},{6,4},{7,5},{8,10},{9,11},{10,... | collective-permute-start | bytes 331784 | tf_op jit(solution)/shard_map/ppermute | solution.py:363
  16.3 3.1 %collective-permute-start.6 = (bf16[20,64,128]{2,1,0:T(8,128)(2,1)S(1)}, bf16[20,64,128]{2,1,0:T(8,128)(2,1)S(1)}, u32[]{:S(2)}, u32[]{:S(2)}) collective-permute-start(bf16[20,64,128]{2,1,0:T(8,128)(2,1)S(1)} %bitcast.14), channel_id=1, source_target_pairs={{0,16},{16,0},{32,48},{48,32},{64,80},{80,64},{96,112},{112,96},{1... | collective-permute-start | bytes 983048 | tf_op jit(solution)/shard_map/ppermute | solution.py:358
  19.5 1.7 %collective-permute-done.4.b3 = bf16[8,6912]{1,0:T(8,128)(2,1)S(1)} collective-permute-done((bf16[8,6912]{1,0:T(8,128)(2,1)S(1)}, bf16[8,6912]{1,0:T(8,128)(2,1)S(1)}, u32[]{:S(2)}, u32[]{:S(2)}) %collective-permute-start.4) | collective-permute-done | bytes 110624 | tf_op jit(solution)/shard_map/ppermute | solution.py:363
  21.7 1.4 %collective-permute-done.7.next_ref = bf16[20,64,128]{2,1,0:T(8,128)(2,1)S(1)} collective-permute-done((bf16[20,64,128]{2,1,0:T(8,128)(2,1)S(1)}, bf16[20,64,128]{2,1,0:T(8,128)(2,1)S(1)}, u32[]{:S(2)}, u32[]{:S(2)}) %collective-permute-start.7) | collective-permute-done | bytes 327712 | tf_op jit(solution)/shard_map/ppermute | solution.py:359
  23.6 2.3 %shard_map.73 = (f32[32,1024]{1,0:T(8,128)S(1)}, bf16[32,384,128]{2,1,0:T(8,128)(2,1)S(1)}) custom-call(bf16[96,1792]{1,0:T(8,128)(2,1)S(1)} %get-tuple-element.71.own_ref, bf16[96,1792]{1,0:T(8,128)(2,1)S(1)} %collective-permute-done.5.got_ref, bf16[20,192,128]{2,1,0:T(8,128)(2,1)S(1)} %shard_map.71.xo_ref, bf16[40,192,128]{2,1,0:T(8,128)(2,1)S(1)} %shard_map.72.xr_ref), custom_call_target="tpu_custom_call" | custom-call | flops 4000000000 | bytes 100000 | tf_op jit(solution)/shard_map/pallas_call | solution.py:20
  26.7 1.2 %collective-permute-start.8 = (bf16[6,32,128]{2,1,0:T(8,128)(2,1)S(1)}, bf16[6,32,128]{2,1,0:T(8,128)(2,1)S(1)}, u32[]{:S(2)}, u32[]{:S(2)}) collective-permute-start(bf16[6,32,128]{2,1,0:T(8,128)(2,1)S(1)} %get-tuple-element.77), channel_id=1, source_target_pairs={{0,16},{16,0},{32,48},{48,32},{64,80},{80,64},{96,112},{112,96},{1... | collective-permute-start | bytes 147464 | tf_op jit(solution)/shard_map/ppermute | solution.py:388
  28.2 1.1 %shard_map.76.dw2_ref = f32[32,3456]{1,0:T(8,128)S(1)} custom-call(bf16[32,384,128]{2,1,0:T(8,128)(2,1)S(1)} %get-tuple-element.74.xa_ref, bf16[6,32,128]{2,1,0:T(8,128)(2,1)S(1)} %get-tuple-element.75.gs0_ref, bf16[6,32,128]{2,1,0:T(8,128)(2,1)S(1)} %get-tuple-element.76.gs1_ref), custom_call_target="tpu_custom_call" | custom-call | flops 2500000000 | bytes 100000 | tf_op jit(solution)/shard_map/pallas_call | solution.py:20
  29.4 2.1 %collective-permute-done.9.next_ref = bf16[6,32,128]{2,1,0:T(8,128)(2,1)S(1)} collective-permute-done((bf16[6,32,128]{2,1,0:T(8,128)(2,1)S(1)}, bf16[6,32,128]{2,1,0:T(8,128)(2,1)S(1)}, u32[]{:S(2)}, u32[]{:S(2)}) %collective-permute-start.9) | collective-permute-done | bytes 49184 | tf_op jit(solution)/shard_map/ppermute | solution.py:389
  32.1 2.5 %collective-permute-start.11 = (bf16[32,1024]{1,0:T(8,128)(2,1)S(1)}, bf16[32,1024]{1,0:T(8,128)(2,1)S(1)}, u32[]{:S(2)}, u32[]{:S(2)}) collective-permute-start(bf16[32,1024]{1,0:T(8,128)(2,1)S(1)} %get-tuple-element.85), channel_id=1, source_target_pairs={{0,8},{1,9},{2,10},{3,11},{4,12},{5,13},{6,14},{7,15},{8,0},{9,1},... | collective-permute-start | bytes 196616 | tf_op jit(solution)/shard_map/ppermute | solution.py:399
  36.2 3.9 %collective-permute-done.12.r3 = bf16[32,1024]{1,0:T(8,128)(2,1)S(1)} collective-permute-done((bf16[32,1024]{1,0:T(8,128)(2,1)S(1)}, bf16[32,1024]{1,0:T(8,128)(2,1)S(1)}, u32[]{:S(2)}, u32[]{:S(2)}) %collective-permute-start.12) | collective-permute-done | bytes 65568 | tf_op jit(solution)/shard_map/ppermute | solution.py:399
  40.9 2.5 %collective-permute-start.13 = (f32[32,2688]{1,0:T(8,128)S(1)}, f32[32,2688]{1,0:T(8,128)S(1)}, u32[]{:S(2)}, u32[]{:S(2)}) collective-permute-start(f32[32,2688]{1,0:T(8,128)S(1)} %get-tuple-element.90), channel_id=1, source_target_pairs={{0,16},{16,0},{32,48},{48,32},{64,80},{80,64},{96,112},{112,96},{1... | collective-permute-start | bytes 1032200 | tf_op jit(solution)/shard_map/ppermute | solution.py:407
  43.4 1.3 %collective-permute-done.13.got_ref = f32[32,2688]{1,0:T(8,128)S(1)} collective-permute-done((f32[32,2688]{1,0:T(8,128)S(1)}, f32[32,2688]{1,0:T(8,128)S(1)}, u32[]{:S(2)}, u32[]{:S(2)}) %collective-permute-start.13) | collective-permute-done | bytes 344096 | tf_op jit(solution)/shard_map/ppermute | solution.py:407
  44.9 2.8 %collective-permute-start.15 = (bf16[8,3712]{1,0:T(8,128)(2,1)S(1)}, bf16[8,3712]{1,0:T(8,128)(2,1)S(1)}, u32[]{:S(2)}, u32[]{:S(2)}) collective-permute-start(bf16[8,3712]{1,0:T(8,128)(2,1)S(1)} %get-tuple-element.95), channel_id=1, source_target_pairs={{0,2},{1,3},{2,0},{3,1},{4,6},{5,7},{6,4},{7,5},{8,10},{9,11},{10,... | collective-permute-start | bytes 178184 | tf_op jit(solution)/shard_map/ppermute | solution.py:414
  47.6 1.1 %collective-permute-start.16 = (bf16[8,3712]{1,0:T(8,128)(2,1)S(1)}, bf16[8,3712]{1,0:T(8,128)(2,1)S(1)}, u32[]{:S(2)}, u32[]{:S(2)}) collective-permute-start(bf16[8,3712]{1,0:T(8,128)(2,1)S(1)} %get-tuple-element.96), channel_id=1, source_target_pairs={{0,3},{1,2},{2,1},{3,0},{4,7},{5,6},{6,5},{7,4},{8,11},{9,10},{10,... | collective-permute-start | bytes 178184 | tf_op jit(solution)/shard_map/ppermute | solution.py:414
  48.7 1.6 %collective-permute-done.15.r2 = bf16[8,3712]{1,0:T(8,128)(2,1)S(1)} collective-permute-done((bf16[8,3712]{1,0:T(8,128)(2,1)S(1)}, bf16[8,3712]{1,0:T(8,128)(2,1)S(1)}, u32[]{:S(2)}, u32[]{:S(2)}) %collective-permute-start.15) | collective-permute-done | bytes 59424 | tf_op jit(solution)/shard_map/ppermute | solution.py:414
  50.3 1.6 %collective-permute-done.16.r3 = bf16[8,3712]{1,0:T(8,128)(2,1)S(1)} collective-permute-done((bf16[8,3712]{1,0:T(8,128)(2,1)S(1)}, bf16[8,3712]{1,0:T(8,128)(2,1)S(1)}, u32[]{:S(2)}, u32[]{:S(2)}) %collective-permute-start.16) | collective-permute-done | bytes 59424 | tf_op jit(solution)/shard_map/ppermute | solution.py:414
  51.9 2.6 %collective-permute-start.19 = (bf16[8,2688]{1,0:T(8,128)(2,1)S(1)}, bf16[8,2688]{1,0:T(8,128)(2,1)S(1)}, u32[]{:S(2)}, u32[]{:S(2)}) collective-permute-start(bf16[8,2688]{1,0:T(8,128)(2,1)S(1)} %get-tuple-element.98), channel_id=1, source_target_pairs={{0,96},{16,112},{32,64},{48,80},{64,32},{80,48},{96,0},{112,16},{1... | collective-permute-start | bytes 129032 | tf_op jit(solution)/shard_map/ppermute | solution.py:418
  56.1 2.9 %collective-permute-done.18 = bf16[8,2688]{1,0:T(8,128)(2,1)S(1)} collective-permute-done((bf16[8,2688]{1,0:T(8,128)(2,1)S(1)}, bf16[8,2688]{1,0:T(8,128)(2,1)S(1)}, u32[]{:S(2)}, u32[]{:S(2)}) %collective-permute-start.18) | collective-permute-done | bytes 43040 | tf_op jit(solution)/shard_map/ppermute | solution.py:418
  59.1 5.3 %collective-permute-start.20 = (bf16[8,2688]{1,0:T(8,128)(2,1)S(1)}, bf16[8,2688]{1,0:T(8,128)(2,1)S(1)}, u32[]{:S(2)}, u32[]{:S(2)}) collective-permute-start(bf16[8,2688]{1,0:T(8,128)(2,1)S(1)} %add_convert_fusion), channel_id=1, source_target_pairs={{0,128},{128,0},{1,129},{129,1},{2,130},{130,2},{3,131},{131,3},{4... | collective-permute-start | bytes 129032 | tf_op jit(solution)/shard_map/ppermute | solution.py:421
  64.4 1.5 %collective-permute-done.20 = bf16[8,2688]{1,0:T(8,128)(2,1)S(1)} collective-permute-done((bf16[8,2688]{1,0:T(8,128)(2,1)S(1)}, bf16[8,2688]{1,0:T(8,128)(2,1)S(1)}, u32[]{:S(2)}, u32[]{:S(2)}) %collective-permute-start.20) | collective-permute-done | bytes 43040 | tf_op jit(solution)/shard_map/ppermute | solution.py:421
  66.0 4.6 %collective-permute-start.21 = (f32[8,2688]{1,0:T(8,128)S(1)}, f32[8,2688]{1,0:T(8,128)S(1)}, u32[]{:S(2)}, u32[]{:S(2)}) collective-permute-start(f32[8,2688]{1,0:T(8,128)S(1)} %convert_add_fusion.own_ref), channel_id=1, source_target_pairs={{0,16},{16,0},{32,48},{48,32},{64,80},{80,64},{96,112},{112,96},{1... | collective-permute-start | bytes 258056 | tf_op jit(solution)/shard_map/ppermute | solution.py:422
  (46 shorter events, 12.2 us)
Async XLA Ops:
  0.6 0.8 %copy-start.1 = (bf16[27,64,8]{1,2,0:T(8,128)(2,1)S(1)}, bf16[27,64,8]{1,2,0:T(8,128)(2,1)}, u32[]{:S(2)}) copy-start(bf16[27,64,8]{1,2,0:T(8,128)(2,1)} %param.5) | copy-start | bytes 82948
  1.5 10.8 %collective-permute-start.1 = (bf16[8,1792]{1,0:T(8,128)(2,1)S(1)}, bf16[8,1792]{1,0:T(8,128)(2,1)S(1)}, u32[]{:S(2)}, u32[]{:S(2)}) collective-permute-start(bf16[8,1792]{1,0:T(8,128)(2,1)S(1)} %shard_map.67.w0_ref), channel_id=1, source_target_pairs={{0,0},{1,1},{2,2},{3,3},{4,4},{5,5},{6,6},{7,7},{8,8},{9,9},{10,10... | collective-permute-start | bytes 86024 | tf_op jit(solution)/shard_map/ppermute | solution.py:345
  8.6 3.7 %collective-permute-start = (bf16[8,1792]{1,0:T(8,128)(2,1)S(1)}, bf16[8,1792]{1,0:T(8,128)(2,1)S(1)}, u32[]{:S(2)}, u32[]{:S(2)}) collective-permute-start(bf16[8,1792]{1,0:T(8,128)(2,1)S(1)} %shard_map.67.w0_ref), channel_id=1, source_target_pairs={{0,4},{1,5},{2,6},{3,7},{4,0},{5,1},{6,2},{7,3},{8,12},{9,13},{10,... | collective-permute-start | bytes 86024 | tf_op jit(solution)/shard_map/ppermute | solution.py:344
  10.0 0.8 %copy-start = (bf16[1,8,2,16,128]{4,3,2,1,0:T(8,128)(2,1)S(1)}, bf16[1,8,2,16,128]{4,3,2,1,0:T(8,128)(2,1)}, u32[]{:S(2)}) copy-start(bf16[1,8,2,16,128]{4,3,2,1,0:T(8,128)(2,1)} %param.7) | copy-start | bytes 196612
  12.4 7.1 %collective-permute-start.2 = (bf16[8,6912]{1,0:T(8,128)(2,1)S(1)}, bf16[8,6912]{1,0:T(8,128)(2,1)S(1)}, u32[]{:S(2)}, u32[]{:S(2)}) collective-permute-start(bf16[8,6912]{1,0:T(8,128)(2,1)S(1)} %get-tuple-element.68), channel_id=1, source_target_pairs={{0,1},{1,0},{2,3},{3,2},{4,5},{5,4},{6,7},{7,6},{8,9},{9,8},{10,11... | collective-permute-start | bytes 331784 | tf_op jit(solution)/shard_map/ppermute | solution.py:363
  13.7 5.9 %collective-permute-start.3 = (bf16[8,6912]{1,0:T(8,128)(2,1)S(1)}, bf16[8,6912]{1,0:T(8,128)(2,1)S(1)}, u32[]{:S(2)}, u32[]{:S(2)}) collective-permute-start(bf16[8,6912]{1,0:T(8,128)(2,1)S(1)} %get-tuple-element.69), channel_id=1, source_target_pairs={{0,2},{1,3},{2,0},{3,1},{4,6},{5,7},{6,4},{7,5},{8,10},{9,11},{10,... | collective-permute-start | bytes 331784 | tf_op jit(solution)/shard_map/ppermute | solution.py:363
  16.1 5.1 %collective-permute-start.4 = (bf16[8,6912]{1,0:T(8,128)(2,1)S(1)}, bf16[8,6912]{1,0:T(8,128)(2,1)S(1)}, u32[]{:S(2)}, u32[]{:S(2)}) collective-permute-start(bf16[8,6912]{1,0:T(8,128)(2,1)S(1)} %get-tuple-element.70), channel_id=1, source_target_pairs={{0,3},{1,2},{2,1},{3,0},{4,7},{5,6},{6,5},{7,4},{8,11},{9,10},{10,... | collective-permute-start | bytes 331784 | tf_op jit(solution)/shard_map/ppermute | solution.py:363
  16.3 6.8 %collective-permute-start.7 = (bf16[20,64,128]{2,1,0:T(8,128)(2,1)S(1)}, bf16[20,64,128]{2,1,0:T(8,128)(2,1)S(1)}, u32[]{:S(2)}, u32[]{:S(2)}) collective-permute-start(bf16[20,64,128]{2,1,0:T(8,128)(2,1)S(1)} %bitcast.13), channel_id=1, source_target_pairs={{0,112},{16,32},{32,16},{48,64},{64,48},{80,96},{96,80},{112,0},{1... | collective-permute-start | bytes 983048 | tf_op jit(solution)/shard_map/ppermute | solution.py:359
  16.3 6.8 %collective-permute-start.6 = (bf16[20,64,128]{2,1,0:T(8,128)(2,1)S(1)}, bf16[20,64,128]{2,1,0:T(8,128)(2,1)S(1)}, u32[]{:S(2)}, u32[]{:S(2)}) collective-permute-start(bf16[20,64,128]{2,1,0:T(8,128)(2,1)S(1)} %bitcast.14), channel_id=1, source_target_pairs={{0,16},{16,0},{32,48},{48,32},{64,80},{80,64},{96,112},{112,96},{1... | collective-permute-start | bytes 983048 | tf_op jit(solution)/shard_map/ppermute | solution.py:358
  21.3 2.2 %collective-permute-start.5 = (bf16[96,1792]{1,0:T(8,128)(2,1)S(1)}, bf16[96,1792]{1,0:T(8,128)(2,1)S(1)}, u32[]{:S(2)}, u32[]{:S(2)}) collective-permute-start(bf16[96,1792]{1,0:T(8,128)(2,1)S(1)} %get-tuple-element.71.own_ref), channel_id=1, source_target_pairs={{0,16},{16,0},{32,48},{48,32},{64,80},{80,64},{96,112},{112,96},{1... | collective-permute-start | bytes 1032200 | tf_op jit(solution)/shard_map/ppermute | solution.py:371
  26.7 2.6 %collective-permute-start.8 = (bf16[6,32,128]{2,1,0:T(8,128)(2,1)S(1)}, bf16[6,32,128]{2,1,0:T(8,128)(2,1)S(1)}, u32[]{:S(2)}, u32[]{:S(2)}) collective-permute-start(bf16[6,32,128]{2,1,0:T(8,128)(2,1)S(1)} %get-tuple-element.77), channel_id=1, source_target_pairs={{0,16},{16,0},{32,48},{48,32},{64,80},{80,64},{96,112},{112,96},{1... | collective-permute-start | bytes 147464 | tf_op jit(solution)/shard_map/ppermute | solution.py:388
  27.9 3.5 %collective-permute-start.9 = (bf16[6,32,128]{2,1,0:T(8,128)(2,1)S(1)}, bf16[6,32,128]{2,1,0:T(8,128)(2,1)S(1)}, u32[]{:S(2)}, u32[]{:S(2)}) collective-permute-start(bf16[6,32,128]{2,1,0:T(8,128)(2,1)S(1)} %get-tuple-element.78), channel_id=1, source_target_pairs={{0,112},{16,32},{32,16},{48,64},{64,48},{80,96},{96,80},{112,0},{1... | collective-permute-start | bytes 147464 | tf_op jit(solution)/shard_map/ppermute | solution.py:389
  32.0 3.6 %collective-permute-start.10 = (bf16[32,1024]{1,0:T(8,128)(2,1)S(1)}, bf16[32,1024]{1,0:T(8,128)(2,1)S(1)}, u32[]{:S(2)}, u32[]{:S(2)}) collective-permute-start(bf16[32,1024]{1,0:T(8,128)(2,1)S(1)} %get-tuple-element.84), channel_id=1, source_target_pairs={{0,4},{1,5},{2,6},{3,7},{4,0},{5,1},{6,2},{7,3},{8,12},{9,13},{10,... | collective-permute-start | bytes 196616 | tf_op jit(solution)/shard_map/ppermute | solution.py:399
  32.1 4.1 %collective-permute-start.11 = (bf16[32,1024]{1,0:T(8,128)(2,1)S(1)}, bf16[32,1024]{1,0:T(8,128)(2,1)S(1)}, u32[]{:S(2)}, u32[]{:S(2)}) collective-permute-start(bf16[32,1024]{1,0:T(8,128)(2,1)S(1)} %get-tuple-element.85), channel_id=1, source_target_pairs={{0,8},{1,9},{2,10},{3,11},{4,12},{5,13},{6,14},{7,15},{8,0},{9,1},... | collective-permute-start | bytes 196616 | tf_op jit(solution)/shard_map/ppermute | solution.py:399
  34.6 5.6 %collective-permute-start.12 = (bf16[32,1024]{1,0:T(8,128)(2,1)S(1)}, bf16[32,1024]{1,0:T(8,128)(2,1)S(1)}, u32[]{:S(2)}, u32[]{:S(2)}) collective-permute-start(bf16[32,1024]{1,0:T(8,128)(2,1)S(1)} %get-tuple-element.86), channel_id=1, source_target_pairs={{0,12},{1,13},{2,14},{3,15},{4,8},{5,9},{6,10},{7,11},{8,4},{9,5},... | collective-permute-start | bytes 196616 | tf_op jit(solution)/shard_map/ppermute | solution.py:399
  40.9 3.8 %collective-permute-start.13 = (f32[32,2688]{1,0:T(8,128)S(1)}, f32[32,2688]{1,0:T(8,128)S(1)}, u32[]{:S(2)}, u32[]{:S(2)}) collective-permute-start(f32[32,2688]{1,0:T(8,128)S(1)} %get-tuple-element.90), channel_id=1, source_target_pairs={{0,16},{16,0},{32,48},{48,32},{64,80},{80,64},{96,112},{112,96},{1... | collective-permute-start | bytes 1032200 | tf_op jit(solution)/shard_map/ppermute | solution.py:407
  44.8 3.9 %collective-permute-start.14 = (bf16[8,3712]{1,0:T(8,128)(2,1)S(1)}, bf16[8,3712]{1,0:T(8,128)(2,1)S(1)}, u32[]{:S(2)}, u32[]{:S(2)}) collective-permute-start(bf16[8,3712]{1,0:T(8,128)(2,1)S(1)} %get-tuple-element.94), channel_id=1, source_target_pairs={{0,1},{1,0},{2,3},{3,2},{4,5},{5,4},{6,7},{7,6},{8,9},{9,8},{10,11... | collective-permute-start | bytes 178184 | tf_op jit(solution)/shard_map/ppermute | solution.py:414
  44.9 5.4 %collective-permute-start.15 = (bf16[8,3712]{1,0:T(8,128)(2,1)S(1)}, bf16[8,3712]{1,0:T(8,128)(2,1)S(1)}, u32[]{:S(2)}, u32[]{:S(2)}) collective-permute-start(bf16[8,3712]{1,0:T(8,128)(2,1)S(1)} %get-tuple-element.95), channel_id=1, source_target_pairs={{0,2},{1,3},{2,0},{3,1},{4,6},{5,7},{6,4},{7,5},{8,10},{9,11},{10,... | collective-permute-start | bytes 178184 | tf_op jit(solution)/shard_map/ppermute | solution.py:414
  47.6 4.3 %collective-permute-start.16 = (bf16[8,3712]{1,0:T(8,128)(2,1)S(1)}, bf16[8,3712]{1,0:T(8,128)(2,1)S(1)}, u32[]{:S(2)}, u32[]{:S(2)}) collective-permute-start(bf16[8,3712]{1,0:T(8,128)(2,1)S(1)} %get-tuple-element.96), channel_id=1, source_target_pairs={{0,3},{1,2},{2,1},{3,0},{4,7},{5,6},{6,5},{7,4},{8,11},{9,10},{10,... | collective-permute-start | bytes 178184 | tf_op jit(solution)/shard_map/ppermute | solution.py:414
  51.9 4.2 %collective-permute-start.19 = (bf16[8,2688]{1,0:T(8,128)(2,1)S(1)}, bf16[8,2688]{1,0:T(8,128)(2,1)S(1)}, u32[]{:S(2)}, u32[]{:S(2)}) collective-permute-start(bf16[8,2688]{1,0:T(8,128)(2,1)S(1)} %get-tuple-element.98), channel_id=1, source_target_pairs={{0,96},{16,112},{32,64},{48,80},{64,32},{80,48},{96,0},{112,16},{1... | collective-permute-start | bytes 129032 | tf_op jit(solution)/shard_map/ppermute | solution.py:418
  54.6 4.5 %collective-permute-start.18 = (bf16[8,2688]{1,0:T(8,128)(2,1)S(1)}, bf16[8,2688]{1,0:T(8,128)(2,1)S(1)}, u32[]{:S(2)}, u32[]{:S(2)}) collective-permute-start(bf16[8,2688]{1,0:T(8,128)(2,1)S(1)} %get-tuple-element.98), channel_id=1, source_target_pairs={{0,64},{16,80},{32,96},{48,112},{64,0},{80,16},{96,32},{112,48},{1... | collective-permute-start | bytes 129032 | tf_op jit(solution)/shard_map/ppermute | solution.py:418
  54.6 4.5 %collective-permute-start.17 = (bf16[8,2688]{1,0:T(8,128)(2,1)S(1)}, bf16[8,2688]{1,0:T(8,128)(2,1)S(1)}, u32[]{:S(2)}, u32[]{:S(2)}) collective-permute-start(bf16[8,2688]{1,0:T(8,128)(2,1)S(1)} %get-tuple-element.98), channel_id=1, source_target_pairs={{0,32},{16,48},{32,0},{48,16},{64,96},{80,112},{96,64},{112,80},{1... | collective-permute-start | bytes 129032 | tf_op jit(solution)/shard_map/ppermute | solution.py:418
  59.1 6.9 %collective-permute-start.20 = (bf16[8,2688]{1,0:T(8,128)(2,1)S(1)}, bf16[8,2688]{1,0:T(8,128)(2,1)S(1)}, u32[]{:S(2)}, u32[]{:S(2)}) collective-permute-start(bf16[8,2688]{1,0:T(8,128)(2,1)S(1)} %add_convert_fusion), channel_id=1, source_target_pairs={{0,128},{128,0},{1,129},{129,1},{2,130},{130,2},{3,131},{131,3},{4... | collective-permute-start | bytes 129032 | tf_op jit(solution)/shard_map/ppermute | solution.py:421
  66.0 5.5 %collective-permute-start.21 = (f32[8,2688]{1,0:T(8,128)S(1)}, f32[8,2688]{1,0:T(8,128)S(1)}, u32[]{:S(2)}, u32[]{:S(2)}) collective-permute-start(f32[8,2688]{1,0:T(8,128)S(1)} %convert_add_fusion.own_ref), channel_id=1, source_target_pairs={{0,16},{16,0},{32,48},{48,32},{64,80},{80,64},{96,112},{112,96},{1... | collective-permute-start | bytes 258056 | tf_op jit(solution)/shard_map/ppermute | solution.py:422
  (1 other events, 0.8 us)
